TPU v7x, 32 devices: a whole 2x2x4 slice. The times are simulated.
32 devices in a mesh: shard: 4 (over y, x), context: 4 (over z), tensor: 2 (over core).
Axes of the slice: x: 2, y: 2, z: 4, core: 2. Of those that a mesh axis runs over, the one named last changes fastest.
Arguments:
- hidden_in: bfloat16 [4, 8, 1024, 768], P(None, 'shard', 'context'), may hold values from -6 to 6
- out_grad: bfloat16 [4, 8, 1024, 768], P(None, 'shard', 'context'), may hold values from -6 to 6
- doc_start: int32 [4, 8, 1024], P(None, 'shard', 'context'), may hold values from 0 to 964, as said below
- norm_in: float32 [768], replicated, may hold values from 0.5 to 1.5
- w_z: bfloat16 [768, 1536], P(('shard', 'context'), 'tensor'), may hold values from -0.21875 to 0.21875
- w_x: bfloat16 [768, 1536], P(('shard', 'context'), 'tensor'), may hold values from -0.21875 to 0.21875
- w_bc: bfloat16 [768, 256], P(('shard', 'context'), 'tensor'), may hold values from -0.21875 to 0.21875
- w_dt: bfloat16 [768, 24], P(('shard', 'context'), 'tensor'), may hold values from -0.21875 to 0.21875
- conv_x: float32 [5, 1536], P(None, 'tensor'), may hold values from -0.5 to 0.5
- conv_bc: float32 [5, 256], P(None, 'tensor'), may hold values from -0.5 to 0.5
- dt_bias: float32 [24], P('tensor'), may hold values from -6 to -2
- a_log: float32 [24], P('tensor'), may hold values from -2 to 1
- skip_d: float32 [24], P('tensor'), may hold values from 0.5 to 1.5
- norm_gate: float32 [1536], P('tensor'), may hold values from 0.5 to 1.5
- w_out: bfloat16 [1536, 768], P('tensor', ('shard', 'context')), may hold values from -0.15625 to 0.15625
Outputs:
- out_hidden: bfloat16 [4, 8, 1024, 768], P(None, 'shard', 'context')
- in_grad: bfloat16 [4, 8, 1024, 768], P(None, 'shard', 'context')
- grad_norm_in: float32 [768], replicated
- grad_w_z: float32 [768, 1536], P(('shard', 'context'), 'tensor')
- grad_w_x: float32 [768, 1536], P(('shard', 'context'), 'tensor')
- grad_w_bc: float32 [768, 256], P(('shard', 'context'), 'tensor')
- grad_w_dt: float32 [768, 24], P(('shard', 'context'), 'tensor')
- grad_conv_x: float32 [5, 1536], P(None, 'tensor')
- grad_conv_bc: float32 [5, 256], P(None, 'tensor')
- grad_dt_bias: float32 [24], P('tensor')
- grad_a_log: float32 [24], P('tensor')
- grad_skip_d: float32 [24], P('tensor')
- grad_norm_gate: float32 [1536], P('tensor')
- grad_w_out: float32 [1536, 768], P('tensor', ('shard', 'context'))
Inputs may be any that keep to these rules, and one draw needn't show every extreme that they name: doc_start[m, s, t] is the first position of the document that holds position t of sequence s; documents follow one another up to the sequence's end, the last one exactly 60 positions long and the others 60 to 800, except the first, which the sequence's start may cut; in each micro-batch, one sequence of each aligned group of 2 instead holds three documents: a first one of 60 to 255 positions, then one that runs up to position 963, then the last one of 60 positions.
All inputs are finite; a program needn't handle non-finite values.
Results may differ from a plain program's by a relative error of at most 0.0083.
Values may be sent and summed in bfloat16 or wider, within the bound.
A program may use at most 256 MiB of HBM per device.

v0:
```python
import jax
import jax.numpy as jnp
from jax import lax
from jax.sharding import PartitionSpec as P

INNER = 1536


EPSILON = 1e-05
HIGHEST = lax.Precision.HIGHEST


def passed_along(value, axis, by):
    length = lax.axis_size(axis)
    pairs = [(i, i + by) for i in range(length) if 0 <= i + by < length]
    return lax.ppermute(value, axis, pairs)


def prefix(value, axis, combine, identity, reverse):
    length, index = (lax.axis_size(axis), lax.axis_index(axis))
    everything = jax.tree.map(lambda part: lax.all_gather(part, axis), value)
    start = jax.tree.map(
        lambda part, zero: jnp.broadcast_to(jnp.asarray(zero, part.dtype), part.shape),
        value,
        identity,
    )

    def lap(k, before):
        at = length - 1 - k if reverse else k
        reached = at > index if reverse else at < index
        new = combine(before, jax.tree.map(lambda part: part[at], everything))
        return jax.tree.map(lambda a, b: jnp.where(reached, a, b), new, before)

    return lax.fori_loop(0, length, lap, start)


def flag(condition):
    return jnp.where(condition, 1.0, 0.0).astype(jnp.float32)


def conv_piece(channels, previous, weights, starts, offset):
    length = channels.shape[1]
    extended = jnp.concatenate([previous, channels], 1)
    position = offset + jnp.arange(length, dtype=jnp.int32)
    running = jnp.zeros_like(channels) + weights[4]
    for lag_count in range(4):
        tapped = extended[:, 3 - lag_count : 3 - lag_count + length]
        keep_tap = (position[None, :] - lag_count >= starts)[:, :, None]
        running = running + weights[lag_count] * jnp.where(keep_tap, tapped, 0.0)
    return jax.nn.silu(running)


def piece_setup(conv_x_out, conv_bc_out, dt_raw, dt_bias, a_log):
    step_size = jax.nn.softplus(dt_raw + dt_bias)
    cumulative = jnp.cumsum(-jnp.exp(a_log) * step_size, 0).T
    length, head_count = dt_raw.shape
    values = conv_x_out.reshape(length, head_count, -1).transpose(1, 0, 2)
    half_width = conv_bc_out.shape[1] // 2
    return (
        step_size.T,
        cumulative,
        values,
        conv_bc_out[:, :half_width],
        conv_bc_out[:, half_width:],
    )


def state_part(conv_x_out, conv_bc_out, dt_raw, dt_bias, a_log, starts, offset):
    step_size, cumulative, values, inputs_b, readout = piece_setup(
        conv_x_out, conv_bc_out, dt_raw, dt_bias, a_log
    )
    position = offset + jnp.arange(dt_raw.shape[0], dtype=jnp.int32)
    weight_end = (
        jnp.exp(cumulative[:, -1:] - cumulative) * flag(position >= starts[-1])[None, :] * step_size
    )
    local_state = jnp.einsum(
        "hjp,jn->hpn", values * weight_end[:, :, None], inputs_b, precision=HIGHEST
    )
    decay_total = jnp.exp(cumulative[:, -1]) * flag(starts[-1] < offset)
    return (decay_total, local_state)


def output_part(conv_x_out, conv_bc_out, dt_raw, dt_bias, a_log, skip_d, state_in, starts, offset):
    step_size, cumulative, values, inputs_b, readout = piece_setup(
        conv_x_out, conv_bc_out, dt_raw, dt_bias, a_log
    )
    length = dt_raw.shape[0]
    position = offset + jnp.arange(length, dtype=jnp.int32)
    row_index = jnp.arange(length, dtype=jnp.int32)[:, None]
    col_index = jnp.arange(length, dtype=jnp.int32)[None, :]
    causal = (col_index <= row_index) & (position[None, :] >= starts[:, None])
    spread = cumulative[:, :, None] - cumulative[:, None, :]
    decay_mat = jnp.where(causal[None], jnp.exp(jnp.minimum(spread, 0.0)), 0.0)
    intersection = jnp.einsum("in,jn->ij", readout, inputs_b, precision=HIGHEST)
    mixing = intersection[None] * decay_mat * step_size[:, None, :]
    within = jnp.einsum("hij,hjp->hip", mixing, values, precision=HIGHEST)
    carried_in = jnp.exp(cumulative) * flag(starts < offset)[None, :]
    across = carried_in[:, :, None] * jnp.einsum(
        "in,hpn->hip", readout, state_in, precision=HIGHEST
    )
    result = within + across + skip_d[:, None, None] * values
    return result.transpose(1, 0, 2).reshape(length, -1)


def link(earlier, later):
    return (earlier[0] * later[0], later[0][:, :, None, None] * earlier[1] + later[1])


def outer_sum(left, right):
    return lax.dot_general(
        left.reshape(-1, left.shape[-1]),
        right.reshape(-1, right.shape[-1]),
        (((0,), (0,)), ((), ())),
        preferred_element_type=jnp.float32,
    )


def project_back(gradient_row_block, weight_matrix):
    return jnp.einsum(
        "rgv,jv->rgj", gradient_row_block, weight_matrix, preferred_element_type=jnp.float32
    )


def silu_slope(values):
    logistic = jax.nn.sigmoid(values)
    return logistic * (1.0 + values * (1.0 - logistic))


def combine_gradient_parts(large_terms, small_terms):
    large_terms = (
        lax.psum_scatter(large_terms[0], ("shard", "context"), scatter_dimension=0, tiled=True),
        lax.psum_scatter(large_terms[1], ("shard", "context"), scatter_dimension=0, tiled=True),
        lax.psum_scatter(large_terms[2], ("shard", "context"), scatter_dimension=0, tiled=True),
        lax.psum_scatter(large_terms[3], ("shard", "context"), scatter_dimension=0, tiled=True),
        lax.psum_scatter(large_terms[4], ("shard", "context"), scatter_dimension=1, tiled=True),
    )
    small_terms = lax.psum(
        (
            small_terms[0],
            small_terms[1],
            small_terms[2],
            small_terms[3],
            small_terms[4],
            small_terms[5],
        ),
        ("shard", "context"),
    )
    return (large_terms, small_terms)


def accumulate(totals, new_terms):
    if totals is None:
        return new_terms
    return jax.tree.map(jnp.add, totals, new_terms)


def input_norm_back(grad_normed, hidden, scale_in, output_gradient_seed, norm_in):
    weighted_in = grad_normed * norm_in
    gain_part = jnp.sum(grad_normed * hidden * scale_in, (0, 1))
    cube_in = scale_in * scale_in * scale_in
    grad_hidden = (
        output_gradient_seed.astype(jnp.float32)
        + scale_in * weighted_in
        - hidden * cube_in * jnp.mean(weighted_in * hidden, -1, keepdims=True)
    )
    return (gain_part, grad_hidden.astype(jnp.bfloat16))


def shards(
    hidden_in,
    out_grad,
    doc_start,
    norm_in,
    w_z,
    w_x,
    w_bc,
    w_dt,
    conv_x,
    conv_bc,
    dt_bias,
    a_log,
    skip_d,
    norm_gate,
    w_out,
):
    piece_len = hidden_in.shape[2]
    offset = lax.axis_index("context") * piece_len
    convolution_taps_weight = jnp.concatenate([conv_x, conv_bc], 1)
    local_inner = w_z.shape[1]
    batch_state = jax.vmap(state_part, in_axes=(0, 0, 0, None, None, 0, None))
    batch_output = jax.vmap(output_part, in_axes=(0, 0, 0, None, None, None, 0, 0, None))
    outputs = []
    input_grads = []
    large_acc = None
    small_acc = None
    for micro_step in range(hidden_in.shape[0]):
        w_z_all, w_x_all, w_bc_all, w_dt_all, full_output_weight = (
            lax.all_gather(w_z, ("shard", "context"), axis=0, tiled=True),
            lax.all_gather(w_x, ("shard", "context"), axis=0, tiled=True),
            lax.all_gather(w_bc, ("shard", "context"), axis=0, tiled=True),
            lax.all_gather(w_dt, ("shard", "context"), axis=0, tiled=True),
            lax.all_gather(w_out, ("shard", "context"), axis=1, tiled=True),
        )
        hidden = hidden_in[micro_step].astype(jnp.float32)
        starts = doc_start[micro_step]
        scale_in = lax.rsqrt(jnp.mean(hidden * hidden, -1, keepdims=True) + EPSILON)
        normed = (hidden * scale_in * norm_in).astype(jnp.bfloat16)
        gate_raw = jnp.dot(normed, w_z_all, preferred_element_type=jnp.float32)
        x_raw = jnp.dot(normed, w_x_all, preferred_element_type=jnp.float32)
        bc_raw = jnp.dot(normed, w_bc_all, preferred_element_type=jnp.float32)
        dt_raw = jnp.dot(normed, w_dt_all, preferred_element_type=jnp.float32)
        channels = jnp.concatenate([x_raw, bc_raw], 2)
        previous = passed_along(channels[:, -3:], "context", 1)
        convolved_output = conv_piece(channels, previous, convolution_taps_weight, starts, offset)
        conv_x_out = convolved_output[:, :, :local_inner]
        conv_bc_out = lax.all_gather(
            convolved_output[:, :, local_inner:], "tensor", axis=2, tiled=True
        )
        decay_total, local_state = batch_state(
            conv_x_out, conv_bc_out, dt_raw, dt_bias, a_log, starts, offset
        )
        identity = (jnp.ones_like(decay_total), jnp.zeros_like(local_state))
        prefix_decay, state_in = prefix(
            (decay_total, local_state), "context", link, identity, False
        )
        mixer = batch_output(
            conv_x_out, conv_bc_out, dt_raw, dt_bias, a_log, skip_d, state_in, starts, offset
        )
        gate_act = jax.nn.silu(gate_raw)
        gated_out = mixer * gate_act
        square_sum = lax.psum(jnp.sum(gated_out * gated_out, -1), "tensor")
        scale_gate = lax.rsqrt(square_sum / INNER + EPSILON)[:, :, None]
        gate_normed = (gated_out * scale_gate * norm_gate).astype(jnp.bfloat16)
        branch_terms = jnp.dot(gate_normed, full_output_weight, preferred_element_type=jnp.float32)
        branch = lax.psum(branch_terms, "tensor")
        out_piece = (hidden + branch).astype(jnp.bfloat16)
        output_gradient_seed = out_grad[micro_step]
        grad_out_w = outer_sum(gate_normed, output_gradient_seed)
        grad_gn = jnp.einsum(
            "zfe,xe->zfx",
            output_gradient_seed,
            full_output_weight,
            preferred_element_type=jnp.float32,
        )
        grad_norm_gate = jnp.sum(grad_gn * gated_out * scale_gate, (0, 1))
        weighted = grad_gn * norm_gate
        gate_dot = lax.psum(jnp.sum(weighted * gated_out, -1), "tensor")
        cube_gate = scale_gate * scale_gate * scale_gate
        grad_gated = scale_gate * weighted - gated_out * cube_gate * (gate_dot / INNER)[:, :, None]
        grad_mixer = grad_gated * gate_act
        grad_gate_raw = grad_gated * mixer * silu_slope(gate_raw)
        unused_out, pull_output = jax.vjp(
            lambda part_x, part_bc, part_dt, part_bias, part_alog, part_skip, part_state: batch_output(
                part_x,
                part_bc,
                part_dt,
                part_bias,
                part_alog,
                part_skip,
                part_state,
                starts,
                offset,
            ),
            conv_x_out,
            conv_bc_out,
            dt_raw,
            dt_bias,
            a_log,
            skip_d,
            state_in,
        )
        (
            grad_x_first,
            grad_bc_first,
            grad_dt_first,
            grad_bias_first,
            grad_alog_first,
            grad_skip,
            grad_state_in,
        ) = pull_output(grad_mixer)
        unused_prod, later_grad = prefix(
            (decay_total, grad_state_in), "context", link, identity, True
        )
        grad_decay = jnp.sum(later_grad * state_in, (2, 3))
        unused_state, pull_state = jax.vjp(
            lambda part_x, part_bc, part_dt, part_bias, part_alog: batch_state(
                part_x, part_bc, part_dt, part_bias, part_alog, starts, offset
            ),
            conv_x_out,
            conv_bc_out,
            dt_raw,
            dt_bias,
            a_log,
        )
        grad_x_second, grad_bc_second, grad_dt_second, grad_bias_second, grad_alog_second = (
            pull_state((grad_decay, later_grad))
        )
        grad_bc_own = lax.psum_scatter(
            grad_bc_first + grad_bc_second, "tensor", scatter_dimension=2, tiled=True
        )
        unused_conv, pull_conv = jax.vjp(
            lambda part_chan, part_prev, part_weights: conv_piece(
                part_chan, part_prev, part_weights, starts, offset
            ),
            channels,
            previous,
            convolution_taps_weight,
        )
        grad_channels, grad_previous, grad_conv = pull_conv(
            jnp.concatenate([grad_x_first + grad_x_second, grad_bc_own], 2)
        )
        from_next = passed_along(grad_previous, "context", -1)
        grad_channels = jnp.concatenate(
            [grad_channels[:, :-3], grad_channels[:, -3:] + from_next], 1
        )
        grad_gate_low = grad_gate_raw.astype(jnp.bfloat16)
        grad_x_low = grad_channels[:, :, :local_inner].astype(jnp.bfloat16)
        grad_bc_low = grad_channels[:, :, local_inner:].astype(jnp.bfloat16)
        grad_dt_low = (grad_dt_first + grad_dt_second).astype(jnp.bfloat16)
        partial_rows = (
            project_back(grad_gate_low, w_z_all)
            + project_back(grad_x_low, w_x_all)
            + project_back(grad_bc_low, w_bc_all)
            + project_back(grad_dt_low, w_dt_all)
        )
        grad_normed = lax.psum(partial_rows, "tensor")
        grad_norm_in, in_whole = input_norm_back(
            grad_normed, hidden, scale_in, output_gradient_seed, norm_in
        )
        outputs.append(out_piece)
        input_grads.append(in_whole)
        large_terms = (
            outer_sum(normed, grad_gate_low),
            outer_sum(normed, grad_x_low),
            outer_sum(normed, grad_bc_low),
            outer_sum(normed, grad_dt_low),
            grad_out_w,
        )
        small_terms = (
            grad_norm_in,
            grad_conv,
            grad_bias_first + grad_bias_second,
            grad_alog_first + grad_alog_second,
            grad_skip,
            grad_norm_gate,
        )
        large_terms, small_terms = combine_gradient_parts(large_terms, small_terms)
        large_acc = accumulate(large_acc, large_terms)
        small_acc = accumulate(small_acc, small_terms)
    total_gain_scale = small_acc[0]
    conv_grads = small_acc[1]
    return (
        jnp.stack(outputs),
        jnp.stack(input_grads),
        total_gain_scale,
        large_acc[0],
        large_acc[1],
        large_acc[2],
        large_acc[3],
        conv_grads[:, :local_inner],
        conv_grads[:, local_inner:],
        small_acc[2],
        small_acc[3],
        small_acc[4],
        small_acc[5],
        large_acc[4],
    )


def solution(mesh):
    placed = (
        P(None, "shard", "context", None),
        P(None, "shard", "context", None),
        P(None, "shard", "context"),
        P(),
        P(("shard", "context"), "tensor"),
        P(("shard", "context"), "tensor"),
        P(("shard", "context"), "tensor"),
        P(("shard", "context"), "tensor"),
        P(None, "tensor"),
        P(None, "tensor"),
        P("tensor"),
        P("tensor"),
        P("tensor"),
        P("tensor"),
        P("tensor", ("shard", "context")),
    )
    return jax.shard_map(
        shards,
        mesh=mesh,
        in_specs=placed,
        out_specs=(
            P(None, "shard", "context", None),
            P(None, "shard", "context", None),
            P(),
            P(("shard", "context"), "tensor"),
            P(("shard", "context"), "tensor"),
            P(("shard", "context"), "tensor"),
            P(("shard", "context"), "tensor"),
            P(None, "tensor"),
            P(None, "tensor"),
            P("tensor"),
            P("tensor"),
            P("tensor"),
            P("tensor"),
            P("tensor", ("shard", "context")),
        ),
        check_vma=False,
    )
```

profile of v0, /device:TPU:0, one launch (start us, length us, event | category | flops | bytes accessed | tf_op | source)
XLA Modules:
  0.0 1709.4 jit_solution(2333088273170240412)
XLA Ops:
  12.6 43.1 %all-gather.8 = bf16[16,48,12]{1,2,0:T(8,128)(2,1)S(1)} all-gather(bf16[1,48,12]{1,2,0:T(8,128)(2,1)S(1)} %bitcast.1080), channel_id=1, replica_groups=mesh['shard'=4,'context'=4,'tensor'=2] {'shard','context'}, dimensions={0}, use_global_device_ids=true | all-gather | bytes 19584 | tf_op jit(solution)/shard_map/all_gather | solution.py:201
  62.1 4.4 broadcast_multiply_fusion.7
  70.5 37.9 %all_gather.115 = bf16[768,128]{1,0:T(8,128)(2,1)S(1)} all-gather(bf16[48,128]{1,0:T(8,128)(2,1)} %param.38), channel_id=1, replica_groups=mesh['shard'=4,'context'=4,'tensor'=2] {'shard','context'}, dimensions={0}, use_global_device_ids=true | all-gather | bytes 208896 | tf_op jit(solution)/shard_map/all_gather | solution.py:200
  183.3 4.3 collective-permute-start.2
  214.7 4.2 collective-permute-start.1
  238.1 4.4 broadcast_multiply_fusion.1
  255.8 12.4 all_gather.118
  277.3 8.6 all_gather.132
  292.8 9.5 all_gather.128
  311.0 9.7 all_gather.124
  341.3 12.2 while.120
  356.4 8.9 fusion.207
  368.4 12.1 while.123
  383.2 9.2 fusion.201
  395.4 12.2 while.122
  410.4 9.0 fusion.203
  422.4 12.1 while.121
  437.3 9.4 fusion.205
  449.8 4.4 all-gather.23.cloned.1.call-done
  454.2 4.5 multiply_reduce_fusion.31
  469.5 8.2 multiply_reduce_fusion.17
  480.3 7.4 multiply_convert_fusion.1
  494.7 7.4 multiply_convert_fusion.2
  529.1 14.1 fusion.373
  543.3 11.7 fusion.371
  555.1 11.8 fusion.369
  582.3 13.6 fusion.367
  600.9 4.4 fusion.311
  646.0 12.6 while.124
  660.7 12.2 while.125
  675.0 9.4 all-gather.39.cloned.1.call-done
  684.5 12.4 while.126
  699.2 6.0 multiply_reduce_fusion.23
  712.5 35.7 %all-gather.41.cloned.1.call-done = f32[8,12,64,128]{3,2,1,0:T(8,128)} async-done(((f32[2,12,64,128]{3,2,1,0:T(8,128)}), f32[8,12,64,128]{3,2,1,0:T(8,128)}) %all-gather.41.cloned.1.call-update) | async-done | bytes 3145744 | tf_op jit(solution)/shard_map/all_gather | solution.py:21
  748.2 12.3 while.127
  760.5 6.3 multiply_reduce_fusion.20
  770.4 6.3 reduce-window.124
  787.7 6.4 reduce-window.126
  802.2 6.3 reduce-window.134
  819.7 6.2 reduce-window.136
  834.0 6.3 reduce-window.144
  851.5 6.3 reduce-window.146
  867.0 6.3 reduce-window.154
  883.9 5.8 reduce-window.156
  893.9 4.3 fusion.323
  901.0 4.4 fusion.329
  933.2 4.3 fusion.332
  940.5 9.7 fusion.199
  950.3 7.0 fusion.193
  957.5 7.0 fusion.190
  974.2 8.4 fusion.196
  995.9 5.1 multiply_reduce_fusion.15
  1001.2 7.1 multiply_reduce_fusion.7
  1008.3 5.0 multiply_reduce_fusion.3
  1013.4 4.2 multiply_select_fusion.3
  1024.7 4.9 multiply_reduce_fusion.11
  1096.6 26.9 %reduce-scatter.28.cloned.1.call-done = f32[48,12]{1,0:T(8,128)} async-done(((f32[768,12]{1,0:T(8,128)}), f32[48,12]{1,0:T(8,128)}) %reduce-scatter.28.cloned.1.call-update) | async-done | bytes 2320
  1125.4 51.0 %all-reduce.62.cloned.1.call-done = (f32[2,256,768]{2,1,0:T(8,128)}, f32[2,256,768]{2,1,0:T(8,128)}, f32[2,256,768]{2,1,0:T(8,128)}, f32[2,256,768]{2,1,0:T(8,12...) async-done(((f32[2,256,768]{2,1,0:T(8,128)}, f32[2,256,768]{2,1,0:T(8,128)}, f32[2,256,768]{2,1,0:T(8,128)}, ...) | async-done | bytes 12582928 | tf_op jit(solution)/shard_map/psum | solution.py:235
  1176.4 4.2 fusion.187
  1180.7 78.8 %all-reduce.56 = (f32[768]{0:T(1024)}, f32[5,896]{1,0:T(8,128)S(1)}, f32[12]{0:T(128)}, f32[12]{0:T(128)}, f32[12]{0:T(128)}, /*index=5*/f32[768]{0:T(1024)}) all-reduce(f32[768]{0:T(1024)S(1)} %add_add_fusion.11, f32[5,896]{1,0:T(8,128)S(1)} %add_add_fusion.9, ...), channel_id=1, replica_groups=mesh['shard'=4,'context'=4,'tensor'=2] {'shard','context'}, use_global_device_ids=true, to_apply=%region_117.119 | all-reduce | flops 6052 | bytes 48416 | tf_op jit(solution)/shard_map/psum | solution.py:137
  1272.1 39.3 %reduce-scatter.26.cloned.1.call-done = f32[768,48]{0,1:T(8,128)} async-done(((f32[768,768]{0,1:T(8,128)}), f32[768,48]{0,1:T(8,128)}) %reduce-scatter.26.cloned.1.call-update) | async-done | bytes 147472 | tf_op jit(solution)/shard_map/reduce_scatter | solution.py:135
  1311.3 132.3 %reduce-scatter.20.cloned.1.call-done = f32[48,768]{1,0:T(8,128)} async-done(((f32[768,768]{1,0:T(8,128)}), f32[48,768]{1,0:T(8,128)}) %reduce-scatter.20.cloned.1.call-update) | async-done | bytes 147472 | tf_op jit(solution)/shard_map/reduce_scatter | solution.py:131
  1443.6 126.3 %reduce-scatter.24.cloned.1.call-done = f32[48,128]{1,0:T(8,128)} async-done(((f32[768,128]{1,0:T(8,128)}), f32[48,128]{1,0:T(8,128)}) %reduce-scatter.24.cloned.1.call-update) | async-done | bytes 24592 | tf_op jit(solution)/shard_map/reduce_scatter | solution.py:133
  1569.9 132.2 %reduce-scatter.22.cloned.1.call-done = f32[48,768]{1,0:T(8,128)} async-done(((f32[768,768]{1,0:T(8,128)}), f32[48,768]{1,0:T(8,128)}) %reduce-scatter.22.cloned.1.call-update) | async-done | bytes 147472 | tf_op jit(solution)/shard_map/reduce_scatter | solution.py:132
  (1447 shorter events, 656.9 us)
Async XLA Ops:
  7.2 109.8 %all-gather.21.cloned.1.call-start = ((), (), s32[]{:S(2)}) async-start(), calls=%async_computation.9 | async-start | bytes 1253376 | tf_op jit(solution)/shard_map/all_gather | solution.py:199
  7.9 318.9 %all-gather.25.cloned.1.call-start = ((), (), s32[]{:S(2)}) async-start(), calls=%async_computation.11 | async-start | bytes 1253376 | tf_op jit(solution)/shard_map/all_gather | solution.py:202
  8.7 332.7 %all-gather.27.cloned.1.call-start = ((), (), s32[]{:S(2)}) async-start(), calls=%async_computation.16 | async-start | bytes 3932160 | tf_op jit(solution)/shard_map/all_gather | solution.py:21
  9.3 100.5 %copy-start.382 = (s32[256]{0:T(256)}, s32[256]{0:T(256)S(1)}, u32[]{:S(2)}) copy-start(s32[256]{0:T(256)S(1)} %get-tuple-element.1520) | copy-start | bytes 3076
  9.9 46.5 %copy-start.7 = (bf16[4,2,256,768]{3,2,1,0:T(8,128)(2,1)S(1)}, bf16[4,2,256,768]{3,2,1,0:T(8,128)(2,1)}, u32[]{:S(2)}) copy-start(bf16[4,2,256,768]{3,2,1,0:T(8,128)(2,1)} %param.32) | copy-start | bytes 9437188
  9.9 46.6 %copy-start.236 = (f32[768]{0:T(1024)S(1)}, f32[768]{0:T(1024)}, u32[]{:S(2)}) copy-start(f32[768]{0:T(1024)} %param.35) | copy-start | bytes 9220
  56.4 60.6 %copy-start.292 = (f32[2,256]{1,0:T(2,128)}, f32[2,256]{1,0:T(2,128)S(1)}, u32[]{:S(2)}) copy-start(f32[2,256]{1,0:T(2,128)S(1)} %get-tuple-element.1514) | copy-start | bytes 6148
  69.3 47.7 %copy-start.318 = (s32[2,256]{1,0:T(2,128)}, s32[2,256]{1,0:T(2,128)S(1)}, u32[]{:S(2)}) copy-start(s32[2,256]{1,0:T(2,128)S(1)} %get-tuple-element.1447) | copy-start | bytes 6148
  69.3 47.7 %copy-start.320 = (s32[2,256]{1,0:T(2,128)}, s32[2,256]{1,0:T(2,128)S(1)}, u32[]{:S(2)}) copy-start(s32[2,256]{1,0:T(2,128)S(1)} %get-tuple-element.1448) | copy-start | bytes 6148
  69.3 47.7 %copy-start.322 = (s32[2,256]{1,0:T(2,128)}, s32[2,256]{1,0:T(2,128)S(1)}, u32[]{:S(2)}) copy-start(s32[2,256]{1,0:T(2,128)S(1)} %get-tuple-element.1449) | copy-start | bytes 6148
  69.3 47.7 %copy-start.324 = (s32[2,256]{1,0:T(2,128)}, s32[2,256]{1,0:T(2,128)S(1)}, u32[]{:S(2)}) copy-start(s32[2,256]{1,0:T(2,128)S(1)} %get-tuple-element.1450) | copy-start | bytes 6148
  70.5 46.4 %copy-start.147 = (f32[2,256]{0,1:T(8,128)}, f32[2,256]{0,1:T(8,128)S(1)}, u32[]{:S(2)}) copy-start(f32[2,256]{0,1:T(8,128)S(1)} %copy.630) | copy-start | bytes 6148
  108.5 103.0 %copy-start.104 = (bf16[768,128]{1,0:T(8,128)(2,1)}, bf16[768,128]{1,0:T(8,128)(2,1)S(1)}, u32[]{:S(2)}) copy-start(bf16[768,128]{1,0:T(8,128)(2,1)S(1)} %all_gather.115) | copy-start | bytes 589828
  120.4 5.4 collective-permute-start
  124.7 34.8 %copy-start.220 = (f32[896]{0:T(1024)}, f32[896]{0:T(1024)S(1)}, u32[]{:S(2)}) copy-start(f32[896]{0:T(1024)S(1)} %get-tuple-element.1169) | copy-start | bytes 10756
  124.7 34.8 %copy-start.224 = (f32[896]{0:T(1024)}, f32[896]{0:T(1024)S(1)}, u32[]{:S(2)}) copy-start(f32[896]{0:T(1024)S(1)} %get-tuple-element.1170) | copy-start | bytes 10756
  124.7 34.8 %copy-start.228 = (f32[896]{0:T(1024)}, f32[896]{0:T(1024)S(1)}, u32[]{:S(2)}) copy-start(f32[896]{0:T(1024)S(1)} %get-tuple-element.1171) | copy-start | bytes 10756
  124.8 34.8 %copy-start.232 = (f32[896]{0:T(1024)}, f32[896]{0:T(1024)S(1)}, u32[]{:S(2)}) copy-start(f32[896]{0:T(1024)S(1)} %get-tuple-element.1172) | copy-start | bytes 10756
  124.8 34.8 %copy-start.251 = (f32[896]{0:T(1024)}, f32[896]{0:T(1024)S(1)}, u32[]{:S(2)}) copy-start(f32[896]{0:T(1024)S(1)} %get-tuple-element.1168) | copy-start | bytes 10756
  142.5 225.9 %all-gather.33.cloned.1.call-start = ((), (), s32[]{:S(2)}) async-start(), calls=%async_computation.19 | async-start | bytes 3932160 | tf_op jit(solution)/shard_map/all_gather | solution.py:21
  151.4 6.3 collective-permute-start.3
  174.4 221.0 %all-gather.31.cloned.1.call-start = ((), (), s32[]{:S(2)}) async-start(), calls=%async_computation.18 | async-start | bytes 3932160 | tf_op jit(solution)/shard_map/all_gather | solution.py:21
  177.0 72.8 %copy-start.214 = (f32[2,12,256]{2,0,1:T(2,128)}, f32[2,12,256]{2,0,1:T(2,128)S(1)}, u32[]{:S(2)}) copy-start(f32[2,12,256]{2,0,1:T(2,128)S(1)} %reduce_window_sum.276) | copy-start | bytes 73732
  183.3 6.5 collective-permute-start.2
  206.4 216.1 %all-gather.29.cloned.1.call-start = ((), (), s32[]{:S(2)}) async-start(), calls=%async_computation.17 | async-start | bytes 3932160 | tf_op jit(solution)/shard_map/all_gather | solution.py:21
  214.7 6.5 collective-permute-start.1
  237.0 217.2 %all-gather.23.cloned.1.call-start = ((), (), s32[]{:S(2)}) async-start(), calls=%async_computation.10 | async-start | bytes 1253376 | tf_op jit(solution)/shard_map/all_gather | solution.py:198
  237.7 408.2 %all-gather.35.cloned.1.call-start = ((), (), s32[]{:S(2)}) async-start(), calls=%async_computation.20 | async-start | bytes 3932160 | tf_op jit(solution)/shard_map/all_gather | solution.py:21
  253.4 67.4 %copy-start.181 = (f32[2,256,12]{2,0,1:T(2,128)S(1)}, f32[2,256,12]{2,0,1:T(2,128)}, u32[]{:S(2)}) copy-start(f32[2,256,12]{2,0,1:T(2,128)} %get-tuple-element.1487) | copy-start | bytes 73732
  288.1 42.4 %copy-start.206 = (f32[2,12,2,128]{3,1,2,0:T(8,128)}, f32[2,12,2,128]{3,1,2,0:T(8,128)S(1)}, u32[]{:S(2)}) copy-start(f32[2,12,2,128]{3,1,2,0:T(8,128)S(1)} %reduce-window.150) | copy-start | bytes 73732
  326.8 163.9 %copy-start.217 = (f32[2,12,256]{2,1,0:T(8,128)}, f32[2,12,256]{2,1,0:T(8,128)S(1)}, u32[]{:S(2)}) copy-start(f32[2,12,256]{2,1,0:T(8,128)S(1)} %copy.686) | copy-start | bytes 73732
  494.6 166.1 %all-gather.37.cloned.1.call-start = ((), (), s32[]{:S(2)}) async-start(), calls=%async_computation.21 | async-start | bytes 3932160 | tf_op jit(solution)/shard_map/all_gather | solution.py:21
  509.1 175.3 %all-gather.39.cloned.1.call-start = ((), (), s32[]{:S(2)}) async-start(), calls=%async_computation.22 | async-start | bytes 3932160 | tf_op jit(solution)/shard_map/all_gather | solution.py:21
  529.0 219.3 %all-gather.41.cloned.1.call-start = ((), (), s32[]{:S(2)}) async-start(), calls=%async_computation.23 | async-start | bytes 3932160 | tf_op jit(solution)/shard_map/all_gather | solution.py:21
  628.5 367.4 %reduce-scatter.12.cloned.1.call-start = ((), (), s32[]{:S(2)}) async-start(), calls=%async_computation.12 | async-start | bytes 786432 | tf_op jit(solution)/shard_map/reduce_scatter | solution.py:298
  846.6 31.8 %copy-start.383 = (f32[2,12]{1,0:T(2,128)}, f32[2,12]{1,0:T(2,128)S(1)}, u32[]{:S(2)}) copy-start(f32[2,12]{1,0:T(2,128)S(1)} %get-tuple-element.1396) | copy-start | bytes 292
  899.2 101.9 %reduce-scatter.16.cloned.1.call-start = ((), (), s32[]{:S(2)}) async-start(), calls=%async_computation.14 | async-start | bytes 786432 | tf_op jit(solution)/shard_map/reduce_scatter | solution.py:298
  919.1 89.1 %reduce-scatter.18.cloned.1.call-start = ((), (), s32[]{:S(2)}) async-start(), calls=%async_computation.15 | async-start | bytes 786432 | tf_op jit(solution)/shard_map/reduce_scatter | solution.py:298
  940.3 82.9 %reduce-scatter.14.cloned.1.call-start = ((), (), s32[]{:S(2)}) async-start(), calls=%async_computation.13 | async-start | bytes 786432 | tf_op jit(solution)/shard_map/reduce_scatter | solution.py:298
  989.4 134.1 %reduce-scatter.28.cloned.1.call-start = ((), (), s32[]{:S(2)}) async-start(), calls=%async_computation.28 | async-start | bytes 417792
  995.7 180.7 %all-reduce.62.cloned.1.call-start = ((), (), s32[]{:S(2)}) async-start(), calls=%async_computation.29 | async-start | bytes 25165824 | tf_op jit(solution)/shard_map/psum | solution.py:235
  1031.2 9.8 collective-permute-start.6
  1036.4 6.0 collective-permute-start.4
  1038.2 6.6 collective-permute-start.5
  1039.7 7.0 collective-permute-start.7
  1062.4 248.9 %reduce-scatter.26.cloned.1.call-start = ((), (), s32[]{:S(2)}) async-start(), calls=%async_computation.27 | async-start | bytes 2506752 | tf_op jit(solution)/shard_map/reduce_scatter | solution.py:135
  1071.2 372.4 %reduce-scatter.20.cloned.1.call-start = ((), (), s32[]{:S(2)}) async-start(), calls=%async_computation.24 | async-start | bytes 2506752 | tf_op jit(solution)/shard_map/reduce_scatter | solution.py:131
  1078.4 491.4 %reduce-scatter.24.cloned.1.call-start = ((), (), s32[]{:S(2)}) async-start(), calls=%async_computation.26 | async-start | bytes 417792 | tf_op jit(solution)/shard_map/reduce_scatter | solution.py:133
  1087.9 614.1 %reduce-scatter.22.cloned.1.call-start = ((), (), s32[]{:S(2)}) async-start(), calls=%async_computation.25 | async-start | bytes 2506752 | tf_op jit(solution)/shard_map/reduce_scatter | solution.py:132
  1094.6 30.4 %copy-start.363 = (f32[896]{0:T(1024)S(1)}, f32[896]{0:T(1024)}, u32[]{:S(2)}) copy-start(f32[896]{0:T(1024)} %get-tuple-element.1141) | copy-start | bytes 10756
  1094.6 30.4 %copy-start.362 = (f32[896]{0:T(1024)S(1)}, f32[896]{0:T(1024)}, u32[]{:S(2)}) copy-start(f32[896]{0:T(1024)} %get-tuple-element.1140) | copy-start | bytes 10756
  1094.6 30.5 %copy-start.371 = (f32[896]{0:T(1024)S(1)}, f32[896]{0:T(1024)}, u32[]{:S(2)}) copy-start(f32[896]{0:T(1024)} %get-tuple-element.1116) | copy-start | bytes 10756
  1094.6 30.5 %copy-start.370 = (f32[896]{0:T(1024)S(1)}, f32[896]{0:T(1024)}, u32[]{:S(2)}) copy-start(f32[896]{0:T(1024)} %get-tuple-element.1118) | copy-start | bytes 10756
  1094.6 30.5 %copy-start.369 = (f32[896]{0:T(1024)S(1)}, f32[896]{0:T(1024)}, u32[]{:S(2)}) copy-start(f32[896]{0:T(1024)} %get-tuple-element.1117) | copy-start | bytes 10756
  1094.7 30.5 %copy-start.368 = (f32[896]{0:T(1024)S(1)}, f32[896]{0:T(1024)}, u32[]{:S(2)}) copy-start(f32[896]{0:T(1024)} %get-tuple-element.1145) | copy-start | bytes 10756
  1094.7 30.5 %copy-start.367 = (f32[896]{0:T(1024)S(1)}, f32[896]{0:T(1024)}, u32[]{:S(2)}) copy-start(f32[896]{0:T(1024)} %get-tuple-element.1144) | copy-start | bytes 10756
  1094.7 30.5 %copy-start.376 = (f32[896]{0:T(1024)S(1)}, f32[896]{0:T(1024)}, u32[]{:S(2)}) copy-start(f32[896]{0:T(1024)} %get-tuple-element.1119) | copy-start | bytes 10756
  1094.7 30.5 %copy-start.375 = (f32[896]{0:T(1024)S(1)}, f32[896]{0:T(1024)}, u32[]{:S(2)}) copy-start(f32[896]{0:T(1024)} %get-tuple-element.1121) | copy-start | bytes 10756
  1094.7 30.5 %copy-start.374 = (f32[896]{0:T(1024)S(1)}, f32[896]{0:T(1024)}, u32[]{:S(2)}) copy-start(f32[896]{0:T(1024)} %get-tuple-element.1120) | copy-start | bytes 10756
  1094.7 30.6 %copy-start.373 = (f32[896]{0:T(1024)S(1)}, f32[896]{0:T(1024)}, u32[]{:S(2)}) copy-start(f32[896]{0:T(1024)} %get-tuple-element.1147) | copy-start | bytes 10756
  1094.7 30.6 %copy-start.372 = (f32[896]{0:T(1024)S(1)}, f32[896]{0:T(1024)}, u32[]{:S(2)}) copy-start(f32[896]{0:T(1024)} %get-tuple-element.1146) | copy-start | bytes 10756
  1176.4 84.2 %copy-start.387 = (f32[2,256]{1,0:T(2,128)S(1)}, f32[2,256]{1,0:T(2,128)}, u32[]{:S(2)}) copy-start(f32[2,256]{1,0:T(2,128)} %get-tuple-element.1465) | copy-start | bytes 6148
  1176.4 84.2 %copy-start.388 = (f32[2,256]{1,0:T(2,128)S(1)}, f32[2,256]{1,0:T(2,128)}, u32[]{:S(2)}) copy-start(f32[2,256]{1,0:T(2,128)} %get-tuple-element.1515) | copy-start | bytes 6148
  1176.4 84.3 %copy-start.389 = (f32[2,256]{1,0:T(2,128)S(1)}, f32[2,256]{1,0:T(2,128)}, u32[]{:S(2)}) copy-start(f32[2,256]{1,0:T(2,128)} %get-tuple-element.1513) | copy-start | bytes 6148
  (385 other events, 1924.3 us)
Sparse Core Ops, SparseCore 0:
  10.8 59.1 all-gather.20
  72.8 55.0 all-gather.24
  142.6 61.5 all-gather.26
  205.6 63.2 all-gather.32
  270.3 62.7 all-gather.30
  334.4 62.0 all-gather.28
  399.3 54.8 all-gather.22
  494.7 62.3 all-gather.34
  558.7 62.1 all-gather.36
  622.3 62.1 all-gather.38
  686.0 62.1 all-gather.40
  899.3 6.5 reduce-scatter.11
  919.2 6.5 reduce-scatter.15
  940.4 6.5 reduce-scatter.17
  989.5 6.5 reduce-scatter.13
  1000.6 122.8 reduce-scatter.27
  1127.0 49.4 all-reduce.61
  1182.5 128.7 reduce-scatter.25
  1316.8 126.7 reduce-scatter.19
  1449.4 120.4 reduce-scatter.23
  1575.4 126.6 reduce-scatter.21
where the time goes:
time: 1730 us; the launch traced here: 1710 us
  waiting for transfers between devices  563 us (33%)
  matrix products  328 us (19%)
  other arithmetic  319 us (18%)
  local copies, waits for them, and re-layouts  241 us (14%)
  blocking collectives  214 us (12%)
  starting transfers between devices  23.2 us (1%)
  between operations  19.9 us (1%)
    reduce_scatter x1, waiting for transfers between devices, combine_gradient_parts(): lax.psum_scatter(large_terms[0], ('shard', 'context'), scatter_dimension=...  132 us
    reduce_scatter x1, waiting for transfers between devices, combine_gradient_parts(): lax.psum_scatter(large_terms[1], ('shard', 'context'), scatter_dimension=...  132 us
    reduce_scatter x1, waiting for transfers between devices, combine_gradient_parts(): lax.psum_scatter(large_terms[2], ('shard', 'context'), scatter_dimension=...  126 us
    dot_general x12, matrix products, output_part(): within = jnp.einsum('hij,hjp->hip', mixing, values, precision=HIGHEST)  120 us
    psum x1, blocking collectives, combine_gradient_parts(): lax.psum((small_terms[0], small_terms[1], small_terms[2], small_terms[3],...  78.8 us
    another operation x52, other arithmetic  76.6 us
    select_n x32, other arithmetic, lap(): return jax.tree.map(lambda a, b: jnp.where(reached, a, b), new, before)  76.4 us
    another operation x82, local copies, waits for them, and re-layouts  52 us
  transfers between devices with their start and end apart: 29, of which 11 were waited for; matrix products, arithmetic and copies ran while one was open for 39% of the time, Pallas kernels for 0%

commit v1 on v0

v1 whole, which is shorter than its diff:
```python
import functools

import jax
import jax.numpy as jnp
import numpy as np
from jax import lax
from jax.experimental import pallas as pl
from jax.experimental.pallas import tpu as pltpu
from jax.sharding import PartitionSpec as P

EPSILON = 1e-05
F32, BF16 = jnp.float32, jnp.bfloat16
HEAD = 64
LANES = 128
HALO = 16
GONE = -1e30
VMEM_BYTES = 60 * 1024 * 1024


def mm(left, right):
    return jnp.dot(left, right, preferred_element_type=F32)


def mm_nt(left, right):
    return lax.dot_general(left, right, (((1,), (1,)), ((), ())), preferred_element_type=F32)


def mm_tn(left, right):
    return lax.dot_general(left, right, (((0,), (0,)), ((), ())), preferred_element_type=F32)


def parts_of(value, count):
    parts = []
    for _ in range(count - 1):
        parts.append(value.astype(BF16))
        value = value - parts[-1].astype(F32)
    return parts + [value.astype(BF16)]


def pick(value, ones, count=2):
    return sum(mm(part, ones) for part in parts_of(value, count))


def pick_left(ones, value, count=3):
    return sum(mm(ones, part) for part in parts_of(value, count))


def softplus(value):
    return jnp.maximum(value, 0.0) + jnp.log1p(jnp.exp(-jnp.abs(value)))


def sigmoid(value):
    return 1.0 / (1.0 + jnp.exp(-value))


def column_blocks(width):
    return [(at, min(LANES, width - at)) for at in range(0, width, LANES)]


def row_index(length):
    return lax.broadcasted_iota(jnp.int32, (length, LANES), 0).astype(F32)


def is_first_step():
    return pl.program_id(0) == 0


def is_last_step():
    return pl.program_id(0) == pl.num_programs(0) - 1


def half_masks(width):
    lane = lax.broadcasted_iota(jnp.int32, (1, width), 1)
    return [(lane // HEAD) == k for k in range(width // HEAD)]


def normalised(hidden, gain):
    scale = lax.rsqrt(jnp.mean(hidden * hidden, -1, keepdims=True) + EPSILON)
    return hidden * scale * gain, scale


def forward_local(hid, halo, age, norm_in, w_in, taps, heads, spread, tri,
                  normed, raw, pre, dt_raw, cum, local, decay, act):
    length = hid.shape[1]
    channels = taps.shape[1]
    bc_width = 2 * LANES
    normed[0, :HALO] = normalised(halo[0].astype(F32), norm_in[...])[0].astype(BF16)
    for at in range(0, length, 64):
        rows = normalised(hid[0, at : at + 64].astype(F32), norm_in[...])[0]
        normed[0, HALO + at : HALO + at + 64] = rows.astype(BF16)
    raw[0, :, :bc_width] = mm(normed[0], w_in[:, :bc_width])
    raw[0, :, bc_width:] = mm(normed[0], w_in[:, bc_width + LANES :])
    dt_raw[0] = mm(normed[0, HALO:], w_in[:, bc_width : bc_width + LANES])
    for at, width in column_blocks(channels):
        cols = slice(at, at + width)
        running = jnp.broadcast_to(taps[4:5, cols], (length, width))
        for lag in range(4):
            tapped = raw[0, HALO - lag : HALO - lag + length, cols]
            if lag:
                tapped = jnp.where(age[0, :, :width] >= lag, tapped, 0.0)
            running = running + taps[lag : lag + 1, cols] * tapped
        pre[0, :, cols] = running
        act[:, cols] = running * sigmoid(running)
    step = softplus(dt_raw[0] + heads[0:1])
    total = pick_left(tri[...], -jnp.exp(heads[1:2]) * step)
    cum[0] = total
    last, age_last = total[length - 1 :], age[0, length - 1 :]
    open_end = row_index(length) - (length - 1) + age_last >= 0
    weight = jnp.where(open_end, jnp.exp(last - total), 0.0) * step
    weighted = (act[:, bc_width:] * pick(weight, spread[...])).astype(BF16)
    local[0] = mm_tn(act[:, :LANES].astype(BF16), weighted).astype(BF16)
    kept = jnp.where(age_last > length - 1, jnp.exp(last), 0.0)
    decay[0] = pick(jnp.broadcast_to(kept, (8, LANES)), spread[...], 3)


def forward_mix(pre, dt_raw, cum, age, state_in, normed, out_grad, w_z, w_out_t, norm_gate, skip, heads, spread,
                mixer, gate, grad_gn, part, stats, near, seg, pair, carried, step_x, gated_low):
    length, inner = mixer.shape[1:]
    bc_width = 2 * LANES
    readout = pre[0, :, LANES:bc_width]
    readout = (readout * sigmoid(readout)).astype(BF16)
    inputs_b = pre[0, :, :LANES]
    inputs_b = (inputs_b * sigmoid(inputs_b)).astype(BF16)
    gate[0] = mm(normed[0, HALO:], w_z[...])
    grad_gn[0] = mm(out_grad[0], w_out_t[...])
    pair[...] = mm_nt(readout, inputs_b)
    row = lax.broadcasted_iota(jnp.int32, (length, length), 0)
    col = lax.broadcasted_iota(jnp.int32, (length, length), 1)
    back = (row - col).astype(F32)
    seg[...] = jnp.where((back >= 0) & (back <= age[0][:, :1]), 0.0, GONE)
    total = cum[0]
    total_t = total.T
    step = softplus(dt_raw[0] + heads[0:1])
    step_x[...] = pick(step, spread[...])
    open_start = age[0] > row_index(length)
    carried[...] = pick(jnp.where(open_start, jnp.exp(total), 0.0), spread[...])
    carried[...] = carried[...] * mm(readout, state_in[0])
    squares = jnp.zeros((length, 1), F32)
    products = jnp.zeros((length, 1), F32)
    for at, width in column_blocks(inner):
        cols = slice(at, at + width)
        x_pre = pre[0, :, bc_width + at : bc_width + at + width]
        values = x_pre * sigmoid(x_pre)
        fed = (values * step_x[:, cols]).astype(BF16)
        masks = half_masks(width)
        near[:, :width] = carried[:, cols] + skip[:, cols] * values
        for start in range(0, length, LANES):
            stop = start + LANES
            found = near[start:stop, :width]
            for k, mask in enumerate(masks):
                head = at // HEAD + k
                spread_log = total[start:stop, head : head + 1] - total_t[head : head + 1, :stop]
                mixing = pair[start:stop, :stop] * jnp.exp(spread_log + seg[start:stop, :stop])
                found = found + mm(mixing.astype(BF16), jnp.where(mask, fed[:stop], 0))
            near[start:stop, :width] = found
        mixed = near[:, :width]
        mixer[0, :, cols] = mixed
        raw_gate = gate[0, :, cols]
        gated = mixed * (raw_gate * sigmoid(raw_gate))
        weighted = gated * norm_gate[:, cols]
        gated_low[:, cols] = weighted.astype(BF16)
        squares = squares + jnp.sum(gated * gated, 1, keepdims=True)
        products = products + jnp.sum(grad_gn[0, :, cols] * weighted, 1, keepdims=True)
    part[0] = mm_nt(gated_low[...], w_out_t[...]).astype(BF16)
    lane = lax.broadcasted_iota(jnp.int32, (length, LANES), 1)
    stats[0] = jnp.where(lane == 0, squares, jnp.where(lane == 1, products, 0.0))


def backward_local(inner_all, mixer, gate, grad_gn, stats, pre, dt_raw, cum, age, age_row, state_in, normed, out_grad,
                   norm_gate, skip, heads, spread, gather,
                   grad_fed, grad_mix, grad_gate, grad_cum, grad_bc, grad_state, grad_wz, grad_wo, sums,
                   sum_z, sum_o, near, seg, pair, grad_pair, carried, step_x, gated_low, from_state):
    length, inner = mixer.shape[1:]
    bc_width = 2 * LANES

    @pl.when(is_first_step())
    def _():
        sum_z[...] = jnp.zeros_like(sum_z)
        sum_o[...] = jnp.zeros_like(sum_o)
        sums[...] = jnp.zeros_like(sums)

    readout = pre[0, :, LANES:bc_width]
    readout = (readout * sigmoid(readout)).astype(BF16)
    inputs_b = pre[0, :, :LANES]
    inputs_b = (inputs_b * sigmoid(inputs_b)).astype(BF16)
    pair[...] = mm_nt(inputs_b, readout)
    grad_pair[...] = jnp.zeros_like(grad_pair)
    row = lax.broadcasted_iota(jnp.int32, (length, length), 0)
    col = lax.broadcasted_iota(jnp.int32, (length, length), 1)
    back = (col - row).astype(F32)
    seg[...] = jnp.where((back >= 0) & (back <= age_row[0][:1]), 0.0, GONE)
    total = cum[0]
    total_t = total.T
    step = softplus(dt_raw[0] + heads[0:1])
    step_x[...] = pick(step, spread[...])
    open_start = age[0] > row_index(length)
    carried[...] = pick(jnp.where(open_start, jnp.exp(total), 0.0), spread[...])
    scale = lax.rsqrt(stats[0][:, :1] / inner_all + EPSILON)
    pull = scale * scale * scale * (stats[0][:, 1:2] / inner_all)
    rows_sum = jnp.zeros((length, LANES), F32)
    for at, width in column_blocks(inner):
        cols = slice(at, at + width)
        x_pre = pre[0, :, bc_width + at : bc_width + at + width]
        values = x_pre * sigmoid(x_pre)
        fed = (values * step_x[:, cols]).astype(BF16)
        mixed = mixer[0, :, cols]
        raw_gate = gate[0, :, cols]
        logistic = sigmoid(raw_gate)
        acted = raw_gate * logistic
        gated = mixed * acted
        grad_out = grad_gn[0, :, cols]
        gated_scaled = gated * scale
        gated_low[:, cols] = (gated_scaled * norm_gate[:, cols]).astype(BF16)
        grad_gated = scale * (grad_out * norm_gate[:, cols]) - gated * pull
        grad_gate[0, :, cols] = (grad_gated * mixed * (logistic * (1.0 + raw_gate * (1.0 - logistic)))).astype(BF16)
        mix_low = (grad_gated * acted).astype(BF16)
        grad_mix[0, :, cols] = mix_low
        mix_wide = mix_low.astype(F32)
        sums[0:1, cols] += jnp.sum(grad_out * gated_scaled, 0, keepdims=True)
        sums[1:2, cols] += jnp.sum(mix_wide * values, 0, keepdims=True)
        rows_sum = rows_sum + pick(mix_wide * (mixed - skip[:, cols] * values), gather[cols])
        from_state[:, cols] = (carried[:, cols] * mix_wide).astype(BF16)
        masks = half_masks(width)
        for start in range(0, length, LANES):
            stop = start + LANES
            found = jnp.zeros((LANES, width), F32)
            for k, mask in enumerate(masks):
                head = at // HEAD + k
                spread_log = total_t[head : head + 1, start:] - total[start:stop, head : head + 1]
                decayed = jnp.exp(spread_log + seg[start:stop, start:])
                mixing = (pair[start:stop, start:] * decayed).astype(BF16)
                grad_mixing = mm_nt(jnp.where(mask, fed[start:stop], 0), mix_low[start:])
                grad_pair[start:stop, start:] += grad_mixing * decayed
                found = found + mm(mixing, jnp.where(mask, mix_low[start:], 0))
            near[start:stop, :width] = found
        grad_fed[0, :, cols] = near[:, :width]
        rows_sum = rows_sum - pick(near[:, :width] * fed.astype(F32), gather[cols])
    grad_cum[0] = rows_sum
    pair_low = grad_pair[...].astype(BF16)
    grad_bc[0, :, :LANES] = mm(pair_low, readout)
    grad_bc[0, :, LANES:] = mm_tn(pair_low, inputs_b) + mm_nt(from_state[...], state_in[0])
    grad_state[0] = mm_tn(readout, from_state[...]).astype(BF16)
    sum_z[...] += mm_tn(normed[0, HALO:], grad_gate[0])
    sum_o[...] += mm_tn(out_grad[0], gated_low[...])

    @pl.when(is_last_step())
    def _():
        grad_wz[...] = sum_z[...].astype(BF16)
        grad_wo[...] = sum_o[...].astype(BF16)


def backward_finish(grad_later, state_in, pre, raw, dt_raw, cum, age, grad_fed, grad_mix, grad_cum, grad_bc, grad_gate,
                    normed, hid, halo, w_in, w_z, taps, skip, norm_in, heads, spread, gather, tri_up,
                    grad_normed, grad_halo, grad_w, conv_sums, head_sums, norm_sums,
                    sum_w, step_x, open_x, from_state, fed_state, slope, age_long, grad_in, wide):
    length, inner = grad_fed.shape[1:]
    channels = taps.shape[1]
    bc_width = 2 * LANES
    lead = HALO + length

    @pl.when(is_first_step())
    def _():
        sum_w[...] = jnp.zeros_like(sum_w)
        conv_sums[...] = jnp.zeros_like(conv_sums)
        head_sums[...] = jnp.zeros_like(head_sums)
        norm_sums[...] = jnp.zeros_like(norm_sums)
        slope[:HALO] = jnp.zeros((HALO, channels), F32)
        slope[lead:] = jnp.zeros((8, channels), F32)
        age_long[:HALO] = jnp.zeros((HALO, LANES), F32)
        age_long[lead:] = jnp.zeros((8, LANES), F32)
        grad_in[:HALO, bc_width : bc_width + LANES] = jnp.zeros((HALO, LANES), BF16)

    age_long[HALO:lead] = age[0]
    total = cum[0]
    step_raw = dt_raw[0] + heads[0:1]
    step = softplus(step_raw)
    rate = -jnp.exp(heads[1:2])
    step_x[...] = pick(step, spread[...])
    last, age_last = total[length - 1 :], age[0, length - 1 :]
    open_end = row_index(length) - (length - 1) + age_last >= 0
    open_x[...] = pick(jnp.where(open_end, jnp.exp(last - total), 0.0), spread[...])
    b_pre = pre[0, :, :LANES]
    inputs_b = (b_pre * sigmoid(b_pre)).astype(BF16)
    from_state[...] = open_x[...] * mm(inputs_b, grad_later[0])
    state_sum = jnp.zeros((length, LANES), F32)
    step_sum = jnp.zeros((length, LANES), F32)
    for at, width in column_blocks(inner):
        cols = slice(at, at + width)
        x_pre = pre[0, :, bc_width + at : bc_width + at + width]
        logistic = sigmoid(x_pre)
        values = x_pre * logistic
        fed = values * step_x[:, cols]
        fed_state[:, cols] = (fed * open_x[:, cols]).astype(BF16)
        arrived = from_state[:, cols]
        grad = grad_fed[0, :, cols] + arrived
        state_sum = state_sum + pick(fed * arrived, gather[cols])
        step_sum = step_sum + pick(values * grad, gather[cols])
        grad_values = grad * step_x[:, cols] + skip[:, cols] * grad_mix[0, :, cols].astype(F32)
        slope[HALO:lead, bc_width + at : bc_width + at + width] = grad_values * (
            logistic * (1.0 + x_pre * (1.0 - logistic))
        )
    for at, extra in ((0, mm_nt(fed_state[...], grad_later[0])), (LANES, 0.0)):
        cols = slice(at, at + LANES)
        bc_pre = pre[0, :, cols]
        logistic = sigmoid(bc_pre)
        slope[HALO:lead, cols] = (grad_bc[0, :, cols] + extra) * (logistic * (1.0 + bc_pre * (1.0 - logistic)))
    kept = jnp.where(age_last > length - 1, jnp.exp(last), 0.0)
    met = jnp.sum(grad_later[0].astype(F32) * state_in[0].astype(F32), 0, keepdims=True)
    met = pick(jnp.broadcast_to(met, (8, inner)), gather[...], 3)[:1]
    end = met * kept + jnp.sum(state_sum, 0, keepdims=True)
    grad_a = pick_left(tri_up[...], grad_cum[0] - state_sum) + end
    head_sums[1:2] += jnp.sum(grad_a * rate * step, 0, keepdims=True)
    grad_step = (step_sum + grad_a * rate) * sigmoid(step_raw)
    head_sums[0:1] += jnp.sum(grad_step, 0, keepdims=True)
    grad_in[HALO:, bc_width : bc_width + LANES] = grad_step.astype(BF16)
    for at, width in column_blocks(channels):
        cols = slice(at, at + width)
        shifted = at if at < bc_width else at + LANES
        own = slope[HALO:lead, cols]
        total_in = taps[0:1, cols] * slope[:lead, cols]
        conv_sums[0:1, cols] += jnp.sum(own * raw[0, HALO:, cols], 0, keepdims=True)
        for lag in range(1, 4):
            kept_lag = jnp.where(age[0, :, :width] >= lag, own, 0.0)
            conv_sums[lag : lag + 1, cols] += jnp.sum(
                kept_lag * raw[0, HALO - lag : lead - lag, cols], 0, keepdims=True
            )
            later = jnp.where(age_long[lag : lead + lag, :width] >= lag, slope[lag : lead + lag, cols], 0.0)
            total_in = total_in + taps[lag : lag + 1, cols] * later
        conv_sums[4:5, cols] += jnp.sum(own, 0, keepdims=True)
        grad_in[:, shifted : shifted + width] = total_in.astype(BF16)
    wide[...] = mm_nt(grad_in[...], w_in[...])
    wide[HALO:] += mm_nt(grad_gate[0], w_z[...])
    hidden = halo[0].astype(F32)
    scale = normalised(hidden, 1.0)[1]
    norm_sums[0:1] += jnp.sum(wide[:HALO] * hidden * scale, 0, keepdims=True)
    for at in range(0, length, 64):
        hidden = hid[0, at : at + 64].astype(F32)
        scale = normalised(hidden, 1.0)[1]
        norm_sums[0:1] += jnp.sum(wide[HALO + at : HALO + at + 64] * hidden * scale, 0, keepdims=True)
    grad_halo[0] = wide[:HALO].astype(BF16)
    grad_normed[0] = wide[HALO:].astype(BF16)
    sum_w[...] += mm_tn(normed[0], grad_in[...])

    @pl.when(is_last_step())
    def _():
        grad_w[...] = sum_w[...].astype(BF16)


def finish(inner_all, hid, out_grad, stats, norm_in, own_part, other_part, own_grad, other_grad, own_tail, other_tail,
           out, in_grad, total):
    length = hid.shape[1]

    def added(own, others, rows):
        found = own[0, rows].astype(F32)
        for k in range(others.shape[0]):
            found = found + others[k, 0, rows].astype(F32)
        return found

    everything = slice(None)
    total[...] = added(own_grad, other_grad, everything)
    total[length - HALO :] += added(own_tail, other_tail, everything)
    for at in range(0, length, 64):
        rows = slice(at, at + 64)
        hidden = hid[0, rows].astype(F32)
        scale_gate = lax.rsqrt(stats[0, rows, :1] / inner_all + EPSILON)
        out[0, rows] = (hidden + scale_gate * added(own_part, other_part, rows)).astype(BF16)
        scale = normalised(hidden, 1.0)[1]
        weighted = total[rows] * norm_in[...]
        inner_mean = jnp.mean(weighted * hidden, -1, keepdims=True)
        in_grad[0, rows] = (
            out_grad[0, rows].astype(F32) + scale * weighted - hidden * (scale * scale * scale * inner_mean)
        ).astype(BF16)


def by_piece(array):
    rest = array.shape[1:]
    return pl.BlockSpec((1,) + rest, lambda i: (i,) + (0,) * len(rest))


def by_piece_second(array):
    rest = array.shape[2:]
    return pl.BlockSpec((array.shape[0], 1) + rest, lambda i: (0, i) + (0,) * len(rest))


def fixed(array):
    return pl.BlockSpec(array.shape, lambda i: (0,) * len(array.shape))


def call(kernel, pieces, inputs, outputs, scratch, name):
    return pl.pallas_call(
        kernel,
        grid=(pieces,),
        in_specs=[cut(array) for array, cut in inputs],
        out_specs=[cut(shape) for shape, cut in outputs],
        out_shape=[shape for shape, _ in outputs],
        scratch_shapes=[pltpu.VMEM(shape, kind) for shape, kind in scratch],
        compiler_params=pltpu.CompilerParams(vmem_limit_bytes=VMEM_BYTES),
        name=name,
    )(*[array for array, _ in inputs])


def shaped(kind, *dims):
    return jax.ShapeDtypeStruct(dims, kind)


def gather_rows(rows):
    return lax.all_gather(rows, ("shard", "context"), axis=0, tiled=True)


def scatter_rows(rows):
    return lax.psum_scatter(rows.astype(F32), ("shard", "context"), scatter_dimension=0, tiled=True)


def passed_along(value, by):
    length = lax.axis_size("context")
    return lax.ppermute(value, "context", [(i, i + by) for i in range(length) if 0 <= i + by < length])


def chain(local, decay, by):
    arrived = jnp.zeros_like(local)
    for _ in range(lax.axis_size("context") - 1):
        leaving = decay[:, :1] * arrived.astype(F32) + local.astype(F32)
        arrived = passed_along(leaving.astype(BF16), by)
    return arrived


def exchange(value):
    everything = lax.all_gather(value, "tensor")
    return everything[0], everything[1:]


def shards(inner_all, hidden_in, out_grad, doc_start, norm_in, w_z, w_x, w_bc, w_dt, conv_x, conv_bc, dt_bias, a_log,
           skip_d, norm_gate, w_out):
    micro, per_device, length, model = hidden_in.shape
    pieces = micro * per_device
    inner = w_z.shape[1]
    head_count = w_dt.shape[1]
    bc_width = w_bc.shape[1] * lax.axis_size("tensor")
    channels = bc_width + inner
    in_width = channels + LANES
    lead = HALO + length
    offset = lax.axis_index("context") * length

    head_of = np.arange(inner) // HEAD
    gather = jnp.asarray(head_of[:, None] == np.arange(LANES)[None], BF16)
    spread = jnp.asarray(head_of[None] == np.arange(LANES)[:, None], BF16)
    tri = jnp.asarray(np.tril(np.ones((length, length))), BF16)
    tri_up = jnp.asarray(np.triu(np.ones((length, length))), BF16)

    def head_row(row):
        return jnp.pad(row, (0, LANES - head_count))

    heads = jnp.stack([head_row(dt_bias), head_row(a_log)] + [jnp.zeros((LANES,), F32)] * 6)
    skip = jnp.repeat(skip_d, HEAD)[None]
    norm_in, norm_gate = norm_in[None], norm_gate[None]
    conv_bc_all = lax.all_gather(conv_bc, "tensor", axis=1, tiled=True)
    taps = jnp.pad(jnp.concatenate([conv_bc_all, conv_x], 1), ((0, 3), (0, 0)))
    w_bc_all = lax.all_gather(w_bc, "tensor", axis=1, tiled=True)
    w_dt_wide = jnp.pad(w_dt, ((0, 0), (0, LANES - head_count)))
    w_in = gather_rows(jnp.concatenate([w_bc_all, w_dt_wide, w_x], 1))
    w_z_all = gather_rows(w_z)
    w_out_t = gather_rows(w_out.T)

    hid = hidden_in.reshape(pieces, length, model)
    seed = out_grad.reshape(pieces, length, model)
    halo = passed_along(hid[:, length - HALO :], 1)
    ages = (offset + jnp.arange(length, dtype=jnp.int32) - doc_start.reshape(pieces, length)).astype(F32)
    age = jnp.broadcast_to(ages[:, :, None], (pieces, length, LANES))
    age_row = jnp.broadcast_to(ages[:, None, :], (pieces, 8, length))

    token = functools.partial(shaped, F32, pieces, length)
    token_low = functools.partial(shaped, BF16, pieces, length)
    state = shaped(BF16, pieces, LANES, inner)
    normed, raw, pre, dt_raw, cum, local, decay = call(
        forward_local, pieces,
        [(hid, by_piece), (halo, by_piece), (age, by_piece), (norm_in, fixed), (w_in, fixed), (taps, fixed),
         (heads, fixed), (spread, fixed), (tri, fixed)],
        [(shaped(BF16, pieces, lead, model), by_piece), (shaped(F32, pieces, lead, channels), by_piece),
         (token(channels), by_piece), (token(LANES), by_piece), (token(LANES), by_piece), (state, by_piece),
         (shaped(F32, pieces, 8, inner), by_piece)],
        [((length, channels), F32)], "forward_local",
    )

    state_in = chain(local, decay, 1)

    square = ((length, length), F32)
    token_wide = ((length, inner), F32)
    token_narrow = ((length, inner), BF16)
    mixer, gate, grad_gn, part, stats = call(
        forward_mix, pieces,
        [(pre, by_piece), (dt_raw, by_piece), (cum, by_piece), (age, by_piece), (state_in, by_piece), (normed, by_piece),
         (seed, by_piece), (w_z_all, fixed), (w_out_t, fixed), (norm_gate, fixed), (skip, fixed), (heads, fixed),
         (spread, fixed)],
        [(token(inner), by_piece), (token(inner), by_piece), (token(inner), by_piece), (token_low(model), by_piece),
         (token(LANES), by_piece)],
        [((length, LANES), F32), square, square, token_wide, token_wide, token_narrow], "forward_mix",
    )

    stats = lax.psum(stats, "tensor")

    grad_fed, grad_mix, grad_gate, grad_cum, grad_bc, grad_state, grad_wz, grad_wo, sums = call(
        functools.partial(backward_local, inner_all), pieces,
        [(mixer, by_piece), (gate, by_piece), (grad_gn, by_piece), (stats, by_piece), (pre, by_piece),
         (dt_raw, by_piece), (cum, by_piece), (age, by_piece), (age_row, by_piece), (state_in, by_piece),
         (normed, by_piece), (seed, by_piece), (norm_gate, fixed), (skip, fixed), (heads, fixed), (spread, fixed),
         (gather, fixed)],
        [(token(inner), by_piece), (token_low(inner), by_piece), (token_low(inner), by_piece), (token(LANES), by_piece),
         (token(bc_width), by_piece), (state, by_piece), (shaped(BF16, model, inner), fixed),
         (shaped(BF16, model, inner), fixed), (shaped(F32, 8, inner), fixed)],
        [((model, inner), F32), ((model, inner), F32), ((length, LANES), F32), square, square, square, token_wide,
         token_wide, token_narrow, token_narrow], "backward_local",
    )

    grad_later = chain(grad_state, decay, -1)

    grad_normed, grad_halo, grad_w, conv_sums, head_sums, norm_sums = call(
        backward_finish, pieces,
        [(grad_later, by_piece), (state_in, by_piece), (pre, by_piece), (raw, by_piece), (dt_raw, by_piece),
         (cum, by_piece), (age, by_piece), (grad_fed, by_piece), (grad_mix, by_piece), (grad_cum, by_piece),
         (grad_bc, by_piece), (grad_gate, by_piece), (normed, by_piece), (hid, by_piece), (halo, by_piece),
         (w_in, fixed), (w_z_all, fixed), (taps, fixed), (skip, fixed), (norm_in, fixed), (heads, fixed),
         (spread, fixed), (gather, fixed), (tri_up, fixed)],
        [(token_low(model), by_piece), (shaped(BF16, pieces, HALO, model), by_piece),
         (shaped(BF16, model, in_width), fixed), (shaped(F32, 8, channels), fixed), (shaped(F32, 8, LANES), fixed),
         (shaped(F32, 8, model), fixed)],
        [((model, in_width), F32), token_wide, token_wide, token_wide, token_narrow,
         ((lead + 8, channels), F32), ((lead + 8, LANES), F32), ((lead, in_width), BF16), ((lead, model), F32)],
        "backward_finish",
    )

    own_part, other_part = exchange(part)
    own_grad, other_grad = exchange(grad_normed)
    own_tail, other_tail = exchange(passed_along(grad_halo, -1))
    out, in_grad = call(
        functools.partial(finish, inner_all), pieces,
        [(hid, by_piece), (seed, by_piece), (stats, by_piece), (norm_in, fixed), (own_part, by_piece),
         (other_part, by_piece_second), (own_grad, by_piece), (other_grad, by_piece_second), (own_tail, by_piece),
         (other_tail, by_piece_second)],
        [(token_low(model), by_piece), (token_low(model), by_piece)],
        [((length, model), F32)], "finish",
    )

    mine = lax.axis_index("tensor")
    own_bc = w_bc.shape[1]
    grad_w = scatter_rows(grad_w)
    grad_w_bc = lax.psum_scatter(grad_w[:, :bc_width], "tensor", scatter_dimension=1, tiled=True)
    norm_sums, conv_bc_sums = lax.psum((norm_sums[0], conv_sums[:5, :bc_width]), ("shard", "context", "tensor"))
    conv_x_sums, head_sums, sums = lax.psum((conv_sums[:5, bc_width:], head_sums[:2], sums[:2]), ("shard", "context"))
    return (
        out.reshape(hidden_in.shape),
        in_grad.reshape(hidden_in.shape),
        norm_sums,
        scatter_rows(grad_wz),
        grad_w[:, bc_width + LANES :],
        grad_w_bc,
        grad_w[:, bc_width : bc_width + head_count],
        conv_x_sums,
        lax.dynamic_slice_in_dim(conv_bc_sums, mine * own_bc, own_bc, 1),
        head_sums[0, :head_count],
        head_sums[1, :head_count],
        jnp.sum(sums[1].reshape(head_count, HEAD), 1),
        sums[0],
        scatter_rows(grad_wo).T,
    )


def solution(mesh):
    whole = P(None, "shard", "context", None)
    rows = P(("shard", "context"), "tensor")
    lanes = P(None, "tensor")
    heads = P("tensor")
    w_out = P("tensor", ("shard", "context"))
    inputs = (whole, whole, P(None, "shard", "context"), P(), rows, rows, rows, rows, lanes, lanes, heads, heads, heads, heads, w_out)
    outputs = (whole, whole, P(), rows, rows, rows, rows, lanes, lanes, heads, heads, heads, heads, w_out)

    def placed(*arrays):
        inner_all = arrays[4].shape[1]
        return jax.shard_map(
            functools.partial(shards, inner_all), mesh=mesh, in_specs=inputs, out_specs=outputs, check_vma=False
        )(*arrays)

    return placed
```

time: 1730 us -> 916 us (0.53); the launches traced: 1710 us -> 915 us
  matrix products: 328 us -> 0 us
  other arithmetic: 319 us -> 20 us
  local copies, waits for them, and re-layouts: 241 us -> 31.4 us
  Pallas kernels: 0 us -> 139 us
  blocking collectives: 214 us -> 123 us
    dot_general x108 -> x0, matrix products: 328 us -> none  [the longest x12 120 us: output_part(): within = jnp.einsum('hij,hjp->hip', mixing, values, precision=HIGHEST)]
    ppermute x8, waiting for transfers between devices: 3.02 us -> 198 us  [passed_along(): lax.ppermute(value, 'context', [(i, i + by) for i in range(length) if 0 <...]
    reduce_scatter x8 -> x4, waiting for transfers between devices: 430 us -> 257 us  [the longest x3 247 us: scatter_rows(): lax.psum_scatter(rows.astype(F32), ('shard', 'context'), scatter_dimensio...]
    pallas_call x0 -> x5, Pallas kernels: none -> 139 us  [call(): pl.pallas_call(kernel, grid=(pieces,), in_specs=[cut(array) for array, cu...]
    all_gather x10 -> x3, blocking collectives: 130 us -> 6.24 us  [the longest x1 2.24 us: shards(): w_bc_all = lax.all_gather(w_bc, 'tensor', axis=1, tiled=True)]
    another operation x56 -> x1, other arithmetic: 86.5 us -> 0.66 us  [shards(): jnp.stack([head_row(dt_bias), head_row(a_log)] + [jnp.zeros((LANES,), F32...]
    select_n x41 -> x0, other arithmetic: 85.3 us -> none  [the longest x32 76.4 us: lap(): return jax.tree.map(lambda a, b: jnp.where(reached, a, b), new, before)]
    reduce_sum x18 -> x1, other arithmetic: 56.9 us -> 0.63 us  [shards(): jnp.sum(sums[1].reshape(head_count, HEAD), 1)]
  transfers between devices with their start and end apart: 29 -> 18, of which waited for: 11 -> 13; matrix products, arithmetic and copies ran while one was open for 39% -> 5% of each run, Pallas kernels for 0% -> 11%
where the time goes in v1:
time: 916 us; the launch traced here: 915 us
  waiting for transfers between devices  563 us (61%)
  Pallas kernels  139 us (15%)
  blocking collectives  123 us (13%)
  local copies, waits for them, and re-layouts  31.4 us (3%)
  starting transfers between devices  23.9 us (3%)
  other arithmetic  20 us (2%)
  between operations  14.4 us (2%)
    reduce_scatter x3, waiting for transfers between devices, scatter_rows(): lax.psum_scatter(rows.astype(F32), ('shard', 'context'), scatter_dimensio...  247 us
    ppermute x8, waiting for transfers between devices, passed_along(): lax.ppermute(value, 'context', [(i, i + by) for i in range(length) if 0 <...  198 us
    pallas_call x5, Pallas kernels, call(): pl.pallas_call(kernel, grid=(pieces,), in_specs=[cut(array) for array, cu...  139 us
    psum x1, blocking collectives, shards(): lax.psum((conv_sums[:5, bc_width:], head_sums[:2], sums[:2]), ('shard', '...  75.8 us
    all_gather x3, waiting for transfers between devices, gather_rows(): return lax.all_gather(rows, ('shard', 'context'), axis=0, tiled=True)  73.3 us
    psum x1, blocking collectives, shards(): lax.psum((norm_sums[0], conv_sums[:5, :bc_width]), ('shard', 'context', '...  41.1 us
    ppermute x8, starting transfers between devices, passed_along(): lax.ppermute(value, 'context', [(i, i + by) for i in range(length) if 0 <...  23.3 us
    psum x1, waiting for transfers between devices, shards(): stats = lax.psum(stats, 'tensor')  20.9 us
  transfers between devices with their start and end apart: 18, of which 13 were waited for; matrix products, arithmetic and copies ran while one was open for 5% of the time, Pallas kernels for 11%

profile of v1, /device:TPU:0, one launch (start us, length us, event | category | flops | bytes accessed | tf_op | source)
XLA Modules:
  0.0 915.2 jit_solution(8952534374530765212)
XLA Ops:
  7.2 2.2 all_gather.33
  9.5 0.8 copy.35
  10.3 1.5 fusion.9
  11.9 0.9 slice.91
  12.8 4.8 collective-permute-start
  17.7 0.7 reshape.84
  18.5 1.3 broadcast_in_dim.11.norm_in
  19.8 1.9 all_gather.35
  21.7 0.7 pad_bitcast_fusion
  22.4 1.4 select_maximum_fusion.taps
  23.8 0.7 maximum_maximum_fusion.heads
  24.4 49.1 %all-gather.9.cloned.1.call-done.w_in = bf16[768,1152]{1,0:T(8,128)(2,1)} async-done(((bf16[48,1152]{1,0:T(8,128)(2,1)}), bf16[768,1152]{1,0:T(8,128)(2,1)}) %all-gather.9.cloned.1.call-update) | async-done | bytes 1769488 | tf_op jit(solution)/shard_map/all_gather | solution.py:407
  73.5 1.3 broadcast_in_dim.10.age
  74.8 19.1 %forward_local.1 = (bf16[8,272,768]{2,1,0:T(8,128)(2,1)}, f32[8,272,1024]{2,1,0:T(8,128)}, f32[8,256,1024]{2,1,0:T(8,128)}, f32[8,256,128]{2,1,0:T(8,128)}, f32[...) custom-call(bf16[8,256,768]{2,1,0:T(8,128)(2,1)} %bitcast.26, ...), custom_call_target="tpu_custom_call" | custom-call | tf_op jit(solution)/shard_map/forward_local/pallas_call | solution.py:390
  93.9 1.1 slice.66
  95.0 1.7 fusion
  96.7 4.0 collective-permute-start.1
  100.8 36.2 %collective-permute-done.1 = bf16[8,128,768]{2,1,0:T(8,128)(2,1)} collective-permute-done((bf16[8,128,768]{2,1,0:T(8,128)(2,1)S(1)}, bf16[8,128,768]{2,1,0:T(8,128)(2,1)}, u32[]{:S(2)}, u32[]{:S(2)}) %collective-permute-start.1) | collective-permute-done | bytes 1572896 | tf_op jit(solution)/shard_map/ppermute | solution.py:416
  137.0 3.0 fusion.1
  140.1 4.7 collective-permute-start.2
  144.9 37.8 %collective-permute-done.2 = bf16[8,128,768]{2,1,0:T(8,128)(2,1)S(1)} collective-permute-done((bf16[8,128,768]{2,1,0:T(8,128)(2,1)}, bf16[8,128,768]{2,1,0:T(8,128)(2,1)S(1)}, u32[]{:S(2)}, u32[]{:S(2)}) %collective-permute-start.2) | collective-permute-done | bytes 1572896 | tf_op jit(solution)/shard_map/ppermute | solution.py:416
  182.6 1.6 fusion.2
  184.3 4.4 collective-permute-start.3
  188.7 0.7 broadcast_in_dim_reshape.3.skip
  190.0 24.2 %all-gather.13.cloned.1.call-done.w_out_t = bf16[768,768]{1,0:T(8,128)(2,1)} async-done(((bf16[48,768]{1,0:T(8,128)(2,1)}), bf16[768,768]{1,0:T(8,128)(2,1)}) %all-gather.13.cloned.1.call-update) | async-done | bytes 1179664 | tf_op jit(solution)/shard_map/all_gather | solution.py:407
  214.1 14.7 %collective-permute-done.3.state_in = bf16[8,128,768]{2,1,0:T(8,128)(2,1)S(1)} collective-permute-done((bf16[8,128,768]{2,1,0:T(8,128)(2,1)}, bf16[8,128,768]{2,1,0:T(8,128)(2,1)S(1)}, u32[]{:S(2)}, u32[]{:S(2)}) %collective-permute-start.3) | collective-permute-done | bytes 1572896 | tf_op jit(solution)/shard_map/ppermute | solution.py:416
  228.8 1.2 copy-done
  230.1 23.5 %forward_mix.1 = (f32[8,256,768]{2,1,0:T(8,128)}, f32[8,256,768]{2,1,0:T(8,128)}, f32[8,256,768]{2,1,0:T(8,128)}, bf16[8,256,768]{2,1,0:T(8,128)(2,1)}, f32[8,256,128]{2,1,0:T(8,128)}) custom-call(f32[8,256,1024]{2,1,0:T(8,128)} %get-tuple-element.43.pre, f32[8,256,128]{2,1,0:T(8,128)} %get-tuple-element.44.dt_raw, f32[8,256,128]{2,1,0:T(8,128)} %get-tuple-element.45.cum, ...), custom_call_target="tpu_custom_call" | custom-call | tf_op jit(solution)/shard_map/forward_mix/pallas_call | solution.py:390
  254.4 20.9 %all-reduce.8.cloned.1.call-done.stats = f32[8,256,128]{2,1,0:T(8,128)} async-done(((f32[8,256,128]{2,1,0:T(8,128)}), f32[8,256,128]{2,1,0:T(8,128)}) %all-reduce.8.cloned.1.call-update) | async-done | bytes 1048592 | tf_op jit(solution)/shard_map/psum | solution.py:499
  275.3 0.6 broadcast_in_dim.26.age_row
  275.9 40.0 %backward_local.1 = (f32[8,256,768]{2,1,0:T(8,128)}, bf16[8,256,768]{2,1,0:T(8,128)(2,1)}, bf16[8,256,768]{2,1,0:T(8,128)(2,1)}, f32[8,256,128]{2,1,0:T(8,128)},...) custom-call(f32[8,256,768]{2,1,0:T(8,128)} %get-tuple-element.51.mix, ...), custom_call_target="tpu_custom_call" | custom-call | tf_op jit(solution)/shard_map/backward_local/pallas_call | solution.py:390
  316.0 1.8 fusion.3
  317.8 1.3 collective-permute-start.4
  319.1 37.2 %collective-permute-done.4 = bf16[8,128,768]{2,1,0:T(8,128)(2,1)S(1)} collective-permute-done((bf16[8,128,768]{2,1,0:T(8,128)(2,1)S(1)}, bf16[8,128,768]{2,1,0:T(8,128)(2,1)S(1)}, u32[]{:S(2)}, u32[]{:S(2)}) %collective-permute-start.4) | collective-permute-done | bytes 1572896 | tf_op jit(solution)/shard_map/ppermute | solution.py:416
  356.8 1.3 collective-permute-start.5
  358.1 36.4 %collective-permute-done.5 = bf16[8,128,768]{2,1,0:T(8,128)(2,1)S(1)} collective-permute-done((bf16[8,128,768]{2,1,0:T(8,128)(2,1)S(1)}, bf16[8,128,768]{2,1,0:T(8,128)(2,1)S(1)}, u32[]{:S(2)}, u32[]{:S(2)}) %collective-permute-start.5) | collective-permute-done | bytes 1572896 | tf_op jit(solution)/shard_map/ppermute | solution.py:416
  395.0 1.5 collective-permute-start.6
  396.5 35.3 %collective-permute-done.6.grad_later = bf16[8,128,768]{2,1,0:T(8,128)(2,1)S(1)} collective-permute-done((bf16[8,128,768]{2,1,0:T(8,128)(2,1)S(1)}, bf16[8,128,768]{2,1,0:T(8,128)(2,1)S(1)}, u32[]{:S(2)}, u32[]{:S(2)}) %collective-permute-start.6) | collective-permute-done | bytes 1572896 | tf_op jit(solution)/shard_map/ppermute | solution.py:416
  431.8 1.1 copy-done.3
  432.9 43.9 %backward_finish.1 = (bf16[8,256,768]{2,1,0:T(8,128)(2,1)}, bf16[8,16,768]{2,1,0:T(8,128)(2,1)}, bf16[768,1152]{1,0:T(8,128)(2,1)}, f32[8,1024]{1,0:T(8,128)}, f32[8,128]{1,0:T(8,128)}, /*index=5*/f32[8,768]{1,0:T(8,128)}) custom-call(bf16[8,128,768]{2,1,0:T(8,128)(2,1)} %copy-done.3, bf16[8,128,768]{2,1,0:T(8,128)(2,1)} %copy-done, ...), custom_call_target="tpu_custom_call" | custom-call | tf_op jit(solution)/shard_map/backward_finish/pallas_call | solution.py:390
  476.9 3.5 convert_element_type.84
  480.5 0.7 all-gather.17.cloned.1.call-update
  481.6 1.6 convert_element_type.85
  483.3 1.6 convert_element_type.83
  485.0 0.7 slice.82
  485.7 0.7 slice.79
  486.4 75.8 %all-reduce.5 = (f32[5,768]{1,0:T(8,128)}, f32[2,128]{1,0:T(2,128)S(1)}, f32[2,768]{1,0:T(2,128)S(1)}) all-reduce(f32[5,768]{1,0:T(8,128)S(1)} %slice.77, f32[2,128]{1,0:T(2,128)S(1)} %slice.79, f32[2,768]{1,0:T(2,128)S(1)} %slice.82), channel_id=1, replica_groups=mesh['shard'=4,'context'=4,'tensor'=2] {'shard','context'}, use_global_device_ids=true, to_apply=%region_5.6 | all-reduce | flops 5632 | bytes 45056 | tf_op jit(solution)/shard_map/psum | solution.py:548
  562.2 0.6 slice_reduce_fusion
  562.9 0.6 reduce_sum.9
  563.6 1.3 collective-permute-start.7
  564.8 0.8 slice_reduce_fusion.2
  565.6 41.1 %all-reduce.4 = (f32[768]{0:T(1024)}, f32[5,256]{1,0:T(8,128)S(1)}) all-reduce(f32[768]{0:T(1024)S(1)} %slice_reduce_fusion.2, f32[5,256]{1,0:T(8,128)S(1)} %slice.78), channel_id=1, replica_groups=mesh['shard'=4,'context'=4,'tensor'=2] {'shard','context','tensor'}, use_global_device_ids=true, to_apply=%region_1.2 | all-reduce | flops 2048 | bytes 16384 | tf_op jit(solution)/shard_map/psum | solution.py:547
  607.8 2.1 all-gather.2
  609.9 0.8 slice_bitcast_fusion.2
  610.7 6.1 slice_bitcast_fusion.1
  616.8 1.4 slice.99
  618.3 13.6 %all-gather.17.cloned.1.call-done = bf16[16,256,768]{2,1,0:T(8,128)(2,1)} async-done(((bf16[8,256,768]{2,1,0:T(8,128)(2,1)}), bf16[16,256,768]{2,1,0:T(8,128)(2,1)}) %all-gather.17.cloned.1.call-update) | async-done | bytes 6291472 | tf_op jit(solution)/shard_map/all_gather | solution.py:428
  631.9 6.0 slice_bitcast_fusion
  637.9 12.4 %finish.1 = (bf16[8,256,768]{2,1,0:T(8,128)(2,1)}, bf16[8,256,768]{2,1,0:T(8,128)(2,1)}) custom-call(bf16[8,256,768]{2,1,0:T(8,128)(2,1)} %bitcast.28, bf16[8,256,768]{2,1,0:T(8,128)(2,1)} %bitcast.31, f32[8,256,128]{2,1,0:T(8,128)} %all-reduce.8.cloned.1.call-done.stats, f32[1,768]{1,0:T(1,128)} %broadcast_in_dim.11.norm_in, ...), custom_call_target="tpu_custom_call" | custom-call | tf_op jit(solution)/shard_map/finish/pallas_call | solution.py:390
  650.3 0.7 copy.36
  651.0 0.7 slice.98
  651.7 115.1 %reduce-scatter.11.cloned.1.call-done = f32[48,768]{1,0:T(8,128)} async-done(((f32[768,768]{1,0:T(8,128)}), f32[48,768]{1,0:T(8,128)}) %reduce-scatter.11.cloned.1.call-update) | async-done | bytes 147472 | tf_op jit(solution)/shard_map/reduce_scatter | solution.py:411
  766.8 132.3 %reduce-scatter.5.cloned.1.call-done = f32[48,768]{1,0:T(8,128)} async-done(((f32[768,768]{1,0:T(8,128)}), f32[48,768]{1,0:T(8,128)}) %reduce-scatter.5.cloned.1.call-update) | async-done | bytes 147472 | tf_op jit(solution)/shard_map/reduce_scatter | solution.py:411
  899.1 9.3 %reduce-scatter.9.cloned.1.call-done = f32[48,128]{1,0:T(8,128)} async-done(((f32[48,256]{1,0:T(8,128)}), f32[48,128]{1,0:T(8,128)}) %reduce-scatter.9.cloned.1.call-update) | async-done | bytes 24592 | tf_op jit(solution)/shard_map/reduce_scatter | solution.py:546
  (65 shorter events, 4.8 us)
Async XLA Ops:
  7.2 66.3 %all-gather.9.cloned.1.call-start = ((), (), s32[]{:S(2)}) async-start(), calls=%async_computation.4 | async-start | bytes 1880064 | tf_op jit(solution)/shard_map/all_gather | solution.py:407
  11.8 178.1 %all-gather.11.cloned.1.call-start = ((), (), s32[]{:S(2)}) async-start(), calls=%async_computation.5 | async-start | bytes 1253376 | tf_op jit(solution)/shard_map/all_gather | solution.py:407
  12.8 11.6 %collective-permute-start = (bf16[8,16,768]{2,1,0:T(8,128)(2,1)S(1)}, bf16[8,16,768]{2,1,0:T(8,128)(2,1)S(1)}, u32[]{:S(2)}, u32[]{:S(2)}) collective-permute-start(bf16[8,16,768]{2,1,0:T(8,128)(2,1)S(1)} %slice.91), channel_id=1, source_target_pairs={{0,2},{2,4},{4,6},{1,3},{3,5},{5,7},{8,10},{10,12},{12,14},{9,11},... | collective-permute-start | bytes 589832 | tf_op jit(solution)/shard_map/ppermute | solution.py:416
  24.4 50.4 %copy-start.6 = (bf16[8,16,768]{2,1,0:T(8,128)(2,1)}, bf16[8,16,768]{2,1,0:T(8,128)(2,1)S(1)}, u32[]{:S(2)}) copy-start(bf16[8,16,768]{2,1,0:T(8,128)(2,1)S(1)} %collective-permute-done.halo) | copy-start | bytes 589828
  93.9 43.1 %copy-start.1 = (bf16[8,128,768]{2,1,0:T(8,128)(2,1)S(1)}, bf16[8,128,768]{2,1,0:T(8,128)(2,1)}, u32[]{:S(2)}) copy-start(bf16[8,128,768]{2,1,0:T(8,128)(2,1)} %get-tuple-element.47) | copy-start | bytes 4718596
  96.7 40.3 %collective-permute-start.1 = (bf16[8,128,768]{2,1,0:T(8,128)(2,1)S(1)}, bf16[8,128,768]{2,1,0:T(8,128)(2,1)}, u32[]{:S(2)}, u32[]{:S(2)}) collective-permute-start(bf16[8,128,768]{2,1,0:T(8,128)(2,1)S(1)} %fusion), channel_id=1, source_target_pairs={{0,2},{2,4},{4,6},{1,3},{3,5},{5,7},{8,10},{10,12},{12,14},{9,11},... | collective-permute-start | bytes 4718600 | tf_op jit(solution)/shard_map/ppermute | solution.py:416
  100.7 113.4 %all-gather.13.cloned.1.call-start = ((), (), s32[]{:S(2)}) async-start(), calls=%async_computation.6 | async-start | bytes 1253376 | tf_op jit(solution)/shard_map/all_gather | solution.py:407
  140.1 48.6 %copy-start.10 = (f32[12]{0:T(128)S(1)}, f32[12]{0:T(128)}, u32[]{:S(2)}) copy-start(f32[12]{0:T(128)} %param.31) | copy-start | bytes 148
  140.1 49.3 %copy-start.9 = (f32[768]{0:T(1024)S(1)}, f32[768]{0:T(1024)}, u32[]{:S(2)}) copy-start(f32[768]{0:T(1024)} %param.32) | copy-start | bytes 9220
  140.1 42.6 %collective-permute-start.2 = (bf16[8,128,768]{2,1,0:T(8,128)(2,1)}, bf16[8,128,768]{2,1,0:T(8,128)(2,1)S(1)}, u32[]{:S(2)}, u32[]{:S(2)}) collective-permute-start(bf16[8,128,768]{2,1,0:T(8,128)(2,1)} %fusion.1), channel_id=1, source_target_pairs={{0,2},{2,4},{4,6},{1,3},{3,5},{5,7},{8,10},{10,12},{12,14},{9,11},... | collective-permute-start | bytes 4718600 | tf_op jit(solution)/shard_map/ppermute | solution.py:416
  144.8 130.5 %all-reduce.8.cloned.1.call-start = ((), (), s32[]{:S(2)}) async-start(), calls=%async_computation.7 | async-start | bytes 2097152 | tf_op jit(solution)/shard_map/psum | solution.py:499
  184.3 44.6 %collective-permute-start.3 = (bf16[8,128,768]{2,1,0:T(8,128)(2,1)}, bf16[8,128,768]{2,1,0:T(8,128)(2,1)S(1)}, u32[]{:S(2)}, u32[]{:S(2)}) collective-permute-start(bf16[8,128,768]{2,1,0:T(8,128)(2,1)} %fusion.2), channel_id=1, source_target_pairs={{0,2},{2,4},{4,6},{1,3},{3,5},{5,7},{8,10},{10,12},{12,14},{9,11},... | collective-permute-start | bytes 4718600 | tf_op jit(solution)/shard_map/ppermute | solution.py:416
  228.8 1.2 copy-start
  253.5 357.2 %all-gather.15.cloned.1.call-start = ((), (), s32[]{:S(2)}) async-start(), calls=%async_computation.12 | async-start | bytes 9437184 | tf_op jit(solution)/shard_map/all_gather | solution.py:428
  254.1 362.7 %reduce-scatter.7.cloned.1.call-start = ((), (), s32[]{:S(2)}) async-start(), calls=%async_computation.9 | async-start | bytes 3760128 | tf_op jit(solution)/shard_map/reduce_scatter | solution.py:411
  316.0 40.3 %copy-start.2 = (bf16[8,128,768]{2,1,0:T(8,128)(2,1)S(1)}, bf16[8,128,768]{2,1,0:T(8,128)(2,1)}, u32[]{:S(2)}) copy-start(bf16[8,128,768]{2,1,0:T(8,128)(2,1)} %get-tuple-element.54) | copy-start | bytes 4718596
  317.8 38.5 %collective-permute-start.4 = (bf16[8,128,768]{2,1,0:T(8,128)(2,1)S(1)}, bf16[8,128,768]{2,1,0:T(8,128)(2,1)S(1)}, u32[]{:S(2)}, u32[]{:S(2)}) collective-permute-start(bf16[8,128,768]{2,1,0:T(8,128)(2,1)S(1)} %fusion.3), channel_id=1, source_target_pairs={{2,0},{4,2},{6,4},{3,1},{5,3},{7,5},{10,8},{12,10},{14,12},{11,9},... | collective-permute-start | bytes 4718600 | tf_op jit(solution)/shard_map/ppermute | solution.py:416
  356.8 37.7 %collective-permute-start.5 = (bf16[8,128,768]{2,1,0:T(8,128)(2,1)S(1)}, bf16[8,128,768]{2,1,0:T(8,128)(2,1)S(1)}, u32[]{:S(2)}, u32[]{:S(2)}) collective-permute-start(bf16[8,128,768]{2,1,0:T(8,128)(2,1)S(1)} %fusion.4), channel_id=1, source_target_pairs={{2,0},{4,2},{6,4},{3,1},{5,3},{7,5},{10,8},{12,10},{14,12},{11,9},... | collective-permute-start | bytes 4718600 | tf_op jit(solution)/shard_map/ppermute | solution.py:416
  395.0 36.8 %collective-permute-start.6 = (bf16[8,128,768]{2,1,0:T(8,128)(2,1)S(1)}, bf16[8,128,768]{2,1,0:T(8,128)(2,1)S(1)}, u32[]{:S(2)}, u32[]{:S(2)}) collective-permute-start(bf16[8,128,768]{2,1,0:T(8,128)(2,1)S(1)} %fusion.5), channel_id=1, source_target_pairs={{2,0},{4,2},{6,4},{3,1},{5,3},{7,5},{10,8},{12,10},{14,12},{11,9},... | collective-permute-start | bytes 4718600 | tf_op jit(solution)/shard_map/ppermute | solution.py:416
  431.8 1.1 copy-start.3
  480.4 1.3 copy-start.5
  480.4 151.5 %all-gather.17.cloned.1.call-start = ((), (), s32[]{:S(2)}) async-start(), calls=%async_computation.13 | async-start | bytes 9437184 | tf_op jit(solution)/shard_map/all_gather | solution.py:428
  481.2 2.2 copy-start.4
  481.2 285.6 %reduce-scatter.11.cloned.1.call-start = ((), (), s32[]{:S(2)}) async-start(), calls=%async_computation.11 | async-start | bytes 2506752 | tf_op jit(solution)/shard_map/reduce_scatter | solution.py:411
  483.2 2.5 copy-start.8
  483.2 80.3 %copy-start.11 = (bf16[8,16,768]{2,1,0:T(8,128)(2,1)S(1)}, bf16[8,16,768]{2,1,0:T(8,128)(2,1)}, u32[]{:S(2)}) copy-start(bf16[8,16,768]{2,1,0:T(8,128)(2,1)} %get-tuple-element.62) | copy-start | bytes 589828
  483.3 415.8 %reduce-scatter.5.cloned.1.call-start = ((), (), s32[]{:S(2)}) async-start(), calls=%async_computation.8 | async-start | bytes 2506752 | tf_op jit(solution)/shard_map/reduce_scatter | solution.py:411
  484.9 423.5 %reduce-scatter.9.cloned.1.call-start = ((), (), s32[]{:S(2)}) async-start(), calls=%async_computation.10 | async-start | bytes 73728 | tf_op jit(solution)/shard_map/reduce_scatter | solution.py:546
  563.6 44.3 %collective-permute-start.7 = (bf16[8,16,768]{2,1,0:T(8,128)(2,1)S(1)}, bf16[8,16,768]{2,1,0:T(8,128)(2,1)S(1)}, u32[]{:S(2)}, u32[]{:S(2)}) collective-permute-start(bf16[8,16,768]{2,1,0:T(8,128)(2,1)S(1)} %copy-done.11), channel_id=1, source_target_pairs={{2,0},{4,2},{6,4},{3,1},{5,3},{7,5},{10,8},{12,10},{14,12},{11,9},... | collective-permute-start | bytes 589832 | tf_op jit(solution)/shard_map/ppermute | solution.py:416
  637.9 12.4 %slice-start = ((f32[48,1152]{1,0:T(8,128)}), f32[48,12]{1,0:T(8,128)S(1)}, s32[]{:S(2)}) async-start(f32[48,1152]{1,0:T(8,128)} %reduce-scatter.7.cloned.1.call-done), calls=%async_computation.14 | async-start | bytes 49152 | tf_op jit(solution)/shard_map/slice | solution.py:556
  637.9 13.1 %copy-start.7 = (f32[48,1152]{1,0:T(8,128)S(1)}, f32[48,1152]{1,0:T(8,128)}, u32[]{:S(2)}) copy-start(f32[48,1152]{1,0:T(8,128)} %reduce-scatter.7.cloned.1.call-done) | copy-start | bytes 663556
Sparse Core Ops, SparseCore 0:
  11.9 61.5 all-gather.8
  100.9 54.0 all-gather.10
  157.7 56.3 all-gather.12
  253.7 21.5 all-reduce.7
  277.3 17.9 all-gather.14
  480.5 133.9 reduce-scatter.6
  616.1 15.6 all-gather.16
  638.1 128.6 reduce-scatter.10
  772.3 126.7 reduce-scatter.4
  901.7 6.5 reduce-scatter.8

commit v2 on v1

--- a/solution.py
+++ b/solution.py
@@ -163,7 +163,8 @@
         products = products + jnp.sum(grad_gn[0, :, cols] * weighted, 1, keepdims=True)
     part[0] = mm_nt(gated_low[...], w_out_t[...]).astype(BF16)
     lane = lax.broadcasted_iota(jnp.int32, (length, LANES), 1)
-    stats[0] = jnp.where(lane == 0, squares, jnp.where(lane == 1, products, 0.0))
+    columns = jnp.where(lane == 0, squares, jnp.where(lane == 1, products, 0.0))
+    stats[0] = columns.T[:8]
 
 
 def backward_local(inner_all, mixer, gate, grad_gn, stats, pre, dt_raw, cum, age, age_row, state_in, normed, out_grad,
@@ -195,8 +196,9 @@
     step_x[...] = pick(step, spread[...])
     open_start = age[0] > row_index(length)
     carried[...] = pick(jnp.where(open_start, jnp.exp(total), 0.0), spread[...])
-    scale = lax.rsqrt(stats[0][:, :1] / inner_all + EPSILON)
-    pull = scale * scale * scale * (stats[0][:, 1:2] / inner_all)
+    means = stats[0].T / inner_all
+    scale = lax.rsqrt(means[:, :1] + EPSILON)
+    pull = scale * scale * scale * means[:, 1:2]
     rows_sum = jnp.zeros((length, LANES), F32)
     for at, width in column_blocks(inner):
         cols = slice(at, at + width)
@@ -347,7 +349,9 @@
 
 
 def finish(inner_all, hid, out_grad, stats, norm_in, own_part, other_part, own_grad, other_grad, own_tail, other_tail,
-           out, in_grad, total):
+           sums_zo, sums_w, conv_sums, norm_sums, head_sums, inner_sums, gather,
+           out, in_grad, grad_wz, grad_wx, grad_wbc, grad_wdt, grad_wo, grad_conv_x, grad_conv_bc, grad_dt_bias,
+           grad_a_log, grad_skip, grad_norm_gate, grad_norm_in, total):
     length = hid.shape[1]
 
     def added(own, others, rows):
@@ -359,17 +363,33 @@
     everything = slice(None)
     total[...] = added(own_grad, other_grad, everything)
     total[length - HALO :] += added(own_tail, other_tail, everything)
+    scales = lax.rsqrt(stats[0].T[:, :1] / inner_all + EPSILON)
     for at in range(0, length, 64):
         rows = slice(at, at + 64)
         hidden = hid[0, rows].astype(F32)
-        scale_gate = lax.rsqrt(stats[0, rows, :1] / inner_all + EPSILON)
-        out[0, rows] = (hidden + scale_gate * added(own_part, other_part, rows)).astype(BF16)
+        out[0, rows] = (hidden + scales[rows] * added(own_part, other_part, rows)).astype(BF16)
         scale = normalised(hidden, 1.0)[1]
         weighted = total[rows] * norm_in[...]
         inner_mean = jnp.mean(weighted * hidden, -1, keepdims=True)
         in_grad[0, rows] = (
             out_grad[0, rows].astype(F32) + scale * weighted - hidden * (scale * scale * scale * inner_mean)
         ).astype(BF16)
+
+    @pl.when(is_last_step())
+    def _():
+        inner, own_bc, head_count = grad_wz.shape[1], grad_wbc.shape[1], grad_wdt.shape[1]
+        grad_wz[...] = sums_zo[:, :inner]
+        grad_wo[...] = sums_zo[:, inner:].T
+        grad_wbc[...] = sums_w[:, :own_bc]
+        grad_wdt[...] = sums_w[:, own_bc : own_bc + head_count]
+        grad_wx[...] = sums_w[:, own_bc + LANES :]
+        grad_conv_bc[...] = conv_sums[:5, :own_bc]
+        grad_conv_x[...] = conv_sums[:5, own_bc:]
+        grad_dt_bias[...] = head_sums[0:1, :head_count]
+        grad_a_log[...] = head_sums[1:2, :head_count]
+        grad_norm_in[...] = norm_sums[0:1]
+        grad_norm_gate[...] = inner_sums[0:1]
+        grad_skip[...] = pick(inner_sums[...], gather[...], 3)[1:2, :head_count]
 
 
 def by_piece(array):
@@ -403,6 +423,409 @@
     return jax.ShapeDtypeStruct(dims, kind)
 
 
+MESH = pl.DeviceIdType.MESH
+UP, DOWN, NEXT_X, NEXT_Y = range(4)
+
+
+def coordinates():
+    return lax.axis_index("shard"), lax.axis_index("context"), lax.axis_index("tensor")
+
+
+def greet(partners):
+    barrier = pltpu.get_barrier_semaphore()
+    count = 0
+    for there, device in partners:
+        if there is True:
+            pl.semaphore_signal(barrier, inc=1, device_id=device, device_id_type=MESH)
+            count = count + 1
+        else:
+            pl.when(there)(
+                functools.partial(pl.semaphore_signal, barrier, inc=1, device_id=device, device_id_type=MESH)
+            )
+            count = count + there.astype(jnp.int32)
+    pl.semaphore_wait(barrier, count)
+
+
+class Copies:
+    def __init__(self, send):
+        self.send, self.used, self.started = send, 0, []
+
+    def make(self, source, target, received, device, send=0):
+        return pltpu.make_async_remote_copy(
+            src_ref=source, dst_ref=target, send_sem=self.send.at[send], recv_sem=received,
+            device_id=device, device_id_type=MESH,
+        )
+
+    def start(self, source, target, received, device, there=True):
+        copy = self.make(source, target, received, device, self.used)
+        self.used += 1
+        self.started.append((there, copy))
+        if there is True:
+            copy.start()
+        else:
+            pl.when(there)(copy.start)
+
+    def arrived(self, target, received, there=True):
+        copy = self.make(target, target, received, {"tensor": 1 - lax.axis_index("tensor")})
+        if there is True:
+            copy.wait_recv()
+        else:
+            pl.when(there)(copy.wait_recv)
+
+    def finish(self):
+        for there, copy in self.started:
+            if there is True:
+                copy.wait_send()
+            else:
+                pl.when(there)(copy.wait_send)
+
+
+def neighbours(place):
+    shard, context, _ = place
+    count = lax.axis_size("context")
+    return [
+        (context + 1 < count, {"context": context + 1}),
+        (context > 0, {"context": context - 1}),
+        (True, {"shard": shard ^ 1}),
+        (True, {"shard": shard ^ 2}),
+    ]
+
+
+def gather_blocks(copies, place, stage, out, received, own):
+    shard, context, _ = place
+    count = lax.axis_size("context")
+    up, down, next_x, next_y = neighbours(place)
+    mine, beside_x, beside_y, across = [(shard ^ k) * count for k in (0, 1, 2, 3)]
+
+    def pass_on(source, slot, to, there=True):
+        if to[0] is not True:
+            there = to[0] if there is True else there & to[0]
+        copies.start(source, out.at[slot], received.at[slot], to[1], there)
+
+    local = pltpu.make_async_copy(stage, out.at[mine + context], own)
+    local.start()
+    for to in (up, down, next_x, next_y):
+        pass_on(stage, mine + context, to)
+    yield
+    for distance in range(1, count):
+        for at, there, to in ((context - distance, context >= distance, up),
+                              (context + distance, context + distance < count, down)):
+            slot = mine + jnp.clip(at, 0, count - 1)
+            copies.arrived(out.at[slot], received.at[slot], there)
+            for target in (to, next_x, next_y):
+                pass_on(out.at[slot], slot, target, there)
+        yield
+    for distance in range(count):
+        for at, there in ((context - distance, context >= distance),
+                          (context + distance, context + distance < count))[: 2 if distance else 1]:
+            at = jnp.clip(at, 0, count - 1)
+            low = at < count // 2
+            copies.arrived(out.at[beside_x + at], received.at[beside_x + at], there)
+            pass_on(out.at[beside_x + at], beside_x + at, next_y, there & low)
+            copies.arrived(out.at[beside_y + at], received.at[beside_y + at], there)
+            pass_on(out.at[beside_y + at], beside_y + at, next_x, there & (at >= count // 2))
+        yield
+    for at in range(count):
+        copies.arrived(out.at[across + at], received.at[across + at])
+    local.wait()
+
+
+GATHER_COPIES = 64
+
+
+def scatter_scratch(rows, width):
+    block = pltpu.VMEM((4, rows, width), BF16)
+    return [block, block, block, block, block, block, block, block, pltpu.VMEM((4, rows, width), F32),
+            pltpu.SemaphoreType.DMA((5, 4))]
+
+
+SCATTER_COPIES = 20
+
+
+def scatter_blocks(copies, place, blocks, out, first, from_x, from_y, from_up, from_down, to_first, to_up, to_down,
+                   column, received):
+    shard, context, _ = place
+    count = lax.axis_size("context")
+    up, down, next_x, next_y = neighbours(place)
+    mine, beside_x, beside_y, across = [(shard ^ k) * count for k in (0, 1, 2, 3)]
+    low, high = range(count // 2), range(count // 2, count)
+    for at in range(count // 2):
+        for k, to in ((at, next_y), (at + count // 2, next_x)):
+            copies.start(blocks.at[across + k], first.at[k], received.at[0, k], to[1])
+    for k in reversed(high):
+        copies.start(blocks.at[beside_x + k], from_x.at[k], received.at[1, k], next_x[1])
+    for k in low:
+        copies.start(blocks.at[beside_y + k], from_y.at[k], received.at[2, k], next_y[1])
+    yield
+    for at in range(count // 2):
+        for k, beside, buffers, row, to in ((at, beside_x, from_x, 1, next_x), (count - 1 - at, beside_y, from_y, 2, next_y)):
+            copies.arrived(first.at[k], received.at[0, k])
+            to_first[k] = (blocks[beside + k].astype(F32) + first[k].astype(F32)).astype(BF16)
+            copies.start(to_first.at[k], buffers.at[k], received.at[row, k], to[1])
+        yield
+    for at in range(count):
+        k = count - 1 - at // 2 if at % 2 == 0 else at // 2
+        copies.arrived(from_x.at[k], received.at[1, k])
+        copies.arrived(from_y.at[k], received.at[2, k])
+        column[k] = blocks[mine + k].astype(F32) + from_x[k].astype(F32) + from_y[k].astype(F32)
+        yield
+    for at in range(count - 1):
+        k = count - 1 - at
+
+        @pl.when(context < k)
+        def _(k=k):
+            @pl.when(context > 0)
+            def _():
+                copies.arrived(from_down.at[k], received.at[3, k])
+                to_up[k] = (column[k] + from_down[k].astype(F32)).astype(BF16)
+
+            @pl.when(context == 0)
+            def _():
+                to_up[k] = column[k].astype(BF16)
+
+        copies.start(to_up.at[k], from_down.at[k], received.at[3, k], up[1], context < k)
+        k = at
+
+        @pl.when(context > k)
+        def _(k=k):
+            @pl.when(context < count - 1)
+            def _():
+                copies.arrived(from_up.at[k], received.at[4, k])
+                to_down[k] = (column[k] + from_up[k].astype(F32)).astype(BF16)
+
+            @pl.when(context == count - 1)
+            def _():
+                to_down[k] = column[k].astype(BF16)
+
+        copies.start(to_down.at[k], from_up.at[k], received.at[4, k], down[1], context > k)
+        yield
+    out[...] = column[context]
+
+    @pl.when(context > 0)
+    def _():
+        copies.arrived(from_down.at[context], received.at[3, context])
+        out[...] += from_down[context].astype(F32)
+
+    @pl.when(context < count - 1)
+    def _():
+        copies.arrived(from_up.at[context], received.at[4, context])
+        out[...] += from_up[context].astype(F32)
+
+
+def gather_inputs(w_bc, w_dt, w_x, conv_bc, conv_x, hid, out, halo, taps, stage, send, received, others, own):
+    place = shard, context, tensor = coordinates()
+    length = hid.shape[1]
+    own_bc, head_count = w_bc.shape[1], w_dt.shape[1]
+    bc_width = 2 * LANES
+    partner = {"tensor": 1 - tensor}
+    around = neighbours(place)
+    stage[:, bc_width : bc_width + LANES] = jnp.zeros((stage.shape[0], LANES), BF16)
+    stage[:, bc_width : bc_width + head_count] = w_dt[...]
+    stage[:, bc_width + LANES :] = w_x[...]
+    cols = pl.ds(pl.multiple_of(tensor * own_bc, LANES), own_bc)
+    other_cols = pl.ds(pl.multiple_of((1 - tensor) * own_bc, LANES), own_bc)
+    stage[:, cols] = w_bc[...]
+    taps[...] = jnp.zeros_like(taps)
+    taps[:5, cols] = conv_bc[...]
+    taps[:5, bc_width:] = conv_x[...]
+    greet(around + [(True, partner)])
+    copies = Copies(send)
+    copies.start(stage.at[:, cols], stage.at[:, cols], others.at[0], partner)
+    copies.start(taps.at[:, cols], taps.at[:, cols], others.at[1], partner)
+    tail = pl.ds(length - HALO, HALO)
+    copies.start(hid.at[:, tail], halo, others.at[2], around[UP][1], around[UP][0])
+    copies.arrived(stage.at[:, other_cols], others.at[0])
+    for _ in gather_blocks(copies, place, stage, out, received, own):
+        pass
+    copies.arrived(taps.at[:, other_cols], others.at[1])
+    copies.arrived(halo, others.at[2], context > 0)
+
+    @pl.when(context == 0)
+    def _():
+        clear = pltpu.make_async_copy(hid.at[:, tail], halo, others.at[2])
+        clear.start()
+        clear.wait()
+
+    copies.finish()
+
+
+def chain_states(copies, place, local, decay, arrived, leaving, received, by):
+    _, context, _ = place
+    count = lax.axis_size("context")
+    first = context == (0 if by > 0 else count - 1)
+    last = context == (count - 1 if by > 0 else 0)
+    to = {"context": context + by}
+    pieces = local.shape[0]
+
+    def sent(i):
+        return pltpu.make_async_remote_copy(
+            src_ref=leaving.at[i], dst_ref=arrived.at[i], send_sem=received.at[1, i], recv_sem=received.at[0, i],
+            device_id=to, device_id_type=MESH,
+        )
+
+    for i in range(pieces):
+
+        @pl.when(first)
+        def _(i=i):
+            arrived[i] = jnp.zeros_like(arrived[i])
+            leaving[i] = local[i]
+
+        @pl.when(jnp.logical_not(first))
+        def _(i=i):
+            copies.arrived(arrived.at[i], received.at[0, i])
+
+        @pl.when(jnp.logical_not(first | last))
+        def _(i=i):
+            leaving[i] = (decay[i, :1] * arrived[i].astype(F32) + local[i].astype(F32)).astype(BF16)
+
+        pl.when(jnp.logical_not(last))(sent(i).start)
+        yield
+    for i in range(pieces):
+        pl.when(jnp.logical_not(last))(sent(i).wait_send)
+
+
+def in_turn(*steps):
+    steps = list(steps)
+    while steps:
+        for one in list(steps):
+            try:
+                next(one)
+            except StopIteration:
+                steps.remove(one)
+
+
+def states_up(local, decay, w_z, w_out, arrived, out, stage, leaving, send, received, own, states):
+    place = coordinates()
+    inner = w_z.shape[1]
+    stage[:, :inner] = w_z[...]
+    stage[:, inner:] = w_out[...].astype(F32).T.astype(BF16)
+    greet(neighbours(place))
+    copies = Copies(send)
+    in_turn(
+        gather_blocks(copies, place, stage, out, received, own),
+        chain_states(copies, place, local, decay, arrived, leaving, states, 1),
+    )
+    copies.finish()
+
+
+def add_over_cores(own, out, other, send, received):
+    _, _, tensor = coordinates()
+    partner = {"tensor": 1 - tensor}
+    greet([(True, partner)])
+    copies = Copies(send)
+    copies.start(own, other, received.at[0], partner)
+    copies.arrived(other, received.at[0])
+    out[...] = own[...] + other[...]
+    copies.finish()
+
+
+def states_down(local, decay, grad_wz, grad_wo, part, arrived, out, other_part, stage, leaving, send, others, states,
+                *buffers):
+    place = _, _, tensor = coordinates()
+    inner = grad_wz.shape[2]
+    stage[:, :, :inner] = grad_wz[...]
+    stage[:, :, inner:] = grad_wo[...]
+    partner = {"tensor": 1 - tensor}
+    greet(neighbours(place) + [(True, partner)])
+    copies = Copies(send)
+    copies.start(part, other_part.at[0], others.at[0], partner)
+    in_turn(
+        scatter_blocks(copies, place, stage, out, *buffers),
+        chain_states(copies, place, local, decay, arrived, leaving, states, -1),
+    )
+    copies.arrived(other_part.at[0], others.at[0])
+    copies.finish()
+
+
+def last_sums(grad_w, grad_normed, grad_halo, conv_sums, norm_sums, head_sums, inner_sums,
+              out, other_grad, own_tail, other_tail, conv_out, norm_out, head_out, inner_out,
+              stage, half, small, seen, tails, send, others, *buffers):
+    place = shard, context, tensor = coordinates()
+    count = lax.axis_size("context")
+    bc_width = 2 * LANES
+    own_bc = bc_width // 2
+    inner, model = inner_sums.shape[1], norm_sums.shape[1]
+    partner = {"tensor": 1 - tensor}
+    around = neighbours(place)
+    cols = pl.ds(pl.multiple_of(tensor * own_bc, LANES), own_bc)
+    other_cols = pl.ds(pl.multiple_of((1 - tensor) * own_bc, LANES), own_bc)
+    small[0, :5] = conv_sums[:5]
+    small[0, 5:6, :model] = norm_sums[:1]
+    small[0, 5:6, model : model + LANES] = head_sums[:1]
+    small[0, 5:6, model + LANES :] = head_sums[1:2]
+    small[0, 6:8, :inner] = inner_sums[:2]
+    small[0, 6:8, inner:] = jnp.zeros((2, small.shape[2] - inner), F32)
+    below, above = (around[DOWN][0], around[UP][0])
+    greet(around + [(True, partner), (True, {"context": context ^ 2}),
+                    (above, {"context": context + 1, "tensor": 1 - tensor}),
+                    (below, {"context": context - 1, "tensor": 1 - tensor})])
+    copies = Copies(send)
+    copies.start(small.at[0], seen.at[0], others.at[4], partner)
+    copies.start(grad_w.at[:, :, other_cols], half, others.at[0], partner)
+    copies.start(grad_normed, other_grad.at[0], others.at[1], partner)
+    copies.start(grad_halo, own_tail, others.at[2], around[DOWN][1], below)
+    copies.start(grad_halo, other_tail.at[0], others.at[3], {"context": context - 1, "tensor": 1 - tensor}, below)
+    stage[:, :, own_bc:] = grad_w[:, :, bc_width:]
+    copies.arrived(half, others.at[0])
+    mixed = grad_w[:, :, cols].astype(F32) + half[...].astype(F32)
+    stage[:, :, :own_bc] = mixed.astype(BF16)
+    row = lax.broadcasted_iota(jnp.int32, small.shape[1:], 0)
+    lane = lax.broadcasted_iota(jnp.int32, small.shape[1:], 1)
+    shared = ((row < 5) & (lane < bc_width)) | ((row == 5) & (lane < model))
+    copies.arrived(seen.at[0], others.at[4])
+    small[1] = small[0] + jnp.where(shared, seen[0], 0.0)
+    copies.start(small.at[1], seen.at[1], others.at[5], {"shard": shard ^ 1})
+    for _ in scatter_blocks(copies, place, stage, out, *buffers):
+        pass
+    for step, device in ((1, {"shard": shard ^ 1}), (2, {"shard": shard ^ 2}), (3, {"context": context ^ 1}),
+                         (4, {"context": context ^ 2})):
+        if step > 1:
+            copies.start(small.at[step], seen.at[step], others.at[4 + step], device)
+        copies.arrived(seen.at[step], others.at[4 + step])
+        small[step + 1] = small[step] + seen[step]
+    total = small.at[5]
+    conv_out[:, :own_bc] = total[:, cols]
+    conv_out[:, own_bc:] = total[:, bc_width:]
+    norm_out[...] = jnp.broadcast_to(total[5:6, :model], norm_out.shape)
+    head_out[...] = jnp.zeros_like(head_out)
+    head_out[0:1] = total[5:6, model : model + LANES]
+    head_out[1:2] = total[5:6, model + LANES : model + 2 * LANES]
+    inner_out[...] = jnp.zeros_like(inner_out)
+    inner_out[0:2] = total[6:8, :inner]
+    copies.arrived(other_grad.at[0], others.at[1])
+    copies.arrived(own_tail, others.at[2], above)
+    copies.arrived(other_tail.at[0], others.at[3], above)
+
+    @pl.when(jnp.logical_not(above))
+    def _():
+        tails[...] = jnp.zeros_like(tails)
+        for target, k in ((own_tail, 2), (other_tail.at[0], 3)):
+            clear = pltpu.make_async_copy(tails, target, others.at[k])
+            clear.start()
+            clear.wait()
+
+    copies.finish()
+
+
+ANY = pl.BlockSpec(memory_space=pl.ANY)
+IN_VMEM = pl.BlockSpec(memory_space=pltpu.VMEM)
+DMA = pltpu.SemaphoreType.DMA
+
+
+def call_between(kernel, collective_id, inputs, outputs, scratch):
+    return pl.pallas_call(
+        kernel,
+        in_specs=[spec for _, spec in inputs],
+        out_specs=[spec for _, spec in outputs],
+        out_shape=[shape for shape, _ in outputs],
+        scratch_shapes=scratch,
+        compiler_params=pltpu.CompilerParams(
+            collective_id=collective_id, has_side_effects=True, vmem_limit_bytes=VMEM_BYTES
+        ),
+        name=kernel.__name__,
+    )(*[array for array, _ in inputs])
+
+
 def gather_rows(rows):
     return lax.all_gather(rows, ("shard", "context"), axis=0, tiled=True)
 
@@ -427,6 +850,121 @@
 def exchange(value):
     everything = lax.all_gather(value, "tensor")
     return everything[0], everything[1:]
+
+
+def part_of(width, at):
+    return lambda array: pl.BlockSpec((array.shape[0], width), lambda i: (0, at))
+
+
+class AnyMesh:
+    def inputs(self, hid, w_bc, w_dt, w_x, conv_bc, conv_x):
+        conv_bc_all = lax.all_gather(conv_bc, "tensor", axis=1, tiled=True)
+        taps = jnp.pad(jnp.concatenate([conv_bc_all, conv_x], 1), ((0, 3), (0, 0)))
+        w_bc_all = lax.all_gather(w_bc, "tensor", axis=1, tiled=True)
+        w_dt_wide = jnp.pad(w_dt, ((0, 0), (0, LANES - w_dt.shape[1])))
+        w_in = gather_rows(jnp.concatenate([w_bc_all, w_dt_wide, w_x], 1))
+        return w_in, passed_along(hid[:, hid.shape[1] - HALO :], 1), taps
+
+    def states_up(self, local, decay, w_z, w_out):
+        return chain(local, decay, 1), (gather_rows(w_z), fixed), (gather_rows(w_out.T), fixed)
+
+    def over_cores(self, stats):
+        return lax.psum(stats, "tensor")
+
+    def states_down(self, local, decay, grad_wz, grad_wo, part):
+        sums = jnp.concatenate([scatter_rows(grad_wz), scatter_rows(grad_wo)], 1)
+        return chain(local, decay, -1), sums, exchange(part)
+
+    def last_sums(self, grad_w, grad_normed, grad_halo, conv_sums, norm_sums, head_sums, inner_sums, own_bc):
+        mine, bc_width = lax.axis_index("tensor"), 2 * LANES
+        grad_w = scatter_rows(grad_w)
+        grad_w_bc = lax.psum_scatter(grad_w[:, :bc_width], "tensor", scatter_dimension=1, tiled=True)
+        norm_sums, conv_bc = lax.psum((norm_sums, conv_sums[:, :bc_width]), ("shard", "context", "tensor"))
+        conv_x, head_sums, inner_sums = lax.psum(
+            (conv_sums[:, bc_width:], head_sums, inner_sums), ("shard", "context")
+        )
+        conv_bc = lax.dynamic_slice_in_dim(conv_bc, mine * own_bc, own_bc, 1)
+        return (
+            jnp.concatenate([grad_w_bc, grad_w[:, bc_width:]], 1),
+            exchange(grad_normed),
+            exchange(passed_along(grad_halo, -1)),
+            (jnp.concatenate([conv_bc, conv_x], 1), norm_sums, head_sums, inner_sums),
+        )
+
+
+class FourByFourByTwo:
+    def inputs(self, hid, w_bc, w_dt, w_x, conv_bc, conv_x):
+        rows, inner = w_x.shape
+        pieces, _, model = hid.shape
+        blocks = model // rows
+        in_width = 3 * LANES + inner
+        w_in, halo, taps = call_between(
+            gather_inputs, 1,
+            [(w_bc, IN_VMEM), (w_dt, IN_VMEM), (w_x, IN_VMEM), (conv_bc, IN_VMEM), (conv_x, IN_VMEM), (hid, ANY)],
+            [(shaped(BF16, blocks, rows, in_width), ANY), (shaped(BF16, pieces, HALO, model), ANY),
+             (shaped(F32, 8, 2 * LANES + inner), IN_VMEM)],
+            [pltpu.VMEM((rows, in_width), BF16), DMA((GATHER_COPIES,)), DMA((blocks,)), DMA((3,)), DMA],
+        )
+        return w_in.reshape(model, in_width), halo, taps
+
+    def states_up(self, local, decay, w_z, w_out):
+        rows, inner = w_z.shape
+        model = w_out.shape[1] * 16
+        pieces = local.shape[0]
+        arrived, both = call_between(
+            states_up, 2,
+            [(local, IN_VMEM), (decay, IN_VMEM), (w_z, IN_VMEM), (w_out, IN_VMEM)],
+            [(shaped(BF16, *local.shape), IN_VMEM), (shaped(BF16, 16, rows, 2 * inner), ANY)],
+            [pltpu.VMEM((rows, 2 * inner), BF16), pltpu.VMEM(local.shape, BF16), DMA((GATHER_COPIES,)), DMA((16,)), DMA,
+             DMA((2, pieces))],
+        )
+        both = both.reshape(model, 2 * inner)
+        return arrived, (both, part_of(inner, 0)), (both, part_of(inner, 1))
+
+    def over_cores(self, stats):
+        return call_between(
+            add_over_cores, 3, [(stats, IN_VMEM)], [(shaped(F32, *stats.shape), IN_VMEM)],
+            [pltpu.VMEM(stats.shape, F32), DMA((1,)), DMA((1,))],
+        )[0]
+
+    def states_down(self, local, decay, grad_wz, grad_wo, part):
+        model, inner = grad_wz.shape
+        rows = model // 16
+        pieces = local.shape[0]
+        arrived, sums, other = call_between(
+            states_down, 4,
+            [(local, IN_VMEM), (decay, IN_VMEM), (grad_wz.reshape(16, rows, inner), IN_VMEM),
+             (grad_wo.reshape(16, rows, inner), IN_VMEM), (part, ANY)],
+            [(shaped(BF16, *local.shape), IN_VMEM), (shaped(F32, rows, 2 * inner), IN_VMEM),
+             (shaped(BF16, 1, *part.shape), ANY)],
+            [pltpu.VMEM((16, rows, 2 * inner), BF16), pltpu.VMEM(local.shape, BF16), DMA((SCATTER_COPIES,)), DMA((1,)),
+             DMA((2, pieces))] + scatter_scratch(rows, 2 * inner),
+        )
+        return arrived, sums, (part, other)
+
+    def last_sums(self, grad_w, grad_normed, grad_halo, conv_sums, norm_sums, head_sums, inner_sums, own_bc):
+        model, in_width = grad_w.shape
+        rows = model // 16
+        width = in_width - own_bc
+        channels = conv_sums.shape[1]
+        out, other_grad, own_tail, other_tail, *small = call_between(
+            last_sums, 5,
+            [(grad_w.reshape(16, rows, in_width), IN_VMEM), (grad_normed, ANY), (grad_halo, ANY),
+             (conv_sums, IN_VMEM), (norm_sums, IN_VMEM), (head_sums, IN_VMEM), (inner_sums, IN_VMEM)],
+            [(shaped(F32, rows, width), IN_VMEM), (shaped(BF16, 1, *grad_normed.shape), ANY),
+             (shaped(BF16, *grad_halo.shape), ANY), (shaped(BF16, 1, *grad_halo.shape), ANY),
+             (shaped(F32, 8, channels - own_bc), IN_VMEM), (shaped(F32, 8, model), IN_VMEM),
+             (shaped(F32, 8, LANES), IN_VMEM), (shaped(F32, *inner_sums.shape), IN_VMEM)],
+            [pltpu.VMEM((16, rows, width), BF16), pltpu.VMEM((16, rows, own_bc), BF16),
+             pltpu.VMEM((6, 8, channels), F32), pltpu.VMEM((5, 8, channels), F32), pltpu.VMEM(grad_halo.shape, BF16),
+             DMA((SCATTER_COPIES + 9,)), DMA((9,))] + scatter_scratch(rows, width),
+        )
+        return out, (grad_normed, other_grad), (own_tail, other_tail), small
+
+
+def links():
+    sizes = tuple(lax.axis_size(axis) for axis in ("shard", "context", "tensor"))
+    return FourByFourByTwo() if sizes == (4, 4, 2) else AnyMesh()
 
 
 def shards(inner_all, hidden_in, out_grad, doc_start, norm_in, w_z, w_x, w_bc, w_dt, conv_x, conv_bc, dt_bias, a_log,
@@ -453,17 +991,10 @@
     heads = jnp.stack([head_row(dt_bias), head_row(a_log)] + [jnp.zeros((LANES,), F32)] * 6)
     skip = jnp.repeat(skip_d, HEAD)[None]
     norm_in, norm_gate = norm_in[None], norm_gate[None]
-    conv_bc_all = lax.all_gather(conv_bc, "tensor", axis=1, tiled=True)
-    taps = jnp.pad(jnp.concatenate([conv_bc_all, conv_x], 1), ((0, 3), (0, 0)))
-    w_bc_all = lax.all_gather(w_bc, "tensor", axis=1, tiled=True)
-    w_dt_wide = jnp.pad(w_dt, ((0, 0), (0, LANES - head_count)))
-    w_in = gather_rows(jnp.concatenate([w_bc_all, w_dt_wide, w_x], 1))
-    w_z_all = gather_rows(w_z)
-    w_out_t = gather_rows(w_out.T)
-
     hid = hidden_in.reshape(pieces, length, model)
     seed = out_grad.reshape(pieces, length, model)
-    halo = passed_along(hid[:, length - HALO :], 1)
+    between = links()
+    w_in, halo, taps = between.inputs(hid, w_bc, w_dt, w_x, conv_bc, conv_x)
     ages = (offset + jnp.arange(length, dtype=jnp.int32) - doc_start.reshape(pieces, length)).astype(F32)
     age = jnp.broadcast_to(ages[:, :, None], (pieces, length, LANES))
     age_row = jnp.broadcast_to(ages[:, None, :], (pieces, 8, length))
@@ -481,7 +1012,7 @@
         [((length, channels), F32)], "forward_local",
     )
 
-    state_in = chain(local, decay, 1)
+    state_in, w_z_all, w_out_t = between.states_up(local, decay, w_z, w_out)
 
     square = ((length, length), F32)
     token_wide = ((length, inner), F32)
@@ -489,14 +1020,14 @@
     mixer, gate, grad_gn, part, stats = call(
         forward_mix, pieces,
         [(pre, by_piece), (dt_raw, by_piece), (cum, by_piece), (age, by_piece), (state_in, by_piece), (normed, by_piece),
-         (seed, by_piece), (w_z_all, fixed), (w_out_t, fixed), (norm_gate, fixed), (skip, fixed), (heads, fixed),
+         (seed, by_piece), w_z_all, w_out_t, (norm_gate, fixed), (skip, fixed), (heads, fixed),
          (spread, fixed)],
         [(token(inner), by_piece), (token(inner), by_piece), (token(inner), by_piece), (token_low(model), by_piece),
-         (token(LANES), by_piece)],
+         (shaped(F32, pieces, 8, length), by_piece)],
         [((length, LANES), F32), square, square, token_wide, token_wide, token_narrow], "forward_mix",
     )
 
-    stats = lax.psum(stats, "tensor")
+    stats = between.over_cores(stats)
 
     grad_fed, grad_mix, grad_gate, grad_cum, grad_bc, grad_state, grad_wz, grad_wo, sums = call(
         functools.partial(backward_local, inner_all), pieces,
@@ -511,14 +1042,14 @@
          token_wide, token_narrow, token_narrow], "backward_local",
     )
 
-    grad_later = chain(grad_state, decay, -1)
+    grad_later, sums_zo, (own_part, other_part) = between.states_down(grad_state, decay, grad_wz, grad_wo, part)
 
     grad_normed, grad_halo, grad_w, conv_sums, head_sums, norm_sums = call(
         backward_finish, pieces,
         [(grad_later, by_piece), (state_in, by_piece), (pre, by_piece), (raw, by_piece), (dt_raw, by_piece),
          (cum, by_piece), (age, by_piece), (grad_fed, by_piece), (grad_mix, by_piece), (grad_cum, by_piece),
          (grad_bc, by_piece), (grad_gate, by_piece), (normed, by_piece), (hid, by_piece), (halo, by_piece),
-         (w_in, fixed), (w_z_all, fixed), (taps, fixed), (skip, fixed), (norm_in, fixed), (heads, fixed),
+         (w_in, fixed), w_z_all, (taps, fixed), (skip, fixed), (norm_in, fixed), (heads, fixed),
          (spread, fixed), (gather, fixed), (tri_up, fixed)],
         [(token_low(model), by_piece), (shaped(BF16, pieces, HALO, model), by_piece),
          (shaped(BF16, model, in_width), fixed), (shaped(F32, 8, channels), fixed), (shaped(F32, 8, LANES), fixed),
@@ -528,39 +1059,40 @@
         "backward_finish",
     )
 
-    own_part, other_part = exchange(part)
-    own_grad, other_grad = exchange(grad_normed)
-    own_tail, other_tail = exchange(passed_along(grad_halo, -1))
-    out, in_grad = call(
+    own_bc = w_bc.shape[1]
+    sums_w, (own_grad, other_grad), (own_tail, other_tail), small = between.last_sums(
+        grad_w, grad_normed, grad_halo, conv_sums, norm_sums, head_sums, sums, own_bc
+    )
+    rows = w_z.shape[0]
+    outputs = [shaped(F32, rows, inner), shaped(F32, rows, inner), shaped(F32, rows, own_bc),
+               shaped(F32, rows, head_count), shaped(F32, inner, rows), shaped(F32, 5, inner), shaped(F32, 5, own_bc),
+               shaped(F32, 1, head_count), shaped(F32, 1, head_count), shaped(F32, 1, head_count),
+               shaped(F32, 1, inner), shaped(F32, 1, model)]
+    (out, in_grad, grad_wz, grad_wx, grad_wbc, grad_wdt, grad_wo, grad_conv_x, grad_conv_bc, grad_dt_bias, grad_a_log,
+     grad_skip, grad_norm_gate, grad_norm_in) = call(
         functools.partial(finish, inner_all), pieces,
         [(hid, by_piece), (seed, by_piece), (stats, by_piece), (norm_in, fixed), (own_part, by_piece),
          (other_part, by_piece_second), (own_grad, by_piece), (other_grad, by_piece_second), (own_tail, by_piece),
-         (other_tail, by_piece_second)],
-        [(token_low(model), by_piece), (token_low(model), by_piece)],
+         (other_tail, by_piece_second), (sums_zo, fixed), (sums_w, fixed)] + [(array, fixed) for array in small]
+        + [(gather, fixed)],
+        [(token_low(model), by_piece), (token_low(model), by_piece)] + [(shape, fixed) for shape in outputs],
         [((length, model), F32)], "finish",
     )
-
-    mine = lax.axis_index("tensor")
-    own_bc = w_bc.shape[1]
-    grad_w = scatter_rows(grad_w)
-    grad_w_bc = lax.psum_scatter(grad_w[:, :bc_width], "tensor", scatter_dimension=1, tiled=True)
-    norm_sums, conv_bc_sums = lax.psum((norm_sums[0], conv_sums[:5, :bc_width]), ("shard", "context", "tensor"))
-    conv_x_sums, head_sums, sums = lax.psum((conv_sums[:5, bc_width:], head_sums[:2], sums[:2]), ("shard", "context"))
     return (
         out.reshape(hidden_in.shape),
         in_grad.reshape(hidden_in.shape),
-        norm_sums,
-        scatter_rows(grad_wz),
-        grad_w[:, bc_width + LANES :],
-        grad_w_bc,
-        grad_w[:, bc_width : bc_width + head_count],
-        conv_x_sums,
-        lax.dynamic_slice_in_dim(conv_bc_sums, mine * own_bc, own_bc, 1),
-        head_sums[0, :head_count],
-        head_sums[1, :head_count],
-        jnp.sum(sums[1].reshape(head_count, HEAD), 1),
-        sums[0],
-        scatter_rows(grad_wo).T,
+        grad_norm_in[0],
+        grad_wz,
+        grad_wx,
+        grad_wbc,
+        grad_wdt,
+        grad_conv_x,
+        grad_conv_bc,
+        grad_dt_bias[0],
+        grad_a_log[0],
+        grad_skip[0],
+        grad_norm_gate[0],
+        grad_wo,
     )
 
 

time: 916 us -> 385 us (0.42)
  waiting for transfers between devices: 563 us -> 0 us
  Pallas kernels: 139 us -> 364 us
  blocking collectives: 123 us -> 0 us
  starting transfers between devices: 23.9 us -> 0 us
  local copies, waits for them, and re-layouts: 31.4 us -> 13.7 us
  other arithmetic: 20 us -> 3.25 us
  between operations: 14.4 us -> 0.74 us
    reduce_scatter x4 -> x0, waiting for transfers between devices: 257 us -> none  [the longest x3 247 us: scatter_rows(): lax.psum_scatter(rows.astype(F32), ('shard', 'context'), scatter_dimensio...]
    pallas_call x0 -> x5, Pallas kernels: none -> 224 us  [call_between(): pl.pallas_call(kernel, in_specs=[spec for _, spec in inputs], out_specs=[...]
    ppermute x8 -> x0, waiting for transfers between devices: 198 us -> none  [passed_along(): lax.ppermute(value, 'context', [(i, i + by) for i in range(length) if 0 <...]
    psum x2 -> x0, blocking collectives: 117 us -> none  [the longest x1 75.8 us: shards(): lax.psum((conv_sums[:5, bc_width:], head_sums[:2], sums[:2]), ('shard', '...]
    all_gather x5 -> x0, waiting for transfers between devices: 86.9 us -> none  [the longest x3 73.3 us: gather_rows(): return lax.all_gather(rows, ('shard', 'context'), axis=0, tiled=True)]
    ppermute x8 -> x0, starting transfers between devices: 23.3 us -> none  [passed_along(): lax.ppermute(value, 'context', [(i, i + by) for i in range(length) if 0 <...]
    psum x1 -> x0, waiting for transfers between devices: 20.9 us -> none  [shards(): stats = lax.psum(stats, 'tensor')]
    slice x15 -> x0, local copies, waits for them, and re-layouts: 19.8 us -> none  [the longest x3 12.9 us: exchange(): return (everything[0], everything[1:])]
  transfers between devices with their start and end apart: 18 -> 0, of which waited for: 13 -> 0; matrix products, arithmetic and copies ran while one was open for 5% -> 0% of each run, Pallas kernels for 11% -> 0%
where the time goes in v2:
time: 385 us; the launch traced here: 382 us
  Pallas kernels  364 us (95%)
  local copies, waits for them, and re-layouts  13.7 us (4%)
    pallas_call x5, Pallas kernels, call_between(): pl.pallas_call(kernel, in_specs=[spec for _, spec in inputs], out_specs=[...  224 us
    pallas_call x5, Pallas kernels, call(): pl.pallas_call(kernel, grid=(pieces,), in_specs=[cut(array) for array, cu...  141 us

profile of v2, /device:TPU:0, one launch (start us, length us, event | category | flops | bytes accessed | tf_op | source)
XLA Modules:
  0.0 382.2 jit_solution(3325938720082608713)
XLA Ops:
  0.7 0.1 pad.12.clone
  0.7 0.1 pad.11.clone
  0.8 0.7 pad_bitcast_fusion
  1.5 0.7 maximum_maximum_fusion.heads
  2.2 1.3 broadcast_in_dim.11.norm_in
  3.4 1.3 broadcast_in_dim.24.norm_gate
  4.7 0.7 reshape.99
  5.4 0.7 broadcast_in_dim.25
  6.1 0.7 broadcast_in_dim_reshape.3.skip
  6.8 1.4 copy.33.w_dt
  8.2 0.6 broadcast_in_dim.26.age_row
  8.8 1.7 copy.34.w_out
  10.5 1.3 broadcast_in_dim.10.age
  11.8 39.0 %gather_inputs.1 = (bf16[16,48,1152]{2,1,0:T(8,128)(2,1)}, bf16[8,16,768]{2,1,0:T(8,128)(2,1)}, f32[8,1024]{1,0:T(8,128)}) custom-call(bf16[48,128]{1,0:T(8,128)(2,1)} %w_bc.1, bf16[48,12]{1,0:T(8,128)(2,1)} %copy.33.w_dt, bf16[48,768]{1,0:T(8,128)(2,1)} %w_x.1, f32[5,128]{1,0:T(8,128)} %conv_bc.1, f32[5,768]{1,0:T(8,128)} %conv_x.1, ...), custom_call_target="tpu_custom_call" | custom-call | tf_op jit(solution)/shard_map/gather_inputs/pallas_call | solution.py:816
  50.8 19.1 %forward_local.1 = (bf16[8,272,768]{2,1,0:T(8,128)(2,1)}, f32[8,272,1024]{2,1,0:T(8,128)}, f32[8,256,1024]{2,1,0:T(8,128)}, f32[8,256,128]{2,1,0:T(8,128)}, f32[...) custom-call(bf16[8,256,768]{2,1,0:T(8,128)(2,1)} %bitcast.17, ...), custom_call_target="tpu_custom_call" | custom-call | tf_op jit(solution)/shard_map/forward_local/pallas_call | solution.py:410
  69.9 41.2 %states_up.1 = (bf16[8,128,768]{2,1,0:T(8,128)(2,1)}, bf16[16,48,1536]{2,1,0:T(8,128)(2,1)}) custom-call(bf16[8,128,768]{2,1,0:T(8,128)(2,1)} %get-tuple-element.77.local, f32[8,8,768]{2,1,0:T(8,128)} %get-tuple-element.78.decay, bf16[48,768]{1,0:T(8,128)(2,1)} %w_z.1, bf16[768,48]{1,0:T(8,128)(2,1)} %copy.34.w_out), custom_call_target="tpu_custom_call" | custom-call | tf_op jit(solution)/shard_map/states_up/pallas_call | solution.py:816
  111.0 23.5 %forward_mix.1 = (f32[8,256,768]{2,1,0:T(8,128)}, f32[8,256,768]{2,1,0:T(8,128)}, f32[8,256,768]{2,1,0:T(8,128)}, bf16[8,256,768]{2,1,0:T(8,128)(2,1)}, f32[8,8,256]{2,1,0:T(8,128)}) custom-call(f32[8,256,1024]{2,1,0:T(8,128)} %get-tuple-element.74.pre, f32[8,256,128]{2,1,0:T(8,128)} %get-tuple-element.75.dt_raw, f32[8,256,128]{2,1,0:T(8,128)} %get-tuple-element.76.cum, ...), custom_call_target="tpu_custom_call" | custom-call | tf_op jit(solution)/shard_map/forward_mix/pallas_call | solution.py:410
  134.5 2.8 add_over_cores.1.stats
  137.3 40.4 %backward_local.1 = (f32[8,256,768]{2,1,0:T(8,128)}, bf16[8,256,768]{2,1,0:T(8,128)(2,1)}, bf16[8,256,768]{2,1,0:T(8,128)(2,1)}, f32[8,256,128]{2,1,0:T(8,128)},...) custom-call(f32[8,256,768]{2,1,0:T(8,128)} %get-tuple-element.84.mix, ...), custom_call_target="tpu_custom_call" | custom-call | tf_op jit(solution)/shard_map/backward_local/pallas_call | solution.py:410
  177.7 93.6 %states_down.1 = (bf16[8,128,768]{2,1,0:T(8,128)(2,1)}, f32[48,1536]{1,0:T(8,128)}, bf16[1,8,256,768]{3,2,1,0:T(8,128)(2,1)}) custom-call(bf16[8,128,768]{2,1,0:T(8,128)(2,1)} %get-tuple-element.87.local, f32[8,8,768]{2,1,0:T(8,128)} %get-tuple-element.78.decay, bf16[16,48,768]{2,1,0:T(8,128)(2,1)} %bitcast.29, bf16[16,48,768]{2,1,0:T(8,128)(2,1)} %bitcast.30, ...), custom_call_target="tpu_custom_call" | custom-call | tf_op jit(solution)/shard_map/states_down/pallas_call | solution.py:816
  271.3 44.0 %backward_finish.1 = (bf16[8,256,768]{2,1,0:T(8,128)(2,1)}, bf16[8,16,768]{2,1,0:T(8,128)(2,1)}, bf16[768,1152]{1,0:T(8,128)(2,1)}, f32[8,1024]{1,0:T(8,128)}, f32[8,128]{1,0:T(8,128)}, /*index=5*/f32[8,768]{1,0:T(8,128)}) custom-call(bf16[8,128,768]{2,1,0:T(8,128)(2,1)} %get-tuple-element.91.grad_later, bf16[8,128,768]{2,1,0:T(8,128)(2,1)} %get-tuple-element.79.state_in, ...), custom_call_target="tpu_custom_call" | custom-call | tf_op jit(solution)/shard_map/backward_finish/pallas_call | solution.py:410
  315.3 47.4 %last_sums.1 = (f32[48,1024]{1,0:T(8,128)}, bf16[1,8,256,768]{3,2,1,0:T(8,128)(2,1)}, bf16[8,16,768]{2,1,0:T(8,128)(2,1)}, bf16[1,8,16,768]{3,2,1,0:T(8,128)(2,1...) custom-call(bf16[16,48,1152]{2,1,0:T(8,128)(2,1)} %bitcast.28, ...), custom_call_target="tpu_custom_call" | custom-call | tf_op jit(solution)/shard_map/last_sums/pallas_call | solution.py:816
  362.8 13.6 %finish.1 = (bf16[8,256,768]{2,1,0:T(8,128)(2,1)}, bf16[8,256,768]{2,1,0:T(8,128)(2,1)}, f32[48,768]{1,0:T(8,128)}, f32[48,768]{1,0:T(8,128)}, f32[48,128]{1,0:T...) custom-call(bf16[8,256,768]{2,1,0:T(8,128)(2,1)} %bitcast.19, ...), custom_call_target="tpu_custom_call" | custom-call | tf_op jit(solution)/shard_map/finish/pallas_call | solution.py:410
  376.4 1.3 reduce
  377.7 1.3 reduce.1
  378.9 1.4 copy.35
  380.4 1.8 copy.36
  (4 shorter events, 0.0 us)

commit v3 on v2

--- a/solution.py
+++ b/solution.py
@@ -79,92 +79,113 @@
     return hidden * scale * gain, scale
 
 
-def forward_local(hid, halo, age, norm_in, w_in, taps, heads, spread, tri,
-                  normed, raw, pre, dt_raw, cum, local, decay, act):
-    length = hid.shape[1]
-    channels = taps.shape[1]
+def project(hid, halo, age, norm_in, w_in, taps, heads, spread, tri,
+            normed, raw, pre, dt_raw, cum, local, decay, act):
+    length, channels = hid.shape[0], taps.shape[1]
     bc_width = 2 * LANES
-    normed[0, :HALO] = normalised(halo[0].astype(F32), norm_in[...])[0].astype(BF16)
+    normed[:HALO] = normalised(halo[...].astype(F32), norm_in[...])[0].astype(BF16)
     for at in range(0, length, 64):
-        rows = normalised(hid[0, at : at + 64].astype(F32), norm_in[...])[0]
-        normed[0, HALO + at : HALO + at + 64] = rows.astype(BF16)
-    raw[0, :, :bc_width] = mm(normed[0], w_in[:, :bc_width])
-    raw[0, :, bc_width:] = mm(normed[0], w_in[:, bc_width + LANES :])
-    dt_raw[0] = mm(normed[0, HALO:], w_in[:, bc_width : bc_width + LANES])
+        rows = normalised(hid[at : at + 64].astype(F32), norm_in[...])[0]
+        normed[HALO + at : HALO + at + 64] = rows.astype(BF16)
+    raw[:, :bc_width] = mm(normed[...], w_in[:, :bc_width])
+    raw[:, bc_width:] = mm(normed[...], w_in[:, bc_width + LANES :])
+    dt_raw[...] = mm(normed[HALO:], w_in[:, bc_width : bc_width + LANES])
     for at, width in column_blocks(channels):
         cols = slice(at, at + width)
         running = jnp.broadcast_to(taps[4:5, cols], (length, width))
         for lag in range(4):
-            tapped = raw[0, HALO - lag : HALO - lag + length, cols]
+            tapped = raw[HALO - lag : HALO - lag + length, cols]
             if lag:
-                tapped = jnp.where(age[0, :, :width] >= lag, tapped, 0.0)
+                tapped = jnp.where(age[:, :width] >= lag, tapped, 0.0)
             running = running + taps[lag : lag + 1, cols] * tapped
-        pre[0, :, cols] = running
+        pre[:, cols] = running
         act[:, cols] = running * sigmoid(running)
-    step = softplus(dt_raw[0] + heads[0:1])
+    step = softplus(dt_raw[...] + heads[0:1])
     total = pick_left(tri[...], -jnp.exp(heads[1:2]) * step)
-    cum[0] = total
-    last, age_last = total[length - 1 :], age[0, length - 1 :]
+    cum[...] = total
+    last, age_last = total[length - 1 :], age[length - 1 :]
     open_end = row_index(length) - (length - 1) + age_last >= 0
     weight = jnp.where(open_end, jnp.exp(last - total), 0.0) * step
     weighted = (act[:, bc_width:] * pick(weight, spread[...])).astype(BF16)
-    local[0] = mm_tn(act[:, :LANES].astype(BF16), weighted).astype(BF16)
+    local[...] = mm_tn(act[:, :LANES].astype(BF16), weighted).astype(BF16)
     kept = jnp.where(age_last > length - 1, jnp.exp(last), 0.0)
-    decay[0] = pick(jnp.broadcast_to(kept, (8, LANES)), spread[...], 3)
-
-
-def forward_mix(pre, dt_raw, cum, age, state_in, normed, out_grad, w_z, w_out_t, norm_gate, skip, heads, spread,
-                mixer, gate, grad_gn, part, stats, near, seg, pair, carried, step_x, gated_low):
-    length, inner = mixer.shape[1:]
+    decay[...] = pick(jnp.broadcast_to(kept, (8, LANES)), spread[...], 3)
+
+
+def activated(pre):
+    value = pre[...]
+    return (value * sigmoid(value)).astype(BF16)
+
+
+def mix_within(pre, dt_raw, cum, age, normed, out_grad, w_z, w_out_t, skip, heads, spread,
+               near, gate, grad_gn, seg, pair, step_x):
+    length, inner = near.shape
     bc_width = 2 * LANES
-    readout = pre[0, :, LANES:bc_width]
-    readout = (readout * sigmoid(readout)).astype(BF16)
-    inputs_b = pre[0, :, :LANES]
-    inputs_b = (inputs_b * sigmoid(inputs_b)).astype(BF16)
-    gate[0] = mm(normed[0, HALO:], w_z[...])
-    grad_gn[0] = mm(out_grad[0], w_out_t[...])
-    pair[...] = mm_nt(readout, inputs_b)
+    gate[...] = mm(normed[HALO:], w_z())
+    grad_gn[...] = mm(out_grad[...], w_out_t())
+    pair[...] = mm_nt(activated(pre.at[:, LANES:bc_width]), activated(pre.at[:, :LANES]))
     row = lax.broadcasted_iota(jnp.int32, (length, length), 0)
     col = lax.broadcasted_iota(jnp.int32, (length, length), 1)
     back = (row - col).astype(F32)
-    seg[...] = jnp.where((back >= 0) & (back <= age[0][:, :1]), 0.0, GONE)
-    total = cum[0]
+    seg[...] = jnp.where((back >= 0) & (back <= age[:, :1]), 0.0, GONE)
+    total = cum[...]
     total_t = total.T
-    step = softplus(dt_raw[0] + heads[0:1])
-    step_x[...] = pick(step, spread[...])
-    open_start = age[0] > row_index(length)
-    carried[...] = pick(jnp.where(open_start, jnp.exp(total), 0.0), spread[...])
-    carried[...] = carried[...] * mm(readout, state_in[0])
-    squares = jnp.zeros((length, 1), F32)
-    products = jnp.zeros((length, 1), F32)
+    step_x[...] = pick(softplus(dt_raw[...] + heads[0:1]), spread[...])
     for at, width in column_blocks(inner):
         cols = slice(at, at + width)
-        x_pre = pre[0, :, bc_width + at : bc_width + at + width]
+        x_pre = pre[:, bc_width + at : bc_width + at + width]
         values = x_pre * sigmoid(x_pre)
         fed = (values * step_x[:, cols]).astype(BF16)
         masks = half_masks(width)
-        near[:, :width] = carried[:, cols] + skip[:, cols] * values
+        near[:, cols] = skip[:, cols] * values
         for start in range(0, length, LANES):
             stop = start + LANES
-            found = near[start:stop, :width]
+            found = near[start:stop, cols]
             for k, mask in enumerate(masks):
                 head = at // HEAD + k
                 spread_log = total[start:stop, head : head + 1] - total_t[head : head + 1, :stop]
                 mixing = pair[start:stop, :stop] * jnp.exp(spread_log + seg[start:stop, :stop])
                 found = found + mm(mixing.astype(BF16), jnp.where(mask, fed[:stop], 0))
-            near[start:stop, :width] = found
-        mixed = near[:, :width]
-        mixer[0, :, cols] = mixed
-        raw_gate = gate[0, :, cols]
+            near[start:stop, cols] = found
+
+
+def mix_states(pre, cum, age, state_in, near, gate, grad_gn, w_out_t, norm_gate, spread,
+               mixer, part, stats, carried, gated_low):
+    length, inner = near.shape
+    open_start = age[...] > row_index(length)
+    carried[...] = pick(jnp.where(open_start, jnp.exp(cum[...]), 0.0), spread[...])
+    carried[...] = carried[...] * mm(activated(pre.at[:, LANES : 2 * LANES]), state_in[...])
+    squares = jnp.zeros((length, 1), F32)
+    products = jnp.zeros((length, 1), F32)
+    for at, width in column_blocks(inner):
+        cols = slice(at, at + width)
+        mixed = near[:, cols] + carried[:, cols]
+        mixer[:, cols] = mixed
+        raw_gate = gate[:, cols]
         gated = mixed * (raw_gate * sigmoid(raw_gate))
         weighted = gated * norm_gate[:, cols]
         gated_low[:, cols] = weighted.astype(BF16)
         squares = squares + jnp.sum(gated * gated, 1, keepdims=True)
-        products = products + jnp.sum(grad_gn[0, :, cols] * weighted, 1, keepdims=True)
-    part[0] = mm_nt(gated_low[...], w_out_t[...]).astype(BF16)
+        products = products + jnp.sum(grad_gn[:, cols] * weighted, 1, keepdims=True)
+    part[...] = mm_nt(gated_low[...], w_out_t()).astype(BF16)
     lane = lax.broadcasted_iota(jnp.int32, (length, LANES), 1)
     columns = jnp.where(lane == 0, squares, jnp.where(lane == 1, products, 0.0))
-    stats[0] = columns.T[:8]
+    stats[...] = columns.T[:8]
+
+
+def forward_local(hid, halo, age, norm_in, w_in, taps, heads, spread, tri,
+                  normed, raw, pre, dt_raw, cum, local, decay, act):
+    project(hid.at[0], halo.at[0], age.at[0], norm_in, w_in, taps, heads, spread, tri, normed.at[0], raw.at[0],
+            pre.at[0], dt_raw.at[0], cum.at[0], local.at[0], decay.at[0], act)
+
+
+def forward_mix(pre, dt_raw, cum, age, state_in, normed, out_grad, w_z, w_out_t, norm_gate, skip, heads, spread,
+                mixer, gate, grad_gn, part, stats, near, seg, pair, carried, step_x, gated_low):
+    w_z_all, w_out_all = (lambda: w_z[...]), (lambda: w_out_t[...])
+    mix_within(pre.at[0], dt_raw.at[0], cum.at[0], age.at[0], normed.at[0], out_grad.at[0], w_z_all, w_out_all, skip,
+               heads, spread, near, gate.at[0], grad_gn.at[0], seg, pair, step_x)
+    mix_states(pre.at[0], cum.at[0], age.at[0], state_in.at[0], near, gate.at[0], grad_gn.at[0], w_out_all, norm_gate,
+               spread, mixer.at[0], part.at[0], stats.at[0], carried, gated_low)
 
 
 def backward_local(inner_all, mixer, gate, grad_gn, stats, pre, dt_raw, cum, age, age_row, state_in, normed, out_grad,
@@ -491,46 +512,79 @@
     ]
 
 
-def gather_blocks(copies, place, stage, out, received, own):
-    shard, context, _ = place
+def gather_step(step, start, arrived, stage, out, received):
+    place = shard, context, _ = coordinates()
     count = lax.axis_size("context")
     up, down, next_x, next_y = neighbours(place)
     mine, beside_x, beside_y, across = [(shard ^ k) * count for k in (0, 1, 2, 3)]
 
-    def pass_on(source, slot, to, there=True):
+    def pass_on(number, source, slot, to, there=True):
         if to[0] is not True:
             there = to[0] if there is True else there & to[0]
-        copies.start(source, out.at[slot], received.at[slot], to[1], there)
-
-    local = pltpu.make_async_copy(stage, out.at[mine + context], own)
-    local.start()
-    for to in (up, down, next_x, next_y):
-        pass_on(stage, mine + context, to)
-    yield
-    for distance in range(1, count):
-        for at, there, to in ((context - distance, context >= distance, up),
-                              (context + distance, context + distance < count, down)):
-            slot = mine + jnp.clip(at, 0, count - 1)
-            copies.arrived(out.at[slot], received.at[slot], there)
-            for target in (to, next_x, next_y):
-                pass_on(out.at[slot], slot, target, there)
-        yield
-    for distance in range(count):
-        for at, there in ((context - distance, context >= distance),
-                          (context + distance, context + distance < count))[: 2 if distance else 1]:
-            at = jnp.clip(at, 0, count - 1)
-            low = at < count // 2
-            copies.arrived(out.at[beside_x + at], received.at[beside_x + at], there)
-            pass_on(out.at[beside_x + at], beside_x + at, next_y, there & low)
-            copies.arrived(out.at[beside_y + at], received.at[beside_y + at], there)
-            pass_on(out.at[beside_y + at], beside_y + at, next_x, there & (at >= count // 2))
-        yield
-    for at in range(count):
-        copies.arrived(out.at[across + at], received.at[across + at])
-    local.wait()
-
-
-GATHER_COPIES = 64
+        start(number, source, out.at[slot], received.at[slot], to[1], there)
+
+    def both_ways(distance):
+        found = [(context - distance, context >= distance, up),
+                 (context + distance, context + distance < count, down)]
+        return [(jnp.clip(at, 0, count - 1), there, to) for at, there, to in found[: 2 if distance else 1]]
+
+    if step == 0:
+        for k, to in enumerate((up, down, next_x, next_y)):
+            pass_on(k, stage, mine + context, to)
+    elif step < count:
+        for k, (at, there, to) in enumerate(both_ways(step)):
+            slot = mine + at
+            arrived(out.at[slot], received.at[slot], there)
+            for m, target in enumerate((to, next_x, next_y)):
+                pass_on(4 + (step - 1) * 6 + k * 3 + m, out.at[slot], slot, target, there)
+    elif step < 2 * count:
+        for k, (at, there, _) in enumerate(both_ways(step - count)):
+            number = 4 + (count - 1) * 6 + (step - count) * 4 + k * 2
+            slot_x, slot_y = beside_x + at, beside_y + at
+            arrived(out.at[slot_x], received.at[slot_x], there)
+            pass_on(number, out.at[slot_x], slot_x, next_y, there & (at < count // 2))
+            arrived(out.at[slot_y], received.at[slot_y], there)
+            pass_on(number + 1, out.at[slot_y], slot_y, next_x, there & (at >= count // 2))
+    else:
+        for at in range(count):
+            arrived(out.at[across + at], received.at[across + at], True)
+
+
+def gather_steps():
+    return 2 * lax.axis_size("context") + 1
+
+
+GATHER_COPIES = 40
+
+
+class Numbered:
+    def __init__(self, send):
+        self.send = send
+
+    def copy(self, number, source, target, received, device):
+        return pltpu.make_async_remote_copy(
+            src_ref=source, dst_ref=target, send_sem=self.send.at[number], recv_sem=received,
+            device_id=device, device_id_type=MESH,
+        )
+
+    def when(self, there, action):
+        if there is True:
+            action()
+        else:
+            pl.when(there)(action)
+
+    def start(self, number, source, target, received, device, there=True):
+        self.when(there, self.copy(number, source, target, received, device).start)
+
+    def sent(self, number, source, target, received, device, there=True):
+        self.when(there, self.copy(number, source, target, received, device).wait_send)
+
+    def arrived(self, target, received, there=True):
+        other = {"tensor": 1 - lax.axis_index("tensor")}
+        self.when(there, self.copy(0, target, target, received, other).wait_recv)
+
+    def nothing(self, *_):
+        pass
 
 
 def scatter_scratch(rows, width):
@@ -612,7 +666,7 @@
         out[...] += from_up[context].astype(F32)
 
 
-def gather_inputs(w_bc, w_dt, w_x, conv_bc, conv_x, hid, out, halo, taps, stage, send, received, others, own):
+def gather_inputs(w_bc, w_dt, w_x, conv_bc, conv_x, hid, out, halo, taps, stage, passing, send, received, others, own):
     place = shard, context, tensor = coordinates()
     length = hid.shape[1]
     own_bc, head_count = w_bc.shape[1], w_dt.shape[1]
@@ -635,8 +689,14 @@
     tail = pl.ds(length - HALO, HALO)
     copies.start(hid.at[:, tail], halo, others.at[2], around[UP][1], around[UP][0])
     copies.arrived(stage.at[:, other_cols], others.at[0])
-    for _ in gather_blocks(copies, place, stage, out, received, own):
-        pass
+    numbered = Numbered(passing)
+    local = pltpu.make_async_copy(stage, out.at[shard * lax.axis_size("context") + context], own)
+    local.start()
+    for step in range(gather_steps()):
+        gather_step(step, numbered.start, numbered.arrived, stage, out, received)
+    for step in range(gather_steps()):
+        gather_step(step, numbered.sent, numbered.nothing, stage, out, received)
+    local.wait()
     copies.arrived(taps.at[:, other_cols], others.at[1])
     copies.arrived(halo, others.at[2], context > 0)
 
@@ -694,18 +754,109 @@
                 steps.remove(one)
 
 
-def states_up(local, decay, w_z, w_out, arrived, out, stage, leaving, send, received, own, states):
-    place = coordinates()
+GATHER_TURNS = (0, 1, 2, 3, 3, 4, 5, 6, 7)
+
+
+def forward(hid, halo, age, out_grad, norm_in, w_in, w_z, w_out, taps, heads, spread, tri, norm_gate, skip,
+            raw, mixer, part, stats, normed_out, pre_out, dt_out, cum_out, gate_out, grad_gn_out, state_out, decay_out,
+            both_out,
+            normed, pre, dt_raw, cum, gate, grad_gn, near, leaving, arrived, decay, both, stage, act, seg, pair, step_x,
+            gated_low, send, received, own, states, stores):
+    place = shard, context, _ = coordinates()
+    phase, i = pl.program_id(0), pl.program_id(1)
+    pieces = pl.num_programs(1)
     inner = w_z.shape[1]
-    stage[:, :inner] = w_z[...]
-    stage[:, inner:] = w_out[...].astype(F32).T.astype(BF16)
-    greet(neighbours(place))
-    copies = Copies(send)
-    in_turn(
-        gather_blocks(copies, place, stage, out, received, own),
-        chain_states(copies, place, local, decay, arrived, leaving, states, 1),
-    )
-    copies.finish()
+    count = lax.axis_size("context")
+    numbered = Numbered(send)
+
+    def store(k, source, target):
+        return pltpu.make_async_copy(source.at[i], target.at[i], stores.at[k, i])
+
+    first, last = context == 0, context == count - 1
+
+    def passed(c):
+        return pltpu.make_async_remote_copy(
+            src_ref=leaving.at[c], dst_ref=arrived.at[c], send_sem=states.at[1, c], recv_sem=states.at[0, c],
+            device_id={"context": context + 1}, device_id_type=MESH,
+        )
+
+    @pl.when((phase == 0) & (i == 0))
+    def _():
+        stage[:, :inner] = w_z[...]
+        stage[:, inner:] = w_out[...].astype(F32).T.astype(BF16)
+        greet(neighbours(place))
+        gather_step(0, numbered.start, numbered.arrived, stage, both, received)
+        pltpu.make_async_copy(stage, both.at[shard * count + context], own).start()
+
+    turn = phase * pieces + i
+    c = jnp.clip(turn // 2 - context, 0, pieces - 1)
+
+    @pl.when((turn % 2 == 0) & (turn // 2 >= context) & (turn // 2 - context < pieces) & jnp.logical_not(first | last))
+    def _():
+        passed(c).wait_recv()
+        leaving[c] = (decay[c, :1] * arrived[c].astype(F32) + leaving[c].astype(F32)).astype(BF16)
+        passed(c).start()
+
+    @pl.when(phase == 0)
+    def _():
+        project(hid.at[0], halo.at[0], age.at[0], norm_in, w_in, taps, heads, spread, tri, normed.at[i], raw.at[0],
+                pre.at[i], dt_raw.at[i], cum.at[i], leaving.at[i], decay.at[i], act)
+        for k, (source, target) in enumerate(((normed, normed_out), (pre, pre_out), (dt_raw, dt_out), (cum, cum_out),
+                                              (decay, decay_out))):
+            store(k, source, target).start()
+
+        @pl.when(first)
+        def _():
+            arrived[i] = jnp.zeros(arrived.shape[1:], BF16)
+            passed(i).start()
+
+    for step in range(1, gather_steps()):
+
+        @pl.when((phase == 0) & (i == GATHER_TURNS[step]))
+        def _(step=step):
+            gather_step(step, numbered.start, numbered.arrived, stage, both, received)
+
+    @pl.when((phase == 0) & (i == pieces - 1))
+    def _():
+        for step in range(gather_steps()):
+            gather_step(step, numbered.sent, numbered.nothing, stage, both, received)
+        pltpu.make_async_copy(stage, both.at[shard * count + context], own).wait()
+        pltpu.make_async_copy(both, both_out, own).start()
+
+    @pl.when((phase == 1) & (i == pieces - 1))
+    def _():
+        pltpu.make_async_copy(both, both_out, own).wait()
+
+    def w_z_all():
+        return both[:, :, :inner].reshape(-1, inner)
+
+    def w_out_all():
+        return both[:, :, inner:].reshape(-1, inner)
+
+    @pl.when(phase == 1)
+    def _():
+        mix_within(pre.at[i], dt_raw.at[i], cum.at[i], age.at[0], normed.at[i], out_grad.at[0], w_z_all, w_out_all, skip,
+                   heads, spread, near.at[i], gate.at[i], grad_gn.at[i], seg, pair, step_x)
+        store(5, gate, gate_out).start()
+        store(6, grad_gn, grad_gn_out).start()
+
+    @pl.when(phase == 2)
+    def _():
+        @pl.when(last)
+        def _():
+            passed(i).wait_recv()
+
+        store(7, arrived, state_out).start()
+        mix_states(pre.at[i], cum.at[i], age.at[0], arrived.at[i], near.at[i], gate.at[i], grad_gn.at[i], w_out_all,
+                   norm_gate, spread, mixer.at[0], part.at[0], stats.at[0], step_x, gated_low)
+        for k, (source, target) in enumerate(((normed, normed_out), (pre, pre_out), (dt_raw, dt_out), (cum, cum_out),
+                                              (decay, decay_out), (gate, gate_out), (grad_gn, grad_gn_out),
+                                              (arrived, state_out))):
+            store(k, source, target).wait()
+
+        @pl.when(jnp.logical_not(last))
+        def _():
+            passed(i).wait_send()
 
 
 def add_over_cores(own, out, other, send, received):
@@ -865,8 +1016,35 @@
         w_in = gather_rows(jnp.concatenate([w_bc_all, w_dt_wide, w_x], 1))
         return w_in, passed_along(hid[:, hid.shape[1] - HALO :], 1), taps
 
-    def states_up(self, local, decay, w_z, w_out):
-        return chain(local, decay, 1), (gather_rows(w_z), fixed), (gather_rows(w_out.T), fixed)
+    def forward(self, hid, halo, age, seed, norm_in, w_in, w_z, w_out, taps, heads, spread, tri, norm_gate, skip):
+        pieces, length, model = hid.shape
+        inner, channels = w_z.shape[1], taps.shape[1]
+        token = functools.partial(shaped, F32, pieces, length)
+        token_low = functools.partial(shaped, BF16, pieces, length)
+        normed, raw, pre, dt_raw, cum, local, decay = call(
+            forward_local, pieces,
+            [(hid, by_piece), (halo, by_piece), (age, by_piece), (norm_in, fixed), (w_in, fixed), (taps, fixed),
+             (heads, fixed), (spread, fixed), (tri, fixed)],
+            [(shaped(BF16, pieces, HALO + length, model), by_piece),
+             (shaped(F32, pieces, HALO + length, channels), by_piece), (token(channels), by_piece),
+             (token(LANES), by_piece), (token(LANES), by_piece), (shaped(BF16, pieces, LANES, inner), by_piece),
+             (shaped(F32, pieces, 8, inner), by_piece)],
+            [((length, channels), F32)], "forward_local",
+        )
+        state_in = chain(local, decay, 1)
+        w_z_all, w_out_t = gather_rows(w_z), gather_rows(w_out.T)
+        square = ((length, length), F32)
+        token_wide = ((length, inner), F32)
+        mixer, gate, grad_gn, part, stats = call(
+            forward_mix, pieces,
+            [(pre, by_piece), (dt_raw, by_piece), (cum, by_piece), (age, by_piece), (state_in, by_piece),
+             (normed, by_piece), (seed, by_piece), (w_z_all, fixed), (w_out_t, fixed), (norm_gate, fixed),
+             (skip, fixed), (heads, fixed), (spread, fixed)],
+            [(token(inner), by_piece), (token(inner), by_piece), (token(inner), by_piece), (token_low(model), by_piece),
+             (shaped(F32, pieces, 8, length), by_piece)],
+            [token_wide, square, square, token_wide, token_wide, ((length, inner), BF16)], "forward_mix",
+        )
+        return normed, raw, pre, dt_raw, cum, decay, state_in, mixer, gate, grad_gn, part, stats, (w_z_all, fixed)
 
     def over_cores(self, stats):
         return lax.psum(stats, "tensor")
@@ -903,23 +1081,67 @@
             [(w_bc, IN_VMEM), (w_dt, IN_VMEM), (w_x, IN_VMEM), (conv_bc, IN_VMEM), (conv_x, IN_VMEM), (hid, ANY)],
             [(shaped(BF16, blocks, rows, in_width), ANY), (shaped(BF16, pieces, HALO, model), ANY),
              (shaped(F32, 8, 2 * LANES + inner), IN_VMEM)],
-            [pltpu.VMEM((rows, in_width), BF16), DMA((GATHER_COPIES,)), DMA((blocks,)), DMA((3,)), DMA],
+            [pltpu.VMEM((rows, in_width), BF16), DMA((GATHER_COPIES,)), DMA((3,)), DMA((blocks,)), DMA((3,)), DMA],
         )
         return w_in.reshape(model, in_width), halo, taps
 
-    def states_up(self, local, decay, w_z, w_out):
+    def forward(self, hid, halo, age, seed, norm_in, w_in, w_z, w_out, taps, heads, spread, tri, norm_gate, skip):
+        pieces, length, model = hid.shape
         rows, inner = w_z.shape
-        model = w_out.shape[1] * 16
-        pieces = local.shape[0]
-        arrived, both = call_between(
-            states_up, 2,
-            [(local, IN_VMEM), (decay, IN_VMEM), (w_z, IN_VMEM), (w_out, IN_VMEM)],
-            [(shaped(BF16, *local.shape), IN_VMEM), (shaped(BF16, 16, rows, 2 * inner), ANY)],
-            [pltpu.VMEM((rows, 2 * inner), BF16), pltpu.VMEM(local.shape, BF16), DMA((GATHER_COPIES,)), DMA((16,)), DMA,
-             DMA((2, pieces))],
-        )
-        both = both.reshape(model, 2 * inner)
-        return arrived, (both, part_of(inner, 0)), (both, part_of(inner, 1))
+        channels = taps.shape[1]
+        lead = HALO + length
+
+        def at_phase(phase):
+            def cut(array):
+                rest = array.shape[1:]
+
+                def where(p, i):
+                    return (jnp.where(p == phase, i, jnp.where(p < phase, 0, pieces - 1)),) + (0,) * len(rest)
+
+                return pl.BlockSpec((1,) + rest, where)
+
+            return cut
+
+        def always(array):
+            return pl.BlockSpec((1,) + array.shape[1:], lambda p, i: (i,) + (0,) * (array.ndim - 1))
+
+        def once(array):
+            return pl.BlockSpec(array.shape, lambda p, i: (0,) * array.ndim, pipeline_mode=pl.Buffered(1))
+
+        def anywhere(array):
+            return ANY
+
+        token = functools.partial(shaped, F32, pieces, length)
+        state = shaped(BF16, pieces, LANES, inner)
+        normed, pre, narrow = shaped(BF16, pieces, lead, model), token(channels), token(LANES)
+        decay, both = shaped(F32, pieces, 8, inner), shaped(BF16, 16, rows, 2 * inner)
+        inputs = [(hid, at_phase(0)), (halo, at_phase(0)), (age, always), (seed, at_phase(1)), (norm_in, once),
+                  (w_in, once), (w_z, once), (w_out, once), (taps, once), (heads, once), (spread, once), (tri, once),
+                  (norm_gate, once), (skip, once)]
+        outputs = [(shaped(F32, pieces, lead, channels), at_phase(0)), (token(inner), at_phase(2)),
+                   (shaped(BF16, pieces, length, model), at_phase(2)), (shaped(F32, pieces, 8, length), at_phase(2)),
+                   (normed, anywhere), (pre, anywhere), (narrow, anywhere), (narrow, anywhere),
+                   (token(inner), anywhere), (token(inner), anywhere), (state, anywhere), (decay, anywhere),
+                   (both, anywhere)]
+        kept = [normed, pre, narrow, narrow, token(inner), token(inner), token(inner), state, state, decay, both]
+        raw, mixer, part, stats, normed, pre, dt_raw, cum, gate, grad_gn, state_in, decay, both = pl.pallas_call(
+            forward,
+            grid=(3, pieces),
+            in_specs=[cut(array) for array, cut in inputs],
+            out_specs=[cut(shape) for shape, cut in outputs],
+            out_shape=[shape for shape, _ in outputs],
+            scratch_shapes=[pltpu.VMEM(shape.shape, shape.dtype) for shape in kept]
+            + [pltpu.VMEM((rows, 2 * inner), BF16), pltpu.VMEM((length, channels), F32),
+               pltpu.VMEM((length, length), F32), pltpu.VMEM((length, length), F32), pltpu.VMEM((length, inner), F32),
+               pltpu.VMEM((length, inner), BF16), DMA((GATHER_COPIES,)), DMA((16,)), DMA, DMA((2, pieces)),
+               DMA((8, pieces))],
+            compiler_params=pltpu.CompilerParams(
+                collective_id=2, has_side_effects=True, vmem_limit_bytes=VMEM_BYTES
+            ),
+            name="forward",
+        )(*[array for array, _ in inputs])
+        w_z_all = (both.reshape(model, 2 * inner), part_of(inner, 0))
+        return normed, raw, pre, dt_raw, cum, decay, state_in, mixer, gate, grad_gn, part, stats, w_z_all
 
     def over_cores(self, stats):
         return call_between(
@@ -1002,30 +1224,12 @@
     token = functools.partial(shaped, F32, pieces, length)
     token_low = functools.partial(shaped, BF16, pieces, length)
     state = shaped(BF16, pieces, LANES, inner)
-    normed, raw, pre, dt_raw, cum, local, decay = call(
-        forward_local, pieces,
-        [(hid, by_piece), (halo, by_piece), (age, by_piece), (norm_in, fixed), (w_in, fixed), (taps, fixed),
-         (heads, fixed), (spread, fixed), (tri, fixed)],
-        [(shaped(BF16, pieces, lead, model), by_piece), (shaped(F32, pieces, lead, channels), by_piece),
-         (token(channels), by_piece), (token(LANES), by_piece), (token(LANES), by_piece), (state, by_piece),
-         (shaped(F32, pieces, 8, inner), by_piece)],
-        [((length, channels), F32)], "forward_local",
+    normed, raw, pre, dt_raw, cum, decay, state_in, mixer, gate, grad_gn, part, stats, w_z_all = between.forward(
+        hid, halo, age, seed, norm_in, w_in, w_z, w_out, taps, heads, spread, tri, norm_gate, skip
     )
-
-    state_in, w_z_all, w_out_t = between.states_up(local, decay, w_z, w_out)
-
     square = ((length, length), F32)
     token_wide = ((length, inner), F32)
     token_narrow = ((length, inner), BF16)
-    mixer, gate, grad_gn, part, stats = call(
-        forward_mix, pieces,
-        [(pre, by_piece), (dt_raw, by_piece), (cum, by_piece), (age, by_piece), (state_in, by_piece), (normed, by_piece),
-         (seed, by_piece), w_z_all, w_out_t, (norm_gate, fixed), (skip, fixed), (heads, fixed),
-         (spread, fixed)],
-        [(token(inner), by_piece), (token(inner), by_piece), (token(inner), by_piece), (token_low(model), by_piece),
-         (shaped(F32, pieces, 8, length), by_piece)],
-        [((length, LANES), F32), square, square, token_wide, token_wide, token_narrow], "forward_mix",
-    )
 
     stats = between.over_cores(stats)
 

time: 385 us -> 342 us (0.89)
  Pallas kernels: 364 us -> 323 us
    pallas_call x0 -> x1, Pallas kernels: none -> 59.7 us  [forward(): pl.pallas_call(forward, grid=(3, pieces), in_specs=[cut(array) for array,...]
    pallas_call x5 -> x4, Pallas kernels: 224 us -> 165 us  [call_between(): pl.pallas_call(kernel, in_specs=[spec for _, spec in inputs], out_specs=[...]
    pallas_call x5 -> x3, Pallas kernels: 141 us -> 98.1 us  [call(): pl.pallas_call(kernel, grid=(pieces,), in_specs=[cut(array) for array, cu...]
where the time goes in v3:
time: 342 us; the launch traced here: 340 us
  Pallas kernels  323 us (94%)
  local copies, waits for them, and re-layouts  13.7 us (4%)
    pallas_call x4, Pallas kernels, call_between(): pl.pallas_call(kernel, in_specs=[spec for _, spec in inputs], out_specs=[...  165 us
    pallas_call x3, Pallas kernels, call(): pl.pallas_call(kernel, grid=(pieces,), in_specs=[cut(array) for array, cu...  98.1 us
    pallas_call x1, Pallas kernels, forward(): pl.pallas_call(forward, grid=(3, pieces), in_specs=[cut(array) for array,...  59.7 us

profile of v3, /device:TPU:0, one launch (start us, length us, event | category | flops | bytes accessed | tf_op | source)
XLA Modules:
  0.0 340.2 jit_solution(2518139766277583684)
XLA Ops:
  0.7 0.1 pad.12.clone
  0.7 0.1 pad.11.clone
  0.8 0.7 pad_bitcast_fusion
  1.5 0.7 maximum_maximum_fusion.heads
  2.2 1.3 broadcast_in_dim.11.norm_in
  3.4 1.3 broadcast_in_dim.24.norm_gate
  4.7 0.7 reshape.99
  5.4 0.7 broadcast_in_dim.25
  6.1 0.7 broadcast_in_dim_reshape.3.skip
  6.8 1.4 copy.33.w_dt
  8.2 0.6 broadcast_in_dim.26.age_row
  8.8 1.7 copy.34.w_out
  10.5 1.3 broadcast_in_dim.10.age
  11.8 38.8 %gather_inputs.1 = (bf16[16,48,1152]{2,1,0:T(8,128)(2,1)}, bf16[8,16,768]{2,1,0:T(8,128)(2,1)}, f32[8,1024]{1,0:T(8,128)}) custom-call(bf16[48,128]{1,0:T(8,128)(2,1)} %w_bc.1, bf16[48,12]{1,0:T(8,128)(2,1)} %copy.33.w_dt, bf16[48,768]{1,0:T(8,128)(2,1)} %w_x.1, f32[5,128]{1,0:T(8,128)} %conv_bc.1, f32[5,768]{1,0:T(8,128)} %conv_x.1, ...), custom_call_target="tpu_custom_call" | custom-call | tf_op jit(solution)/shard_map/gather_inputs/pallas_call | solution.py:967
  50.6 59.7 %forward.1 = (f32[8,272,1024]{2,1,0:T(8,128)}, f32[8,256,768]{2,1,0:T(8,128)}, bf16[8,256,768]{2,1,0:T(8,128)(2,1)}, f32[8,8,256]{2,1,0:T(8,128)}, bf16[8,272,76...) custom-call(bf16[8,256,768]{2,1,0:T(8,128)(2,1)} %bitcast.17, ...), custom_call_target="tpu_custom_call" | custom-call | tf_op jit(solution)/shard_map/forward/pallas_call | solution.py:1127
  110.3 2.8 add_over_cores.1.stats
  113.1 40.4 %backward_local.1 = (f32[8,256,768]{2,1,0:T(8,128)}, bf16[8,256,768]{2,1,0:T(8,128)(2,1)}, bf16[8,256,768]{2,1,0:T(8,128)(2,1)}, f32[8,256,128]{2,1,0:T(8,128)},...) custom-call(f32[8,256,768]{2,1,0:T(8,128)} %get-tuple-element.75.mix, ...), custom_call_target="tpu_custom_call" | custom-call | tf_op jit(solution)/shard_map/backward_local/pallas_call | solution.py:431
  153.5 76.0 %states_down.1 = (bf16[8,128,768]{2,1,0:T(8,128)(2,1)}, f32[48,1536]{1,0:T(8,128)}, bf16[1,8,256,768]{3,2,1,0:T(8,128)(2,1)}) custom-call(bf16[8,128,768]{2,1,0:T(8,128)(2,1)} %get-tuple-element.83.local, f32[8,8,768]{2,1,0:T(8,128)} %get-tuple-element.84.decay, bf16[16,48,768]{2,1,0:T(8,128)(2,1)} %bitcast.27, bf16[16,48,768]{2,1,0:T(8,128)(2,1)} %bitcast.28, ...), custom_call_target="tpu_custom_call" | custom-call | tf_op jit(solution)/shard_map/states_down/pallas_call | solution.py:967
  229.6 44.0 %backward_finish.1 = (bf16[8,256,768]{2,1,0:T(8,128)(2,1)}, bf16[8,16,768]{2,1,0:T(8,128)(2,1)}, bf16[768,1152]{1,0:T(8,128)(2,1)}, f32[8,1024]{1,0:T(8,128)}, f32[8,128]{1,0:T(8,128)}, /*index=5*/f32[8,768]{1,0:T(8,128)}) custom-call(bf16[8,128,768]{2,1,0:T(8,128)(2,1)} %get-tuple-element.88.grad_later, bf16[8,128,768]{2,1,0:T(8,128)(2,1)} %get-tuple-element.81.state_in, ...), custom_call_target="tpu_custom_call" | custom-call | tf_op jit(solution)/shard_map/backward_finish/pallas_call | solution.py:431
  273.6 47.2 %last_sums.1 = (f32[48,1024]{1,0:T(8,128)}, bf16[1,8,256,768]{3,2,1,0:T(8,128)(2,1)}, bf16[8,16,768]{2,1,0:T(8,128)(2,1)}, bf16[1,8,16,768]{3,2,1,0:T(8,128)(2,1...) custom-call(bf16[16,48,1152]{2,1,0:T(8,128)(2,1)} %bitcast.26, ...), custom_call_target="tpu_custom_call" | custom-call | tf_op jit(solution)/shard_map/last_sums/pallas_call | solution.py:967
  320.8 13.6 %finish.1 = (bf16[8,256,768]{2,1,0:T(8,128)(2,1)}, bf16[8,256,768]{2,1,0:T(8,128)(2,1)}, f32[48,768]{1,0:T(8,128)}, f32[48,768]{1,0:T(8,128)}, f32[48,128]{1,0:T...) custom-call(bf16[8,256,768]{2,1,0:T(8,128)(2,1)} %bitcast.19, ...), custom_call_target="tpu_custom_call" | custom-call | tf_op jit(solution)/shard_map/finish/pallas_call | solution.py:431
  334.4 1.3 reduce
  335.7 1.3 reduce.1
  337.0 1.4 copy.35
  338.4 1.8 copy.36
  (4 shorter events, 0.0 us)

commit v4 on v3

--- a/solution.py
+++ b/solution.py
@@ -188,61 +188,65 @@
                spread, mixer.at[0], part.at[0], stats.at[0], carried, gated_low)
 
 
-def backward_local(inner_all, mixer, gate, grad_gn, stats, pre, dt_raw, cum, age, age_row, state_in, normed, out_grad,
-                   norm_gate, skip, heads, spread, gather,
-                   grad_fed, grad_mix, grad_gate, grad_cum, grad_bc, grad_state, grad_wz, grad_wo, sums,
-                   sum_z, sum_o, near, seg, pair, grad_pair, carried, step_x, gated_low, from_state):
-    length, inner = mixer.shape[1:]
+def gate_back(inner_all, mixer, gate, grad_gn, stats, pre, cum, age, state_in, normed, out_grad, norm_gate, skip,
+              spread, gather, grad_mix, grad_gate, grad_cum, grad_c, grad_state, sums, sum_z, sum_o,
+              carried, gated_low, from_state):
+    length, inner = mixer.shape
     bc_width = 2 * LANES
-
-    @pl.when(is_first_step())
-    def _():
-        sum_z[...] = jnp.zeros_like(sum_z)
-        sum_o[...] = jnp.zeros_like(sum_o)
-        sums[...] = jnp.zeros_like(sums)
-
-    readout = pre[0, :, LANES:bc_width]
-    readout = (readout * sigmoid(readout)).astype(BF16)
-    inputs_b = pre[0, :, :LANES]
-    inputs_b = (inputs_b * sigmoid(inputs_b)).astype(BF16)
+    open_start = age[...] > row_index(length)
+    carried[...] = pick(jnp.where(open_start, jnp.exp(cum[...]), 0.0), spread[...])
+    means = stats[...].T / inner_all
+    scale = lax.rsqrt(means[:, :1] + EPSILON)
+    pull = scale * scale * scale * means[:, 1:2]
+    rows_sum = jnp.zeros((length, LANES), F32)
+    for at, width in column_blocks(inner):
+        cols = slice(at, at + width)
+        x_pre = pre[:, bc_width + at : bc_width + at + width]
+        values = x_pre * sigmoid(x_pre)
+        mixed = mixer[:, cols]
+        raw_gate = gate[:, cols]
+        logistic = sigmoid(raw_gate)
+        acted = raw_gate * logistic
+        gated = mixed * acted
+        grad_out = grad_gn[:, cols]
+        gated_scaled = gated * scale
+        gated_low[:, cols] = (gated_scaled * norm_gate[:, cols]).astype(BF16)
+        grad_gated = scale * (grad_out * norm_gate[:, cols]) - gated * pull
+        grad_gate[:, cols] = (grad_gated * mixed * (logistic * (1.0 + raw_gate * (1.0 - logistic)))).astype(BF16)
+        mix_low = (grad_gated * acted).astype(BF16)
+        grad_mix[:, cols] = mix_low
+        mix_wide = mix_low.astype(F32)
+        sums[0:1, cols] += jnp.sum(grad_out * gated_scaled, 0, keepdims=True)
+        sums[1:2, cols] += jnp.sum(mix_wide * values, 0, keepdims=True)
+        rows_sum = rows_sum + pick(mix_wide * (mixed - skip[:, cols] * values), gather[cols])
+        from_state[:, cols] = (carried[:, cols] * mix_wide).astype(BF16)
+    grad_cum[...] = rows_sum
+    grad_state[...] = mm_tn(activated(pre.at[:, LANES:bc_width]), from_state[...]).astype(BF16)
+    grad_c[...] = mm_nt(from_state[...], state_in[...])
+    sum_z[...] += mm_tn(normed[HALO:], grad_gate[...])
+    sum_o[...] += mm_tn(out_grad[...], gated_low[...])
+
+
+def within_back(pre, dt_raw, cum, age_row, grad_mix, heads, spread, gather, grad_fed, grad_cum, grad_bc,
+                seg, pair, grad_pair, step_x):
+    length, inner = grad_mix.shape
+    bc_width = 2 * LANES
+    readout, inputs_b = activated(pre.at[:, LANES:bc_width]), activated(pre.at[:, :LANES])
     pair[...] = mm_nt(inputs_b, readout)
     grad_pair[...] = jnp.zeros_like(grad_pair)
     row = lax.broadcasted_iota(jnp.int32, (length, length), 0)
     col = lax.broadcasted_iota(jnp.int32, (length, length), 1)
     back = (col - row).astype(F32)
-    seg[...] = jnp.where((back >= 0) & (back <= age_row[0][:1]), 0.0, GONE)
-    total = cum[0]
+    seg[...] = jnp.where((back >= 0) & (back <= age_row[:1]), 0.0, GONE)
+    total = cum[...]
     total_t = total.T
-    step = softplus(dt_raw[0] + heads[0:1])
-    step_x[...] = pick(step, spread[...])
-    open_start = age[0] > row_index(length)
-    carried[...] = pick(jnp.where(open_start, jnp.exp(total), 0.0), spread[...])
-    means = stats[0].T / inner_all
-    scale = lax.rsqrt(means[:, :1] + EPSILON)
-    pull = scale * scale * scale * means[:, 1:2]
-    rows_sum = jnp.zeros((length, LANES), F32)
+    step_x[...] = pick(softplus(dt_raw[...] + heads[0:1]), spread[...])
+    cols_sum = jnp.zeros((length, LANES), F32)
     for at, width in column_blocks(inner):
         cols = slice(at, at + width)
-        x_pre = pre[0, :, bc_width + at : bc_width + at + width]
-        values = x_pre * sigmoid(x_pre)
-        fed = (values * step_x[:, cols]).astype(BF16)
-        mixed = mixer[0, :, cols]
-        raw_gate = gate[0, :, cols]
-        logistic = sigmoid(raw_gate)
-        acted = raw_gate * logistic
-        gated = mixed * acted
-        grad_out = grad_gn[0, :, cols]
-        gated_scaled = gated * scale
-        gated_low[:, cols] = (gated_scaled * norm_gate[:, cols]).astype(BF16)
-        grad_gated = scale * (grad_out * norm_gate[:, cols]) - gated * pull
-        grad_gate[0, :, cols] = (grad_gated * mixed * (logistic * (1.0 + raw_gate * (1.0 - logistic)))).astype(BF16)
-        mix_low = (grad_gated * acted).astype(BF16)
-        grad_mix[0, :, cols] = mix_low
-        mix_wide = mix_low.astype(F32)
-        sums[0:1, cols] += jnp.sum(grad_out * gated_scaled, 0, keepdims=True)
-        sums[1:2, cols] += jnp.sum(mix_wide * values, 0, keepdims=True)
-        rows_sum = rows_sum + pick(mix_wide * (mixed - skip[:, cols] * values), gather[cols])
-        from_state[:, cols] = (carried[:, cols] * mix_wide).astype(BF16)
+        x_pre = pre[:, bc_width + at : bc_width + at + width]
+        fed = (x_pre * sigmoid(x_pre) * step_x[:, cols]).astype(BF16)
+        mix_low = grad_mix[:, cols]
         masks = half_masks(width)
         for start in range(0, length, LANES):
             stop = start + LANES
@@ -255,83 +259,59 @@
                 grad_mixing = mm_nt(jnp.where(mask, fed[start:stop], 0), mix_low[start:])
                 grad_pair[start:stop, start:] += grad_mixing * decayed
                 found = found + mm(mixing, jnp.where(mask, mix_low[start:], 0))
-            near[start:stop, :width] = found
-        grad_fed[0, :, cols] = near[:, :width]
-        rows_sum = rows_sum - pick(near[:, :width] * fed.astype(F32), gather[cols])
-    grad_cum[0] = rows_sum
+            grad_fed[start:stop, cols] = found
+        cols_sum = cols_sum + pick(grad_fed[:, cols] * fed.astype(F32), gather[cols])
+    grad_cum[...] -= cols_sum
     pair_low = grad_pair[...].astype(BF16)
-    grad_bc[0, :, :LANES] = mm(pair_low, readout)
-    grad_bc[0, :, LANES:] = mm_tn(pair_low, inputs_b) + mm_nt(from_state[...], state_in[0])
-    grad_state[0] = mm_tn(readout, from_state[...]).astype(BF16)
-    sum_z[...] += mm_tn(normed[0, HALO:], grad_gate[0])
-    sum_o[...] += mm_tn(out_grad[0], gated_low[...])
-
-    @pl.when(is_last_step())
-    def _():
-        grad_wz[...] = sum_z[...].astype(BF16)
-        grad_wo[...] = sum_o[...].astype(BF16)
-
-
-def backward_finish(grad_later, state_in, pre, raw, dt_raw, cum, age, grad_fed, grad_mix, grad_cum, grad_bc, grad_gate,
-                    normed, hid, halo, w_in, w_z, taps, skip, norm_in, heads, spread, gather, tri_up,
-                    grad_normed, grad_halo, grad_w, conv_sums, head_sums, norm_sums,
-                    sum_w, step_x, open_x, from_state, fed_state, slope, age_long, grad_in, wide):
-    length, inner = grad_fed.shape[1:]
+    grad_bc[:, :LANES] = mm(pair_low, readout)
+    grad_bc[:, LANES:] += mm_tn(pair_low, inputs_b)
+
+
+def state_back(grad_later, state_in, pre, raw, dt_raw, cum, age, grad_fed, grad_mix, grad_cum, grad_bc, taps, skip,
+               heads, spread, gather, tri_up, grad_in, conv_sums, head_sums,
+               step_x, open_x, from_state, fed_state, slope, age_long):
+    length, inner = grad_fed.shape
     channels = taps.shape[1]
     bc_width = 2 * LANES
     lead = HALO + length
-
-    @pl.when(is_first_step())
-    def _():
-        sum_w[...] = jnp.zeros_like(sum_w)
-        conv_sums[...] = jnp.zeros_like(conv_sums)
-        head_sums[...] = jnp.zeros_like(head_sums)
-        norm_sums[...] = jnp.zeros_like(norm_sums)
-        slope[:HALO] = jnp.zeros((HALO, channels), F32)
-        slope[lead:] = jnp.zeros((8, channels), F32)
-        age_long[:HALO] = jnp.zeros((HALO, LANES), F32)
-        age_long[lead:] = jnp.zeros((8, LANES), F32)
-        grad_in[:HALO, bc_width : bc_width + LANES] = jnp.zeros((HALO, LANES), BF16)
-
-    age_long[HALO:lead] = age[0]
-    total = cum[0]
-    step_raw = dt_raw[0] + heads[0:1]
+    grad_in[:HALO, bc_width : bc_width + LANES] = jnp.zeros((HALO, LANES), BF16)
+    age_long[HALO:lead] = age[...]
+    total = cum[...]
+    step_raw = dt_raw[...] + heads[0:1]
     step = softplus(step_raw)
     rate = -jnp.exp(heads[1:2])
     step_x[...] = pick(step, spread[...])
-    last, age_last = total[length - 1 :], age[0, length - 1 :]
+    last, age_last = total[length - 1 :], age[length - 1 :]
     open_end = row_index(length) - (length - 1) + age_last >= 0
     open_x[...] = pick(jnp.where(open_end, jnp.exp(last - total), 0.0), spread[...])
-    b_pre = pre[0, :, :LANES]
-    inputs_b = (b_pre * sigmoid(b_pre)).astype(BF16)
-    from_state[...] = open_x[...] * mm(inputs_b, grad_later[0])
+    from_state[...] = open_x[...] * mm(activated(pre.at[:, :LANES]), grad_later[...])
     state_sum = jnp.zeros((length, LANES), F32)
     step_sum = jnp.zeros((length, LANES), F32)
     for at, width in column_blocks(inner):
         cols = slice(at, at + width)
-        x_pre = pre[0, :, bc_width + at : bc_width + at + width]
+        x_pre = pre[:, bc_width + at : bc_width + at + width]
         logistic = sigmoid(x_pre)
         values = x_pre * logistic
         fed = values * step_x[:, cols]
         fed_state[:, cols] = (fed * open_x[:, cols]).astype(BF16)
         arrived = from_state[:, cols]
-        grad = grad_fed[0, :, cols] + arrived
+        grad = grad_fed[:, cols] + arrived
         state_sum = state_sum + pick(fed * arrived, gather[cols])
         step_sum = step_sum + pick(values * grad, gather[cols])
-        grad_values = grad * step_x[:, cols] + skip[:, cols] * grad_mix[0, :, cols].astype(F32)
+        grad_values = grad * step_x[:, cols] + skip[:, cols] * grad_mix[:, cols].astype(F32)
         slope[HALO:lead, bc_width + at : bc_width + at + width] = grad_values * (
             logistic * (1.0 + x_pre * (1.0 - logistic))
         )
-    for at, extra in ((0, mm_nt(fed_state[...], grad_later[0])), (LANES, 0.0)):
+    for at, extra in ((0, mm_nt(fed_state[...], grad_later[...])), (LANES, 0.0)):
         cols = slice(at, at + LANES)
-        bc_pre = pre[0, :, cols]
+        bc_pre = pre[:, cols]
         logistic = sigmoid(bc_pre)
-        slope[HALO:lead, cols] = (grad_bc[0, :, cols] + extra) * (logistic * (1.0 + bc_pre * (1.0 - logistic)))
+        slope[HALO:lead, cols] = (grad_bc[:, cols] + extra) * (logistic * (1.0 + bc_pre * (1.0 - logistic)))
     kept = jnp.where(age_last > length - 1, jnp.exp(last), 0.0)
-    met = jnp.sum(grad_later[0].astype(F32) * state_in[0].astype(F32), 0, keepdims=True)
+    met = jnp.sum(grad_later[...].astype(F32) * state_in[...].astype(F32), 0, keepdims=True)
     met = pick(jnp.broadcast_to(met, (8, inner)), gather[...], 3)[:1]
     end = met * kept + jnp.sum(state_sum, 0, keepdims=True)
-    grad_a = pick_left(tri_up[...], grad_cum[0] - state_sum) + end
+    grad_a = pick_left(tri_up[...], grad_cum[...] - state_sum) + end
     head_sums[1:2] += jnp.sum(grad_a * rate * step, 0, keepdims=True)
     grad_step = (step_sum + grad_a * rate) * sigmoid(step_raw)
     head_sums[0:1] += jnp.sum(grad_step, 0, keepdims=True)
@@ -341,27 +321,76 @@
         shifted = at if at < bc_width else at + LANES
         own = slope[HALO:lead, cols]
         total_in = taps[0:1, cols] * slope[:lead, cols]
-        conv_sums[0:1, cols] += jnp.sum(own * raw[0, HALO:, cols], 0, keepdims=True)
+        conv_sums[0:1, cols] += jnp.sum(own * raw[HALO:, cols], 0, keepdims=True)
         for lag in range(1, 4):
-            kept_lag = jnp.where(age[0, :, :width] >= lag, own, 0.0)
-            conv_sums[lag : lag + 1, cols] += jnp.sum(
-                kept_lag * raw[0, HALO - lag : lead - lag, cols], 0, keepdims=True
-            )
+            kept_lag = jnp.where(age[:, :width] >= lag, own, 0.0)
+            conv_sums[lag : lag + 1, cols] += jnp.sum(kept_lag * raw[HALO - lag : lead - lag, cols], 0, keepdims=True)
             later = jnp.where(age_long[lag : lead + lag, :width] >= lag, slope[lag : lead + lag, cols], 0.0)
             total_in = total_in + taps[lag : lag + 1, cols] * later
         conv_sums[4:5, cols] += jnp.sum(own, 0, keepdims=True)
         grad_in[:, shifted : shifted + width] = total_in.astype(BF16)
+
+
+def clear_margins(slope, age_long, length):
+    slope[:HALO] = jnp.zeros((HALO, slope.shape[1]), F32)
+    slope[HALO + length :] = jnp.zeros((8, slope.shape[1]), F32)
+    age_long[:HALO] = jnp.zeros((HALO, LANES), F32)
+    age_long[HALO + length :] = jnp.zeros((8, LANES), F32)
+
+
+def features_back(grad_in, grad_gate, hid, halo, w_in, w_z, grad_normed, grad_halo, norm_sums, wide):
+    length = hid.shape[0]
     wide[...] = mm_nt(grad_in[...], w_in[...])
-    wide[HALO:] += mm_nt(grad_gate[0], w_z[...])
-    hidden = halo[0].astype(F32)
+    wide[HALO:] += mm_nt(grad_gate[...], w_z[...])
+    hidden = halo[...].astype(F32)
     scale = normalised(hidden, 1.0)[1]
     norm_sums[0:1] += jnp.sum(wide[:HALO] * hidden * scale, 0, keepdims=True)
     for at in range(0, length, 64):
-        hidden = hid[0, at : at + 64].astype(F32)
+        hidden = hid[at : at + 64].astype(F32)
         scale = normalised(hidden, 1.0)[1]
         norm_sums[0:1] += jnp.sum(wide[HALO + at : HALO + at + 64] * hidden * scale, 0, keepdims=True)
-    grad_halo[0] = wide[:HALO].astype(BF16)
-    grad_normed[0] = wide[HALO:].astype(BF16)
+    grad_halo[...] = wide[:HALO].astype(BF16)
+    grad_normed[...] = wide[HALO:].astype(BF16)
+
+
+def backward_local(inner_all, mixer, gate, grad_gn, stats, pre, dt_raw, cum, age, age_row, state_in, normed, out_grad,
+                   norm_gate, skip, heads, spread, gather,
+                   grad_fed, grad_mix, grad_gate, grad_cum, grad_bc, grad_state, grad_wz, grad_wo, sums,
+                   sum_z, sum_o, seg, pair, grad_pair, carried, step_x, gated_low, from_state):
+    @pl.when(is_first_step())
+    def _():
+        sum_z[...] = jnp.zeros_like(sum_z)
+        sum_o[...] = jnp.zeros_like(sum_o)
+        sums[...] = jnp.zeros_like(sums)
+
+    gate_back(inner_all, mixer.at[0], gate.at[0], grad_gn.at[0], stats.at[0], pre.at[0], cum.at[0], age.at[0],
+              state_in.at[0], normed.at[0], out_grad.at[0], norm_gate, skip, spread, gather, grad_mix.at[0],
+              grad_gate.at[0], grad_cum.at[0], grad_bc.at[0, :, LANES:], grad_state.at[0], sums, sum_z, sum_o,
+              carried, gated_low, from_state)
+    within_back(pre.at[0], dt_raw.at[0], cum.at[0], age_row.at[0], grad_mix.at[0], heads, spread, gather,
+                grad_fed.at[0], grad_cum.at[0], grad_bc.at[0], seg, pair, grad_pair, step_x)
+
+    @pl.when(is_last_step())
+    def _():
+        grad_wz[...] = sum_z[...].astype(BF16)
+        grad_wo[...] = sum_o[...].astype(BF16)
+
+
+def backward_finish(grad_later, state_in, pre, raw, dt_raw, cum, age, grad_fed, grad_mix, grad_cum, grad_bc, grad_gate,
+                    normed, hid, halo, w_in, w_z, taps, skip, heads, spread, gather, tri_up,
+                    grad_normed, grad_halo, grad_w, conv_sums, head_sums, norm_sums,
+                    sum_w, step_x, open_x, from_state, fed_state, slope, age_long, grad_in, wide):
+    @pl.when(is_first_step())
+    def _():
+        for sums in (sum_w, conv_sums, head_sums, norm_sums):
+            sums[...] = jnp.zeros_like(sums)
+        clear_margins(slope, age_long, hid.shape[1])
+
+    state_back(grad_later.at[0], state_in.at[0], pre.at[0], raw.at[0], dt_raw.at[0], cum.at[0], age.at[0],
+               grad_fed.at[0], grad_mix.at[0], grad_cum.at[0], grad_bc.at[0], taps, skip, heads, spread, gather, tri_up,
+               grad_in, conv_sums, head_sums, step_x, open_x, from_state, fed_state, slope, age_long)
+    features_back(grad_in, grad_gate.at[0], hid.at[0], halo.at[0], w_in, w_z, grad_normed.at[0], grad_halo.at[0],
+                  norm_sums, wide)
     sum_w[...] += mm_tn(normed[0], grad_in[...])
 
     @pl.when(is_last_step())
@@ -588,82 +617,69 @@
 
 
 def scatter_scratch(rows, width):
-    block = pltpu.VMEM((4, rows, width), BF16)
-    return [block, block, block, block, block, block, block, block, pltpu.VMEM((4, rows, width), F32),
-            pltpu.SemaphoreType.DMA((5, 4))]
-
-
-SCATTER_COPIES = 20
-
-
-def scatter_blocks(copies, place, blocks, out, first, from_x, from_y, from_up, from_down, to_first, to_up, to_down,
-                   column, received):
-    shard, context, _ = place
+    return [pltpu.VMEM((4, rows, width), BF16) for _ in range(5)] + [DMA((5, 4)), DMA((SCATTER_COPIES,))]
+
+
+SCATTER_COPIES = 18
+
+
+def scatter_steps():
+    return 1 + lax.axis_size("context") // 2 + lax.axis_size("context")
+
+
+def scatter_step(step, start, arrived, blocks, out, first, from_x, from_y, from_up, from_down, received, add=True):
+    shard, context, _ = coordinates()
     count = lax.axis_size("context")
-    up, down, next_x, next_y = neighbours(place)
+    half = count // 2
+    up, down, next_x, next_y = neighbours(coordinates())
     mine, beside_x, beside_y, across = [(shard ^ k) * count for k in (0, 1, 2, 3)]
-    low, high = range(count // 2), range(count // 2, count)
-    for at in range(count // 2):
-        for k, to in ((at, next_y), (at + count // 2, next_x)):
-            copies.start(blocks.at[across + k], first.at[k], received.at[0, k], to[1])
-    for k in reversed(high):
-        copies.start(blocks.at[beside_x + k], from_x.at[k], received.at[1, k], next_x[1])
-    for k in low:
-        copies.start(blocks.at[beside_y + k], from_y.at[k], received.at[2, k], next_y[1])
-    yield
-    for at in range(count // 2):
-        for k, beside, buffers, row, to in ((at, beside_x, from_x, 1, next_x), (count - 1 - at, beside_y, from_y, 2, next_y)):
-            copies.arrived(first.at[k], received.at[0, k])
-            to_first[k] = (blocks[beside + k].astype(F32) + first[k].astype(F32)).astype(BF16)
-            copies.start(to_first.at[k], buffers.at[k], received.at[row, k], to[1])
-        yield
-    for at in range(count):
-        k = count - 1 - at // 2 if at % 2 == 0 else at // 2
-        copies.arrived(from_x.at[k], received.at[1, k])
-        copies.arrived(from_y.at[k], received.at[2, k])
-        column[k] = blocks[mine + k].astype(F32) + from_x[k].astype(F32) + from_y[k].astype(F32)
-        yield
-    for at in range(count - 1):
-        k = count - 1 - at
-
-        @pl.when(context < k)
-        def _(k=k):
-            @pl.when(context > 0)
+    if step == 0:
+        for k in range(count):
+            start(k, blocks.at[across + k], first.at[k], received.at[0, k], (next_y if k < half else next_x)[1], True)
+        for k in range(count):
+            beside, target, row, to = (beside_y, from_y, 2, next_y) if k < half else (beside_x, from_x, 1, next_x)
+            start(count + k, blocks.at[beside + k], target.at[k], received.at[row, k], to[1], True)
+    elif step <= half:
+        for k in (step - 1, count - step):
+            beside, target, row, to = (beside_x, from_x, 1, next_x) if k < half else (beside_y, from_y, 2, next_y)
+            arrived(first.at[k], received.at[0, k], True)
+            if add:
+                blocks[beside + k] = (blocks[beside + k].astype(F32) + first[k].astype(F32)).astype(BF16)
+            start(2 * count + k, blocks.at[beside + k], target.at[k], received.at[row, k], to[1], True)
+    else:
+        at = step - half - 1
+
+        def column(k, extra, row, there):
+            arrived(from_x.at[k], received.at[1, k], True)
+            arrived(from_y.at[k], received.at[2, k], True)
+            found = blocks[mine + k].astype(F32) + from_x[k].astype(F32) + from_y[k].astype(F32)
+            out[...] = found
+
+            @pl.when(there)
             def _():
-                copies.arrived(from_down.at[k], received.at[3, k])
-                to_up[k] = (column[k] + from_down[k].astype(F32)).astype(BF16)
-
-            @pl.when(context == 0)
-            def _():
-                to_up[k] = column[k].astype(BF16)
-
-        copies.start(to_up.at[k], from_down.at[k], received.at[3, k], up[1], context < k)
-        k = at
-
-        @pl.when(context > k)
-        def _(k=k):
+                arrived(extra.at[k], received.at[row, k], True)
+                out[...] += extra[k].astype(F32)
+
+        if at < count - 1:
+            for k, sends, receives, to, row, extra, number in (
+                (count - 1 - at, context < count - 1 - at, context > 0, up, 3, from_down, 0),
+                (at, context > at, context < count - 1, down, 4, from_up, 1),
+            ):
+                if add:
+
+                    @pl.when(sends)
+                    def _(k=k, receives=receives, row=row, extra=extra):
+                        column(k, extra, row, receives)
+                        blocks[mine + k] = out[...].astype(BF16)
+
+                start(3 * count + 2 * at + number, blocks.at[mine + k], extra.at[k], received.at[row, k], to[1], sends)
+        else:
+            column(context, from_down, 3, context > 0)
+
             @pl.when(context < count - 1)
             def _():
-                copies.arrived(from_up.at[k], received.at[4, k])
-                to_down[k] = (column[k] + from_up[k].astype(F32)).astype(BF16)
-
-            @pl.when(context == count - 1)
-            def _():
-                to_down[k] = column[k].astype(BF16)
-
-        copies.start(to_down.at[k], from_up.at[k], received.at[4, k], down[1], context > k)
-        yield
-    out[...] = column[context]
-
-    @pl.when(context > 0)
-    def _():
-        copies.arrived(from_down.at[context], received.at[3, context])
-        out[...] += from_down[context].astype(F32)
-
-    @pl.when(context < count - 1)
-    def _():
-        copies.arrived(from_up.at[context], received.at[4, context])
-        out[...] += from_up[context].astype(F32)
+                arrived(from_up.at[context], received.at[4, context], True)
+                out[...] += from_up[context].astype(F32)
 
 
 def gather_inputs(w_bc, w_dt, w_x, conv_bc, conv_x, hid, out, halo, taps, stage, passing, send, received, others, own):
@@ -709,51 +725,6 @@
     copies.finish()
 
 
-def chain_states(copies, place, local, decay, arrived, leaving, received, by):
-    _, context, _ = place
-    count = lax.axis_size("context")
-    first = context == (0 if by > 0 else count - 1)
-    last = context == (count - 1 if by > 0 else 0)
-    to = {"context": context + by}
-    pieces = local.shape[0]
-
-    def sent(i):
-        return pltpu.make_async_remote_copy(
-            src_ref=leaving.at[i], dst_ref=arrived.at[i], send_sem=received.at[1, i], recv_sem=received.at[0, i],
-            device_id=to, device_id_type=MESH,
-        )
-
-    for i in range(pieces):
-
-        @pl.when(first)
-        def _(i=i):
-            arrived[i] = jnp.zeros_like(arrived[i])
-            leaving[i] = local[i]
-
-        @pl.when(jnp.logical_not(first))
-        def _(i=i):
-            copies.arrived(arrived.at[i], received.at[0, i])
-
-        @pl.when(jnp.logical_not(first | last))
-        def _(i=i):
-            leaving[i] = (decay[i, :1] * arrived[i].astype(F32) + local[i].astype(F32)).astype(BF16)
-
-        pl.when(jnp.logical_not(last))(sent(i).start)
-        yield
-    for i in range(pieces):
-        pl.when(jnp.logical_not(last))(sent(i).wait_send)
-
-
-def in_turn(*steps):
-    steps = list(steps)
-    while steps:
-        for one in list(steps):
-            try:
-                next(one)
-            except StopIteration:
-                steps.remove(one)
-
-
 GATHER_TURNS = (0, 1, 2, 3, 3, 4, 5, 6, 7)
 
 
@@ -859,103 +830,242 @@
             passed(i).wait_send()
 
 
-def add_over_cores(own, out, other, send, received):
-    _, _, tensor = coordinates()
-    partner = {"tensor": 1 - tensor}
-    greet([(True, partner)])
-    copies = Copies(send)
-    copies.start(own, other, received.at[0], partner)
-    copies.arrived(other, received.at[0])
-    out[...] = own[...] + other[...]
-    copies.finish()
-
-
-def states_down(local, decay, grad_wz, grad_wo, part, arrived, out, other_part, stage, leaving, send, others, states,
-                *buffers):
-    place = _, _, tensor = coordinates()
-    inner = grad_wz.shape[2]
-    stage[:, :, :inner] = grad_wz[...]
-    stage[:, :, inner:] = grad_wo[...]
-    partner = {"tensor": 1 - tensor}
-    greet(neighbours(place) + [(True, partner)])
-    copies = Copies(send)
-    copies.start(part, other_part.at[0], others.at[0], partner)
-    in_turn(
-        scatter_blocks(copies, place, stage, out, *buffers),
-        chain_states(copies, place, local, decay, arrived, leaving, states, -1),
-    )
-    copies.arrived(other_part.at[0], others.at[0])
-    copies.finish()
-
-
-def last_sums(grad_w, grad_normed, grad_halo, conv_sums, norm_sums, head_sums, inner_sums,
-              out, other_grad, own_tail, other_tail, conv_out, norm_out, head_out, inner_out,
-              stage, half, small, seen, tails, send, others, *buffers):
-    place = shard, context, tensor = coordinates()
+OUTER_TURNS = (7, 9, 10, 12, 14, 16, 18)
+
+
+def backward(inner_all, mixer, gate, grad_gn, pre, dt_raw, cum, age, age_row, state_in, normed, out_grad, raw, hid, halo,
+             stats, decay, norm_gate, skip, heads, spread, gather, tri_up, taps, w_in, w_z, part,
+             stats_out, sums_zo, sums_w, conv_out, norm_out, head_out, inner_out, other_part, own_grad, other_grad,
+             own_tail, other_tail,
+             grad_mix, grad_gate, grad_cum, grad_bc, grad_fed, sum_all, grad_in, stage, half_out, half_in,
+             leaving, arrived, carried, step_x, low_a, low_b, slope, age_long, wide, seg, pair, grad_pair, tails, blank,
+             stats_in, small, seen, conv_sums, head_sums, norm_sums, inner_sums,
+             send, got, grad_send, grad_got, states, stores, *buffers):
+    outer, last_ones = buffers[:7], buffers[7:]
+    shard, context, tensor = coordinates()
+    phase, i = pl.program_id(0), pl.program_id(1)
+    pieces = pl.num_programs(1)
     count = lax.axis_size("context")
+    model, inner = sum_all.shape[0], grad_mix.shape[2]
+    in_width, channels = w_in.shape[1], taps.shape[1]
+    length = grad_mix.shape[1]
     bc_width = 2 * LANES
     own_bc = bc_width // 2
-    inner, model = inner_sums.shape[1], norm_sums.shape[1]
     partner = {"tensor": 1 - tensor}
-    around = neighbours(place)
+    below, above = context > 0, context < count - 1
+    below_partner = {"context": context - 1, "tensor": 1 - tensor}
+    turn = phase * pieces + i
+    misc = Numbered(send)
+    rows = stage.shape[1]
     cols = pl.ds(pl.multiple_of(tensor * own_bc, LANES), own_bc)
     other_cols = pl.ds(pl.multiple_of((1 - tensor) * own_bc, LANES), own_bc)
-    small[0, :5] = conv_sums[:5]
-    small[0, 5:6, :model] = norm_sums[:1]
-    small[0, 5:6, model : model + LANES] = head_sums[:1]
-    small[0, 5:6, model + LANES :] = head_sums[1:2]
-    small[0, 6:8, :inner] = inner_sums[:2]
-    small[0, 6:8, inner:] = jnp.zeros((2, small.shape[2] - inner), F32)
-    below, above = (around[DOWN][0], around[UP][0])
-    greet(around + [(True, partner), (True, {"context": context ^ 2}),
-                    (above, {"context": context + 1, "tensor": 1 - tensor}),
-                    (below, {"context": context - 1, "tensor": 1 - tensor})])
-    copies = Copies(send)
-    copies.start(small.at[0], seen.at[0], others.at[4], partner)
-    copies.start(grad_w.at[:, :, other_cols], half, others.at[0], partner)
-    copies.start(grad_normed, other_grad.at[0], others.at[1], partner)
-    copies.start(grad_halo, own_tail, others.at[2], around[DOWN][1], below)
-    copies.start(grad_halo, other_tail.at[0], others.at[3], {"context": context - 1, "tensor": 1 - tensor}, below)
-    stage[:, :, own_bc:] = grad_w[:, :, bc_width:]
-    copies.arrived(half, others.at[0])
-    mixed = grad_w[:, :, cols].astype(F32) + half[...].astype(F32)
-    stage[:, :, :own_bc] = mixed.astype(BF16)
-    row = lax.broadcasted_iota(jnp.int32, small.shape[1:], 0)
-    lane = lax.broadcasted_iota(jnp.int32, small.shape[1:], 1)
-    shared = ((row < 5) & (lane < bc_width)) | ((row == 5) & (lane < model))
-    copies.arrived(seen.at[0], others.at[4])
-    small[1] = small[0] + jnp.where(shared, seen[0], 0.0)
-    copies.start(small.at[1], seen.at[1], others.at[5], {"shard": shard ^ 1})
-    for _ in scatter_blocks(copies, place, stage, out, *buffers):
-        pass
-    for step, device in ((1, {"shard": shard ^ 1}), (2, {"shard": shard ^ 2}), (3, {"context": context ^ 1}),
-                         (4, {"context": context ^ 2})):
-        if step > 1:
-            copies.start(small.at[step], seen.at[step], others.at[4 + step], device)
-        copies.arrived(seen.at[step], others.at[4 + step])
-        small[step + 1] = small[step] + seen[step]
-    total = small.at[5]
-    conv_out[:, :own_bc] = total[:, cols]
-    conv_out[:, own_bc:] = total[:, bc_width:]
-    norm_out[...] = jnp.broadcast_to(total[5:6, :model], norm_out.shape)
-    head_out[...] = jnp.zeros_like(head_out)
-    head_out[0:1] = total[5:6, model : model + LANES]
-    head_out[1:2] = total[5:6, model + LANES : model + 2 * LANES]
-    inner_out[...] = jnp.zeros_like(inner_out)
-    inner_out[0:2] = total[6:8, :inner]
-    copies.arrived(other_grad.at[0], others.at[1])
-    copies.arrived(own_tail, others.at[2], above)
-    copies.arrived(other_tail.at[0], others.at[3], above)
-
-    @pl.when(jnp.logical_not(above))
-    def _():
-        tails[...] = jnp.zeros_like(tails)
-        for target, k in ((own_tail, 2), (other_tail.at[0], 3)):
-            clear = pltpu.make_async_copy(tails, target, others.at[k])
-            clear.start()
-            clear.wait()
-
-    copies.finish()
+
+    def link(number, source, target, device):
+        return misc.copy(number, source, target, got.at[number], device)
+
+    def stats_link():
+        return link(0, stats, stats_in, partner)
+
+    def part_link():
+        return link(1, part, other_part.at[0], partner)
+
+    def half_link():
+        return link(2, half_out, half_in, partner)
+
+    def tail_links():
+        return [link(3, tails, own_tail, {"context": context - 1}), link(4, tails, other_tail.at[0], below_partner)]
+
+    def small_link(k):
+        to = [partner, {"shard": shard ^ 1}, {"shard": shard ^ 2}, {"context": context ^ 1}, {"context": context ^ 2}]
+        return link(5 + k, small.at[k], seen.at[k], to[k])
+
+    def grad_link(k):
+        return pltpu.make_async_remote_copy(
+            src_ref=grad_gate.at[k], dst_ref=other_grad.at[0, k], send_sem=grad_send.at[k], recv_sem=grad_got.at[k],
+            device_id=partner, device_id_type=MESH,
+        )
+
+    def grad_store(k):
+        return pltpu.make_async_copy(grad_gate.at[k], own_grad.at[k], stores.at[k])
+
+    def passed(c):
+        return pltpu.make_async_remote_copy(
+            src_ref=leaving.at[c], dst_ref=arrived.at[c], send_sem=states.at[1, c], recv_sem=states.at[0, c],
+            device_id={"context": context - 1}, device_id_type=MESH,
+        )
+
+    first, last = context == count - 1, context == 0
+    hops = count - 1 - context
+
+    @pl.when(turn == 0)
+    def _():
+        for sums in (sum_all, conv_sums, head_sums, norm_sums, inner_sums):
+            sums[...] = jnp.zeros_like(sums)
+        clear_margins(slope, age_long, length)
+        greet(neighbours(coordinates()) + [(True, partner), (True, {"context": context ^ 2}),
+              (above, {"context": context + 1, "tensor": 1 - tensor}), (below, below_partner)])
+        stats_link().start()
+        part_link().start()
+        stats_link().wait_recv()
+        stats_out[...] = stats[...] + stats_in[...]
+
+    c = jnp.clip(turn // 2 - hops, 0, pieces - 1)
+
+    @pl.when((turn % 2 == 0) & (turn // 2 >= hops) & (turn // 2 - hops < pieces) & jnp.logical_not(first | last))
+    def _():
+        passed(c).wait_recv()
+        leaving[c] = (decay[c, :1] * arrived[c].astype(F32) + leaving[c].astype(F32)).astype(BF16)
+        passed(c).start()
+
+    @pl.when(phase == 0)
+    def _():
+        gate_back(inner_all, mixer.at[0], gate.at[0], grad_gn.at[0], stats_out.at[i], pre.at[0], cum.at[0], age.at[0],
+                  state_in.at[0], normed.at[0], out_grad.at[0], norm_gate, skip, spread, gather, grad_mix.at[i],
+                  grad_gate.at[i], grad_cum.at[i], grad_bc.at[i, :, LANES:], leaving.at[i], inner_sums,
+                  sum_all.at[:, :inner], sum_all.at[:, inner:], carried, low_a, low_b)
+
+        @pl.when(first)
+        def _():
+            arrived[i] = jnp.zeros(arrived.shape[1:], BF16)
+            passed(i).start()
+
+    @pl.when(turn == pieces - 1)
+    def _():
+        stage[...] = sum_all[...].reshape(stage.shape).astype(BF16)
+
+    outer_links = Numbered(outer[6])
+    for step in range(scatter_steps()):
+
+        @pl.when(turn == OUTER_TURNS[step])
+        def _(step=step):
+            scatter_step(step, outer_links.start, outer_links.arrived, stage, sums_zo, *outer[:6])
+
+    @pl.when(turn == OUTER_TURNS[-1] + 1)
+    def _():
+        for step in range(scatter_steps() - 1):
+            scatter_step(step, outer_links.sent, outer_links.nothing, stage, sums_zo, *outer[:6], add=False)
+
+    @pl.when(phase == 1)
+    def _():
+        within_back(pre.at[0], dt_raw.at[0], cum.at[0], age_row.at[0], grad_mix.at[i], heads, spread, gather,
+                    grad_fed.at[i], grad_cum.at[i], grad_bc.at[i], seg, pair, grad_pair, step_x)
+
+    @pl.when(phase == 2)
+    def _():
+        @pl.when(i == 0)
+        def _():
+            sum_all[...] = jnp.zeros_like(sum_all)
+
+        @pl.when(last)
+        def _():
+            passed(i).wait_recv()
+
+        state_back(arrived.at[i], state_in.at[0], pre.at[0], raw.at[0], dt_raw.at[0], cum.at[0], age.at[0],
+                   grad_fed.at[i], grad_mix.at[i], grad_cum.at[i], grad_bc.at[i], taps, skip, heads, spread, gather,
+                   tri_up, grad_in.at[i], conv_sums, head_sums, step_x, carried, wide.at[HALO:], low_a, slope,
+                   age_long)
+        sum_all[:, :in_width] += mm_tn(normed[0], grad_in[i])
+
+        @pl.when(jnp.logical_not(last))
+        def _():
+            passed(i).wait_send()
+
+    last_stage = stage.at[:, :, : in_width - own_bc]
+
+    @pl.when(turn == 3 * pieces - 1)
+    def _():
+        half_out[...] = sum_all[:, other_cols].reshape(half_out.shape).astype(BF16)
+        half_link().start()
+        stage[:, :, own_bc : in_width - own_bc] = (
+            sum_all[:, bc_width:in_width].reshape(16, rows, in_width - bc_width).astype(BF16)
+        )
+
+    @pl.when(phase == 3)
+    def _():
+        features_back(grad_in.at[i], grad_gate.at[i], hid.at[0], halo.at[0], w_in, w_z, grad_gate.at[i], tails.at[i],
+                      norm_sums, wide)
+        grad_link(i).start()
+        grad_store(i).start()
+
+    last_links = Numbered(last_ones[6])
+
+    def last_step(step):
+        scatter_step(step, last_links.start, last_links.arrived, last_stage, sums_w, *last_ones[:6])
+
+    @pl.when(turn == 3 * pieces)
+    def _():
+        half_link().wait_recv()
+        own_half = sum_all[:, cols].reshape(half_in.shape) + half_in[...].astype(F32)
+        stage[:, :, :own_bc] = own_half.astype(BF16)
+        last_step(0)
+
+    @pl.when(turn == 3 * pieces + 4)
+    def _():
+        last_step(1)
+
+    @pl.when(turn == 3 * pieces + 5)
+    def _():
+        last_step(2)
+
+    @pl.when(turn == 4 * pieces - 1)
+    def _():
+        for link_down in tail_links():
+            pl.when(below)(link_down.start)
+        small[0, :5] = conv_sums[:5]
+        small[0, 5:6, :model] = norm_sums[:1]
+        small[0, 5:6, model : model + LANES] = head_sums[:1]
+        small[0, 5:6, model + LANES :] = head_sums[1:2]
+        small[0, 6:8, :inner] = inner_sums[:2]
+        small[0, 6:8, inner:] = jnp.zeros((2, channels - inner), F32)
+        row = lax.broadcasted_iota(jnp.int32, small.shape[1:], 0)
+        lane = lax.broadcasted_iota(jnp.int32, small.shape[1:], 1)
+        shared = ((row < 5) & (lane < bc_width)) | ((row == 5) & (lane < model))
+        small_link(0).start()
+        for k in range(5):
+            if k + 3 < scatter_steps():
+                last_step(k + 3)
+            small_link(k).wait_recv()
+            small[k + 1] = small[k] + (jnp.where(shared, seen[k], 0.0) if k == 0 else seen[k])
+            if k < 4:
+                small_link(k + 1).start()
+        total = small.at[5]
+        conv_out[:, :own_bc] = total[:, cols]
+        conv_out[:, own_bc:] = total[:, bc_width:]
+        norm_out[...] = jnp.broadcast_to(total[5:6, :model], norm_out.shape)
+        head_out[...] = jnp.zeros_like(head_out)
+        head_out[0:1] = total[5:6, model : model + LANES]
+        head_out[1:2] = total[5:6, model + LANES : model + 2 * LANES]
+        inner_out[...] = jnp.zeros_like(inner_out)
+        inner_out[0:2] = total[6:8, :inner]
+        for link_down in tail_links():
+            pl.when(above)(link_down.wait_recv)
+
+        @pl.when(jnp.logical_not(above))
+        def _():
+            blank[...] = jnp.zeros_like(blank)
+            for target, k in ((own_tail, 3), (other_tail.at[0], 4)):
+                clear = pltpu.make_async_copy(blank, target, got.at[k])
+                clear.start()
+                clear.wait()
+
+        part_link().wait_recv()
+        for k in range(pieces_of(grad_gate)):
+            grad_link(k).wait_recv()
+            grad_link(k).wait_send()
+            grad_store(k).wait()
+        stats_link().wait_send()
+        part_link().wait_send()
+        half_link().wait_send()
+        for link_down in tail_links():
+            pl.when(below)(link_down.wait_send)
+        for k in range(5):
+            small_link(k).wait_send()
+        for step in range(scatter_steps() - 1):
+            scatter_step(step, last_links.sent, last_links.nothing, last_stage, sums_w, *last_ones[:6], add=False)
+
+
+def pieces_of(array):
+    return array.shape[0]
 
 
 ANY = pl.BlockSpec(memory_space=pl.ANY)
@@ -1046,28 +1156,52 @@
         )
         return normed, raw, pre, dt_raw, cum, decay, state_in, mixer, gate, grad_gn, part, stats, (w_z_all, fixed)
 
-    def over_cores(self, stats):
-        return lax.psum(stats, "tensor")
-
-    def states_down(self, local, decay, grad_wz, grad_wo, part):
-        sums = jnp.concatenate([scatter_rows(grad_wz), scatter_rows(grad_wo)], 1)
-        return chain(local, decay, -1), sums, exchange(part)
-
-    def last_sums(self, grad_w, grad_normed, grad_halo, conv_sums, norm_sums, head_sums, inner_sums, own_bc):
+    def backward(self, inner_all, saved, stats, age_row, seed, hid, halo, age, own_bc, norm_gate, skip, heads, spread,
+                 gather, tri_up, taps, w_in):
+        normed, raw, pre, dt_raw, cum, decay, state_in, mixer, gate, grad_gn, part, _, w_z_all = saved
+        pieces, length, model = hid.shape
+        inner, channels, in_width, lead = mixer.shape[2], taps.shape[1], w_in.shape[1], HALO + length
+        token = functools.partial(shaped, F32, pieces, length)
+        token_low = functools.partial(shaped, BF16, pieces, length)
+        square, token_wide, token_narrow = ((length, length), F32), ((length, inner), F32), ((length, inner), BF16)
+        stats = lax.psum(stats, "tensor")
+        grad_fed, grad_mix, grad_gate, grad_cum, grad_bc, grad_state, grad_wz, grad_wo, sums = call(
+            functools.partial(backward_local, inner_all), pieces,
+            [(mixer, by_piece), (gate, by_piece), (grad_gn, by_piece), (stats, by_piece), (pre, by_piece),
+             (dt_raw, by_piece), (cum, by_piece), (age, by_piece), (age_row, by_piece), (state_in, by_piece),
+             (normed, by_piece), (seed, by_piece), (norm_gate, fixed), (skip, fixed), (heads, fixed), (spread, fixed),
+             (gather, fixed)],
+            [(token(inner), by_piece), (token_low(inner), by_piece), (token_low(inner), by_piece),
+             (token(LANES), by_piece), (token(2 * LANES), by_piece), (shaped(BF16, pieces, LANES, inner), by_piece),
+             (shaped(BF16, model, inner), fixed), (shaped(BF16, model, inner), fixed), (shaped(F32, 8, inner), fixed)],
+            [((model, inner), F32), ((model, inner), F32), square, square, square, token_wide, token_wide, token_narrow,
+             token_narrow], "backward_local",
+        )
+        grad_later = chain(grad_state, decay, -1)
+        grad_normed, grad_halo, grad_w, conv_sums, head_sums, norm_sums = call(
+            backward_finish, pieces,
+            [(grad_later, by_piece), (state_in, by_piece), (pre, by_piece), (raw, by_piece), (dt_raw, by_piece),
+             (cum, by_piece), (age, by_piece), (grad_fed, by_piece), (grad_mix, by_piece), (grad_cum, by_piece),
+             (grad_bc, by_piece), (grad_gate, by_piece), (normed, by_piece), (hid, by_piece), (halo, by_piece),
+             (w_in, fixed), w_z_all, (taps, fixed), (skip, fixed), (heads, fixed), (spread, fixed), (gather, fixed),
+             (tri_up, fixed)],
+            [(token_low(model), by_piece), (shaped(BF16, pieces, HALO, model), by_piece),
+             (shaped(BF16, model, in_width), fixed), (shaped(F32, 8, channels), fixed), (shaped(F32, 8, LANES), fixed),
+             (shaped(F32, 8, model), fixed)],
+            [((model, in_width), F32), token_wide, token_wide, token_wide, token_narrow,
+             ((lead + 8, channels), F32), ((lead + 8, LANES), F32), ((lead, in_width), BF16), ((lead, model), F32)],
+            "backward_finish",
+        )
+        sums_zo = jnp.concatenate([scatter_rows(grad_wz), scatter_rows(grad_wo)], 1)
         mine, bc_width = lax.axis_index("tensor"), 2 * LANES
         grad_w = scatter_rows(grad_w)
         grad_w_bc = lax.psum_scatter(grad_w[:, :bc_width], "tensor", scatter_dimension=1, tiled=True)
         norm_sums, conv_bc = lax.psum((norm_sums, conv_sums[:, :bc_width]), ("shard", "context", "tensor"))
-        conv_x, head_sums, inner_sums = lax.psum(
-            (conv_sums[:, bc_width:], head_sums, inner_sums), ("shard", "context")
-        )
+        conv_x, head_sums, sums = lax.psum((conv_sums[:, bc_width:], head_sums, sums), ("shard", "context"))
         conv_bc = lax.dynamic_slice_in_dim(conv_bc, mine * own_bc, own_bc, 1)
-        return (
-            jnp.concatenate([grad_w_bc, grad_w[:, bc_width:]], 1),
-            exchange(grad_normed),
-            exchange(passed_along(grad_halo, -1)),
-            (jnp.concatenate([conv_bc, conv_x], 1), norm_sums, head_sums, inner_sums),
-        )
+        sums_w = jnp.concatenate([grad_w_bc, grad_w[:, bc_width:]], 1)
+        small = (jnp.concatenate([conv_bc, conv_x], 1), norm_sums, head_sums, sums)
+        return stats, sums_zo, sums_w, small, exchange(part), exchange(grad_normed), exchange(passed_along(grad_halo, -1))
 
 
 class FourByFourByTwo:
@@ -1143,45 +1277,81 @@
         w_z_all = (both.reshape(model, 2 * inner), part_of(inner, 0))
         return normed, raw, pre, dt_raw, cum, decay, state_in, mixer, gate, grad_gn, part, stats, w_z_all
 
-    def over_cores(self, stats):
-        return call_between(
-            add_over_cores, 3, [(stats, IN_VMEM)], [(shaped(F32, *stats.shape), IN_VMEM)],
-            [pltpu.VMEM(stats.shape, F32), DMA((1,)), DMA((1,))],
-        )[0]
-
-    def states_down(self, local, decay, grad_wz, grad_wo, part):
-        model, inner = grad_wz.shape
-        rows = model // 16
-        pieces = local.shape[0]
-        arrived, sums, other = call_between(
-            states_down, 4,
-            [(local, IN_VMEM), (decay, IN_VMEM), (grad_wz.reshape(16, rows, inner), IN_VMEM),
-             (grad_wo.reshape(16, rows, inner), IN_VMEM), (part, ANY)],
-            [(shaped(BF16, *local.shape), IN_VMEM), (shaped(F32, rows, 2 * inner), IN_VMEM),
-             (shaped(BF16, 1, *part.shape), ANY)],
-            [pltpu.VMEM((16, rows, 2 * inner), BF16), pltpu.VMEM(local.shape, BF16), DMA((SCATTER_COPIES,)), DMA((1,)),
-             DMA((2, pieces))] + scatter_scratch(rows, 2 * inner),
-        )
-        return arrived, sums, (part, other)
-
-    def last_sums(self, grad_w, grad_normed, grad_halo, conv_sums, norm_sums, head_sums, inner_sums, own_bc):
-        model, in_width = grad_w.shape
+    def backward(self, inner_all, saved, stats, age_row, seed, hid, halo, age, own_bc, norm_gate, skip, heads, spread,
+                 gather, tri_up, taps, w_in):
+        normed, raw, pre, dt_raw, cum, decay, state_in, mixer, gate, grad_gn, part, _, (w_z, w_z_spec) = saved
+        pieces, length, model = hid.shape
+        inner, channels, in_width, lead = mixer.shape[2], taps.shape[1], w_in.shape[1], HALO + length
         rows = model // 16
         width = in_width - own_bc
-        channels = conv_sums.shape[1]
-        out, other_grad, own_tail, other_tail, *small = call_between(
-            last_sums, 5,
-            [(grad_w.reshape(16, rows, in_width), IN_VMEM), (grad_normed, ANY), (grad_halo, ANY),
-             (conv_sums, IN_VMEM), (norm_sums, IN_VMEM), (head_sums, IN_VMEM), (inner_sums, IN_VMEM)],
-            [(shaped(F32, rows, width), IN_VMEM), (shaped(BF16, 1, *grad_normed.shape), ANY),
-             (shaped(BF16, *grad_halo.shape), ANY), (shaped(BF16, 1, *grad_halo.shape), ANY),
-             (shaped(F32, 8, channels - own_bc), IN_VMEM), (shaped(F32, 8, model), IN_VMEM),
-             (shaped(F32, 8, LANES), IN_VMEM), (shaped(F32, *inner_sums.shape), IN_VMEM)],
-            [pltpu.VMEM((16, rows, width), BF16), pltpu.VMEM((16, rows, own_bc), BF16),
-             pltpu.VMEM((6, 8, channels), F32), pltpu.VMEM((5, 8, channels), F32), pltpu.VMEM(grad_halo.shape, BF16),
-             DMA((SCATTER_COPIES + 9,)), DMA((9,))] + scatter_scratch(rows, width),
-        )
-        return out, (grad_normed, other_grad), (own_tail, other_tail), small
+
+        def during(*phases):
+            def cut(array):
+                rest = array.shape[1:]
+
+                def where(p, i):
+                    at = jnp.where(p < phases[0], 0, pieces - 1)
+                    for phase in phases:
+                        at = jnp.where(p == phase, i, at)
+                    return (at,) + (0,) * len(rest)
+
+                return pl.BlockSpec((1,) + rest, where)
+
+            return cut
+
+        def once(array):
+            return pl.BlockSpec(array.shape, lambda p, i: (0,) * array.ndim, pipeline_mode=pl.Buffered(1))
+
+        def first_columns(array):
+            return pl.BlockSpec((array.shape[0], inner), lambda p, i: (0, 0), pipeline_mode=pl.Buffered(1))
+
+        def kept(array):
+            return pl.BlockSpec(array.shape, lambda p, i: (0,) * array.ndim)
+
+        def anywhere(array):
+            return ANY
+
+        def vmem(kind, *dims):
+            return pltpu.VMEM(dims, kind)
+
+        token_low = shaped(BF16, pieces, length, model)
+        tail = shaped(BF16, pieces, HALO, model)
+        inputs = [(mixer, during(0)), (gate, during(0)), (grad_gn, during(0)), (pre, during(0, 1, 2)),
+                  (dt_raw, during(1, 2)), (cum, during(0, 1, 2)), (age, during(0, 2)), (age_row, during(1)),
+                  (state_in, during(0, 2)), (normed, during(0, 2)), (seed, during(0)), (raw, during(2)), (hid, during(3)),
+                  (halo, during(3)), (stats, once), (decay, once), (norm_gate, once), (skip, once), (heads, once),
+                  (spread, once), (gather, once), (tri_up, once), (taps, once), (w_in, once), (w_z, first_columns),
+                  (part, anywhere)]
+        outputs = [(shaped(F32, *stats.shape), kept), (shaped(F32, rows, 2 * inner), kept), (shaped(F32, rows, width), kept),
+                   (shaped(F32, 8, channels - own_bc), kept), (shaped(F32, 8, model), kept), (shaped(F32, 8, LANES), kept),
+                   (shaped(F32, 8, inner), kept), (shaped(BF16, 1, *part.shape), anywhere), (token_low, anywhere),
+                   (shaped(BF16, 1, *token_low.shape), anywhere), (tail, anywhere),
+                   (shaped(BF16, 1, *tail.shape), anywhere)]
+        square = vmem(F32, length, length)
+        scratch = [
+            vmem(BF16, pieces, length, inner), vmem(BF16, pieces, length, inner), vmem(F32, pieces, length, LANES),
+            vmem(F32, pieces, length, 2 * LANES), vmem(F32, pieces, length, inner), vmem(F32, model, 2 * inner),
+            vmem(BF16, pieces, lead, in_width), vmem(BF16, 16, rows, 2 * inner), vmem(BF16, 16, rows, own_bc),
+            vmem(BF16, 16, rows, own_bc), vmem(BF16, *state_in.shape), vmem(BF16, *state_in.shape),
+            vmem(F32, length, inner), vmem(F32, length, inner), vmem(BF16, length, inner), vmem(BF16, length, inner),
+            vmem(F32, lead + 8, channels), vmem(F32, lead + 8, LANES), vmem(F32, lead, model), square, square, square,
+            vmem(BF16, *tail.shape), vmem(BF16, *tail.shape), vmem(F32, *stats.shape), vmem(F32, 6, 8, channels),
+            vmem(F32, 5, 8, channels), vmem(F32, 8, channels), vmem(F32, 8, LANES), vmem(F32, 8, model),
+            vmem(F32, 8, inner), DMA((10,)), DMA((10,)), DMA((pieces,)), DMA((pieces,)), DMA((2, pieces)), DMA((pieces,)),
+        ]
+        (stats, sums_zo, sums_w, conv_sums, norm_sums, head_sums, sums, other_part, own_grad, other_grad, own_tail,
+         other_tail) = pl.pallas_call(
+            functools.partial(backward, inner_all),
+            grid=(4, pieces),
+            in_specs=[cut(array) for array, cut in inputs],
+            out_specs=[cut(shape) for shape, cut in outputs],
+            out_shape=[shape for shape, _ in outputs],
+            scratch_shapes=scratch + scatter_scratch(rows, 2 * inner) + scatter_scratch(rows, width),
+            compiler_params=pltpu.CompilerParams(collective_id=3, has_side_effects=True, vmem_limit_bytes=VMEM_BYTES),
+            name="backward",
+        )(*[array for array, _ in inputs])
+        small = (conv_sums, norm_sums, head_sums, sums)
+        return stats, sums_zo, sums_w, small, (part, other_part), (own_grad, other_grad), (own_tail, other_tail)
 
 
 def links():
@@ -1224,49 +1394,15 @@
     token = functools.partial(shaped, F32, pieces, length)
     token_low = functools.partial(shaped, BF16, pieces, length)
     state = shaped(BF16, pieces, LANES, inner)
-    normed, raw, pre, dt_raw, cum, decay, state_in, mixer, gate, grad_gn, part, stats, w_z_all = between.forward(
+    saved = between.forward(
         hid, halo, age, seed, norm_in, w_in, w_z, w_out, taps, heads, spread, tri, norm_gate, skip
     )
-    square = ((length, length), F32)
-    token_wide = ((length, inner), F32)
-    token_narrow = ((length, inner), BF16)
-
-    stats = between.over_cores(stats)
-
-    grad_fed, grad_mix, grad_gate, grad_cum, grad_bc, grad_state, grad_wz, grad_wo, sums = call(
-        functools.partial(backward_local, inner_all), pieces,
-        [(mixer, by_piece), (gate, by_piece), (grad_gn, by_piece), (stats, by_piece), (pre, by_piece),
-         (dt_raw, by_piece), (cum, by_piece), (age, by_piece), (age_row, by_piece), (state_in, by_piece),
-         (normed, by_piece), (seed, by_piece), (norm_gate, fixed), (skip, fixed), (heads, fixed), (spread, fixed),
-         (gather, fixed)],
-        [(token(inner), by_piece), (token_low(inner), by_piece), (token_low(inner), by_piece), (token(LANES), by_piece),
-         (token(bc_width), by_piece), (state, by_piece), (shaped(BF16, model, inner), fixed),
-         (shaped(BF16, model, inner), fixed), (shaped(F32, 8, inner), fixed)],
-        [((model, inner), F32), ((model, inner), F32), ((length, LANES), F32), square, square, square, token_wide,
-         token_wide, token_narrow, token_narrow], "backward_local",
+    own_bc = w_bc.shape[1]
+    stats, sums_zo, sums_w, small, (own_part, other_part), (own_grad, other_grad), (own_tail, other_tail) = (
+        between.backward(inner_all, saved, saved[-2], age_row, seed, hid, halo, age, own_bc, norm_gate, skip, heads,
+                         spread, gather, tri_up, taps, w_in)
     )
-
-    grad_later, sums_zo, (own_part, other_part) = between.states_down(grad_state, decay, grad_wz, grad_wo, part)
-
-    grad_normed, grad_halo, grad_w, conv_sums, head_sums, norm_sums = call(
-        backward_finish, pieces,
-        [(grad_later, by_piece), (state_in, by_piece), (pre, by_piece), (raw, by_piece), (dt_raw, by_piece),
-         (cum, by_piece), (age, by_piece), (grad_fed, by_piece), (grad_mix, by_piece), (grad_cum, by_piece),
-         (grad_bc, by_piece), (grad_gate, by_piece), (normed, by_piece), (hid, by_piece), (halo, by_piece),
-         (w_in, fixed), w_z_all, (taps, fixed), (skip, fixed), (norm_in, fixed), (heads, fixed),
-         (spread, fixed), (gather, fixed), (tri_up, fixed)],
-        [(token_low(model), by_piece), (shaped(BF16, pieces, HALO, model), by_piece),
-         (shaped(BF16, model, in_width), fixed), (shaped(F32, 8, channels), fixed), (shaped(F32, 8, LANES), fixed),
-         (shaped(F32, 8, model), fixed)],
-        [((model, in_width), F32), token_wide, token_wide, token_wide, token_narrow,
-         ((lead + 8, channels), F32), ((lead + 8, LANES), F32), ((lead, in_width), BF16), ((lead, model), F32)],
-        "backward_finish",
-    )
-
-    own_bc = w_bc.shape[1]
-    sums_w, (own_grad, other_grad), (own_tail, other_tail), small = between.last_sums(
-        grad_w, grad_normed, grad_halo, conv_sums, norm_sums, head_sums, sums, own_bc
-    )
+    token_low = functools.partial(shaped, BF16, pieces, length)
     rows = w_z.shape[0]
     outputs = [shaped(F32, rows, inner), shaped(F32, rows, inner), shaped(F32, rows, own_bc),
                shaped(F32, rows, head_count), shaped(F32, inner, rows), shaped(F32, 5, inner), shaped(F32, 5, own_bc),

time: 342 us -> 271 us (0.79)
  Pallas kernels: 323 us -> 252 us
    pallas_call x0 -> x1, Pallas kernels: none -> 140 us  [backward(): pl.pallas_call(functools.partial(backward, inner_all), grid=(4, pieces),...]
    pallas_call x4 -> x1, Pallas kernels: 165 us -> 38.8 us  [call_between(): pl.pallas_call(kernel, in_specs=[spec for _, spec in inputs], out_specs=[...]
    pallas_call x3 -> x1, Pallas kernels: 98.1 us -> 13.6 us  [call(): pl.pallas_call(kernel, grid=(pieces,), in_specs=[cut(array) for array, cu...]
where the time goes in v4:
time: 271 us; the launch traced here: 270 us
  Pallas kernels  252 us (93%)
  local copies, waits for them, and re-layouts  13.7 us (5%)
  other arithmetic  3.25 us (1%)
    pallas_call x1, Pallas kernels, backward(): pl.pallas_call(functools.partial(backward, inner_all), grid=(4, pieces),...  140 us
    pallas_call x1, Pallas kernels, forward(): pl.pallas_call(forward, grid=(3, pieces), in_specs=[cut(array) for array,...  59.7 us
    pallas_call x1, Pallas kernels, call_between(): pl.pallas_call(kernel, in_specs=[spec for _, spec in inputs], out_specs=[...  38.8 us
    pallas_call x1, Pallas kernels, call(): pl.pallas_call(kernel, grid=(pieces,), in_specs=[cut(array) for array, cu...  13.6 us
    unnamed x4, local copies, waits for them, and re-layouts  6.29 us

profile of v4, /device:TPU:0, one launch (start us, length us, event | category | flops | bytes accessed | tf_op | source)
XLA Modules:
  0.0 269.9 jit_solution(3430335867866174016)
XLA Ops:
  0.7 0.1 pad.12.clone
  0.7 0.1 pad.11.clone
  0.8 0.7 pad_bitcast_fusion
  1.5 0.7 maximum_maximum_fusion.heads
  2.2 1.3 broadcast_in_dim.11.norm_in
  3.4 1.3 broadcast_in_dim.24.norm_gate
  4.7 0.7 reshape.90
  5.4 0.7 broadcast_in_dim.25
  6.1 0.7 broadcast_in_dim_reshape.3.skip
  6.8 1.4 copy.33.w_dt
  8.2 0.6 broadcast_in_dim.26.age_row
  8.8 1.7 copy.34.w_out
  10.5 1.3 broadcast_in_dim.10.age
  11.8 38.8 %gather_inputs.1 = (bf16[16,48,1152]{2,1,0:T(8,128)(2,1)}, bf16[8,16,768]{2,1,0:T(8,128)(2,1)}, f32[8,1024]{1,0:T(8,128)}) custom-call(bf16[48,128]{1,0:T(8,128)(2,1)} %w_bc.1, bf16[48,12]{1,0:T(8,128)(2,1)} %copy.33.w_dt, bf16[48,768]{1,0:T(8,128)(2,1)} %w_x.1, f32[5,128]{1,0:T(8,128)} %conv_bc.1, f32[5,768]{1,0:T(8,128)} %conv_x.1, ...), custom_call_target="tpu_custom_call" | custom-call | tf_op jit(solution)/shard_map/gather_inputs/pallas_call | solution.py:1077
  50.6 59.7 %forward.1 = (f32[8,272,1024]{2,1,0:T(8,128)}, f32[8,256,768]{2,1,0:T(8,128)}, bf16[8,256,768]{2,1,0:T(8,128)(2,1)}, f32[8,8,256]{2,1,0:T(8,128)}, bf16[8,272,76...) custom-call(bf16[8,256,768]{2,1,0:T(8,128)(2,1)} %bitcast.14, ...), custom_call_target="tpu_custom_call" | custom-call | tf_op jit(solution)/shard_map/forward/pallas_call | solution.py:1261
  110.3 140.2 %backward.1 = (f32[8,8,256]{2,1,0:T(8,128)}, f32[48,1536]{1,0:T(8,128)}, f32[48,1024]{1,0:T(8,128)}, f32[8,896]{1,0:T(8,128)}, f32[8,768]{1,0:T(8,128)}, /*index...) custom-call(f32[8,256,768]{2,1,0:T(8,128)} %get-tuple-element.59.mix, ...), custom_call_target="tpu_custom_call" | custom-call | tf_op jit(solution)/shard_map/backward/pallas_call | solution.py:1343
  250.5 13.6 %finish.1 = (bf16[8,256,768]{2,1,0:T(8,128)(2,1)}, bf16[8,256,768]{2,1,0:T(8,128)(2,1)}, f32[48,768]{1,0:T(8,128)}, f32[48,768]{1,0:T(8,128)}, f32[48,128]{1,0:T...) custom-call(bf16[8,256,768]{2,1,0:T(8,128)(2,1)} %bitcast.16, ...), custom_call_target="tpu_custom_call" | custom-call | tf_op jit(solution)/shard_map/finish/pallas_call | solution.py:460
  264.1 1.3 reduce
  265.4 1.3 reduce.1
  266.6 1.4 copy.35
  268.0 1.8 copy.36
  (4 shorter events, 0.0 us)

commit v5 on v4

v5 whole, which is shorter than its diff:
```python
import functools

import jax
import jax.numpy as jnp
import numpy as np
from jax import lax
from jax.experimental import pallas as pl
from jax.experimental.pallas import tpu as pltpu
from jax.sharding import PartitionSpec as P

EPSILON = 1e-05
F32, BF16 = jnp.float32, jnp.bfloat16
HEAD = 64
LANES = 128
HALO = 16
ROWS = 64
GONE = -1e30
VMEM_BYTES = 60 * 1024 * 1024
BLOCK_VMEM_BYTES = 63 * 1024 * 1024


def mm(left, right):
    return jnp.dot(left, right, preferred_element_type=F32)


def mm_nt(left, right):
    return lax.dot_general(left, right, (((1,), (1,)), ((), ())), preferred_element_type=F32)


def mm_tn(left, right):
    return lax.dot_general(left, right, (((0,), (0,)), ((), ())), preferred_element_type=F32)


def parts_of(value, count):
    parts = []
    for _ in range(count - 1):
        parts.append(value.astype(BF16))
        value = value - parts[-1].astype(F32)
    return parts + [value.astype(BF16)]


def pick(value, ones, count=2):
    return sum(mm(part, ones) for part in parts_of(value, count))


def pick_left(ones, value, count=3):
    found = mm(ones, jnp.concatenate(parts_of(value, count), 1))
    width = value.shape[1]
    return sum(found[:, k * width : (k + 1) * width] for k in range(count))


SLOTS = 16


def three_parts(value):
    high = value.astype(BF16).astype(F32)
    middle = (value - high).astype(BF16).astype(F32)
    lane = lax.broadcasted_iota(jnp.int32, value.shape, 1)
    chosen = jnp.where(lane < SLOTS, high, jnp.where(lane < 2 * SLOTS, middle, value - high - middle))
    return jnp.where(lane < 3 * SLOTS, chosen, 0.0).astype(BF16)


def to_lanes(value, ones):
    return mm(three_parts(value), ones)


def folded(value):
    return jnp.sum(value.reshape(-1, 8, value.shape[1]), 0)


def to_rows(folds):
    rows = [jnp.sum(fold, 0, keepdims=True) for fold in folds]
    return jnp.concatenate(rows + [jnp.zeros_like(rows[0])] * (8 - len(rows)), 0)


def softplus(value):
    return jnp.maximum(value, 0.0) + jnp.log1p(jnp.exp(-jnp.abs(value)))


def sigmoid(value):
    return jax.nn.sigmoid(value)


def column_blocks(width):
    return [(at, min(LANES, width - at)) for at in range(0, width, LANES)]


def row_blocks(length):
    return [(at, min(ROWS, length - at)) for at in range(0, length, ROWS)]


def row_index(length):
    return lax.broadcasted_iota(jnp.int32, (length, LANES), 0).astype(F32)


def is_first_step():
    return pl.program_id(0) == 0


def is_last_step():
    return pl.program_id(0) == pl.num_programs(0) - 1


def half_masks(width):
    lane = lax.broadcasted_iota(jnp.int32, (1, width), 1)
    return [(lane // HEAD) == k for k in range(width // HEAD)]


def normalised(hidden, gain):
    scale = lax.rsqrt(jnp.mean(hidden * hidden, -1, keepdims=True) + EPSILON)
    return hidden * scale * gain, scale


def keep_masks(age, masks):
    for lag in range(1, 4):
        masks[lag - 1] = jnp.where(age[...] >= lag, 1.0, 0.0)


def normalise(hid, norm_in, normed):
    for at in range(0, hid.shape[0], 64):
        rows = slice(at, min(at + 64, hid.shape[0]))
        normed[rows] = normalised(hid[rows].astype(F32), norm_in[...])[0].astype(BF16)


def project(age, w_in, taps, heads, spread, tri,
            normed, raw_low, pre, dt_raw, cum, local, decay, act, masks, raw):
    length, channels = act.shape[0], taps.shape[1]
    bc_width = 2 * LANES
    raw[:, :bc_width] = mm(normed[...], w_in[:, :bc_width])
    raw[:, bc_width:] = mm(normed[...], w_in[:, bc_width + LANES :])
    raw_low[:, :bc_width] = raw[:, :bc_width].astype(BF16)
    raw_low[:, bc_width + LANES :] = raw[:, bc_width:].astype(BF16)
    dt_raw[...] = mm(normed[HALO:], w_in[:, bc_width : bc_width + LANES])
    keep_masks(age, masks)
    for at, width in column_blocks(channels):
        cols = slice(at, at + width)
        running = taps[4:5, cols] + taps[0:1, cols] * raw[HALO:, cols]
        for lag in range(1, 4):
            tapped = masks[lag - 1, :, :width] * raw[HALO - lag : HALO - lag + length, cols]
            running = running + taps[lag : lag + 1, cols] * tapped
        pre[:, cols] = running.astype(BF16)
        running = pre[:, cols].astype(F32)
        act[:, cols] = running * sigmoid(running)
    step = softplus(dt_raw[...] + heads[0:1])
    total = pick_left(tri[...], -jnp.exp(heads[1:2]) * step)
    cum[...] = total
    last, age_last = total[length - 1 :], age[length - 1 :]
    open_end = row_index(length) - (length - 1) + age_last >= 0
    weight = jnp.where(open_end, jnp.exp(last - total), 0.0) * step
    weighted = (act[:, bc_width:] * to_lanes(weight, spread[...])).astype(BF16)
    local[...] = mm_tn(act[:, :LANES].astype(BF16), weighted).astype(BF16)
    kept = jnp.where(age_last > length - 1, jnp.exp(last), 0.0)
    decay[...] = to_lanes(jnp.broadcast_to(kept, (8, LANES)), spread[...])


def activated(pre):
    value = pre[...].astype(F32)
    return (value * sigmoid(value)).astype(BF16)


def wide_mask(back, age):
    age = jnp.concatenate([age] * (back.shape[1] // LANES), 1) if age.shape[0] > 1 else age
    return jnp.where((back >= 0) & (back <= age), 0.0, GONE)


def gate_products(normed, out_grad, w_z, w_out_t, gate, grad_gn):
    gate[...] = mm(normed[HALO:], w_z()).astype(BF16)
    grad_gn[...] = mm(out_grad[...], w_out_t()).astype(BF16)


def mix_within(pre, dt_raw, cum, age, skip, heads, spread, near, seg, pair, step_x):
    length, inner = near.shape
    bc_width = 2 * LANES
    pair[...] = mm_nt(activated(pre.at[:, LANES:bc_width]), activated(pre.at[:, :LANES]))
    row = lax.broadcasted_iota(jnp.int32, (length, length), 0)
    col = lax.broadcasted_iota(jnp.int32, (length, length), 1)
    back = (row - col).astype(F32)
    seg[...] = wide_mask(back, age[...])
    total = cum[...]
    total_t = cum[...].T
    step_x[...] = to_lanes(softplus(dt_raw[...] + heads[0:1]), spread[...])
    for at, width in column_blocks(inner):
        cols = slice(at, at + width)
        x_pre = pre[:, bc_width + at : bc_width + at + width].astype(F32)
        values = x_pre * sigmoid(x_pre)
        fed = (values * step_x[:, cols]).astype(BF16)
        masks = half_masks(width)
        for start in range(0, length, LANES):
            stop = start + LANES
            mixing = []
            for head in range(at // HEAD, (at + width) // HEAD):
                spread_log = total[start:stop, head : head + 1] - total_t[head : head + 1, :stop]
                mixing.append((pair[start:stop, :stop] * jnp.exp(spread_log + seg[start:stop, :stop])).astype(BF16))
            fed_to = jnp.concatenate([jnp.where(mask, fed[:stop], 0) for mask in masks], 0)
            near[start:stop, cols] = skip[:, cols] * values[start:stop] + mm(jnp.concatenate(mixing, 1), fed_to)


def mix_states(pre, cum, age, state_in, near, gate, grad_gn, w_out_t, norm_gate, spread,
               mixer, part, stats, carried, gated_low):
    length, inner = near.shape
    open_start = age[...] > row_index(length)
    carried[...] = to_lanes(jnp.where(open_start, jnp.exp(cum[...]), 0.0), spread[...])
    carried[...] = carried[...] * mm(activated(pre.at[:, LANES : 2 * LANES]), state_in[...])
    squares, products = {}, {}
    for at, width in column_blocks(inner):
        cols = slice(at, at + width)
        mixed = near[:, cols] + carried[:, cols]
        mixer[:, cols] = mixed
        raw_gate = gate[:, cols].astype(F32)
        gated = mixed * (raw_gate * sigmoid(raw_gate))
        weighted = gated * norm_gate[:, cols]
        gated_low[:, cols] = weighted.astype(BF16)
        squares[width] = squares.get(width, 0.0) + gated * gated
        products[width] = products.get(width, 0.0) + grad_gn[:, cols].astype(F32) * weighted
    part[...] = mm_nt(gated_low[...], w_out_t()).astype(BF16)
    lane = lax.broadcasted_iota(jnp.int32, (length, LANES), 1)
    squares = sum(jnp.sum(found, 1, keepdims=True) for found in squares.values())
    products = sum(jnp.sum(found, 1, keepdims=True) for found in products.values())
    columns = jnp.where(lane == 0, squares, jnp.where(lane == 1, products, 0.0))
    stats[...] = columns.T[:8]


def forward_local(hid, halo, age, norm_in, w_in, taps, heads, spread, tri,
                  normed, raw, pre, dt_raw, cum, local, decay, act, masks, raw_wide):
    normalise(halo.at[0], norm_in, normed.at[0, :HALO])
    normalise(hid.at[0], norm_in, normed.at[0, HALO:])
    project(age.at[0], w_in, taps, heads, spread, tri, normed.at[0], raw.at[0],
            pre.at[0], dt_raw.at[0], cum.at[0], local.at[0], decay.at[0], act, masks, raw_wide)


def forward_mix(pre, dt_raw, cum, age, state_in, normed, out_grad, w_z, w_out_t, norm_gate, skip, heads, spread,
                mixer, gate, grad_gn, part, stats, near, seg, pair, carried, step_x, gated_low):
    w_z_all, w_out_all = (lambda: w_z[...]), (lambda: w_out_t[...])
    gate_products(normed.at[0], out_grad.at[0], w_z_all, w_out_all, gate.at[0], grad_gn.at[0])
    mix_within(pre.at[0], dt_raw.at[0], cum.at[0], age.at[0], skip, heads, spread, near, seg, pair, step_x)
    mix_states(pre.at[0], cum.at[0], age.at[0], state_in.at[0], near, gate.at[0], grad_gn.at[0], w_out_all, norm_gate,
               spread, mixer.at[0], part.at[0], stats.at[0], carried, gated_low)


def gate_back(inner_all, mixer, gate, grad_gn, stats, pre, cum, age, state_in, normed, out_grad, norm_gate,
              spread, grad_mix, grad_gate, grad_c, grad_state, sums, sum_z, sum_o,
              carried, gated_low, from_state):
    length, inner = mixer.shape
    bc_width = 2 * LANES
    open_start = age[...] > row_index(length)
    carried[...] = to_lanes(jnp.where(open_start, jnp.exp(cum[...]), 0.0), spread[...])
    means = stats[...].T / inner_all
    scale_all = jnp.broadcast_to(lax.rsqrt(means[:, :1] + EPSILON), (length, LANES))
    pull_all = scale_all * scale_all * scale_all * jnp.broadcast_to(means[:, 1:2], (length, LANES))
    for at, width in column_blocks(inner):
        cols = slice(at, at + width)
        scale, pull = scale_all[:, :width], pull_all[:, :width]
        mixed = mixer[:, cols]
        raw_gate = gate[:, cols].astype(F32)
        logistic = sigmoid(raw_gate)
        acted = raw_gate * logistic
        gated = mixed * acted
        grad_out = grad_gn[:, cols].astype(F32)
        gated_scaled = gated * scale
        gated_low[:, cols] = (gated_scaled * norm_gate[:, cols]).astype(BF16)
        grad_gated = scale * (grad_out * norm_gate[:, cols]) - gated * pull
        grad_gate[:, cols] = (grad_gated * mixed * (logistic * (1.0 + raw_gate * (1.0 - logistic)))).astype(BF16)
        mix_low = (grad_gated * acted).astype(BF16)
        grad_mix[:, cols] = mix_low
        sums[0, :, cols] += folded(grad_out * gated_scaled)
        from_state[:, cols] = (carried[:, cols] * mix_low.astype(F32)).astype(BF16)
    grad_state[...] = mm_tn(activated(pre.at[:, LANES:bc_width]), from_state[...]).astype(BF16)
    grad_c[...] = mm_nt(from_state[...], state_in[...])
    sum_z[...] += mm_tn(normed[HALO:], grad_gate[...])
    sum_o[...] += mm_tn(out_grad[...], gated_low[...])


def within_back(mixer, pre, dt_raw, cum, age_row, grad_mix, skip, heads, spread, gather, grad_fed, grad_cum, grad_bc,
                sums, seg, pair, grad_pair, step_x, high, low):
    length, inner = grad_mix.shape
    bc_width = 2 * LANES
    readout, inputs_b = activated(pre.at[:, LANES:bc_width]), activated(pre.at[:, :LANES])
    pair[...] = mm_nt(inputs_b, readout)
    grad_pair[...] = jnp.zeros_like(grad_pair)
    row = lax.broadcasted_iota(jnp.int32, (length, length), 0)
    col = lax.broadcasted_iota(jnp.int32, (length, length), 1)
    back = (col - row).astype(F32)
    seg[...] = wide_mask(back, age_row[:1])
    total = cum[...]
    total_t = cum[...].T
    step_x[...] = to_lanes(softplus(dt_raw[...] + heads[0:1]), spread[...])
    for at, width in column_blocks(inner):
        cols = slice(at, at + width)
        x_pre = pre[:, bc_width + at : bc_width + at + width].astype(F32)
        values = x_pre * sigmoid(x_pre)
        fed = (values * step_x[:, cols]).astype(BF16)
        mix_low = grad_mix[:, cols]
        mix_wide = mix_low.astype(F32)
        kept = mix_wide * (mixer[:, cols] - skip[:, cols] * values)
        masks = half_masks(width)
        for start in range(0, length, LANES):
            stop = start + LANES
            fed_from = jnp.concatenate([jnp.where(mask, fed[start:stop], 0) for mask in masks], 0)
            grad_mixing = mm_nt(fed_from, mix_low[start:])
            total_pair = grad_pair[start:stop, start:]
            mixing = []
            for k, head in enumerate(range(at // HEAD, (at + width) // HEAD)):
                spread_log = total_t[head : head + 1, start:] - total[start:stop, head : head + 1]
                decayed = jnp.exp(spread_log + seg[start:stop, start:])
                mixing.append((pair[start:stop, start:] * decayed).astype(BF16))
                total_pair = total_pair + grad_mixing[k * LANES : (k + 1) * LANES] * decayed
            grad_pair[start:stop, start:] = total_pair
            mix_to = jnp.concatenate([jnp.where(mask, mix_low[start:], 0) for mask in masks], 0)
            grad_fed[start:stop, cols] = mm(jnp.concatenate(mixing, 1), mix_to)
        sums[1, :, cols] += folded(mix_wide * values)
        kept = kept - grad_fed[:, cols] * fed.astype(F32)
        high[:, cols] = kept.astype(BF16)
        low[:, cols] = (kept - high[:, cols].astype(F32)).astype(BF16)
    grad_cum[...] = mm(high[...], gather[...]) + mm(low[...], gather[...])
    pair_low = grad_pair[...].astype(BF16)
    grad_bc[:, :LANES] = mm(pair_low, readout)
    grad_bc[:, LANES:] += mm_tn(pair_low, inputs_b)


def state_back(grad_later, state_in, pre, raw, dt_raw, cum, age, grad_fed, grad_mix, grad_cum, grad_bc, taps, skip,
               heads, spread, gather, tri_up, grad_in, conv_sums, head_sums,
               step_x, open_x, from_state, fed_state, met_state, met_all, slope, keep):
    length, inner = grad_fed.shape
    channels = taps.shape[1]
    bc_width = 2 * LANES
    lead = HALO + length
    grad_in[:HALO, bc_width : bc_width + LANES] = jnp.zeros((HALO, LANES), BF16)
    for lag in range(1, 4):
        keep[lag - 1, HALO - lag : lead - lag] = jnp.where(age[...] >= lag, 1.0, 0.0)
    total = cum[...]
    step_raw = dt_raw[...] + heads[0:1]
    step = softplus(step_raw)
    rate = -jnp.exp(heads[1:2])
    step_x[...] = to_lanes(step, spread[...])
    last, age_last = total[length - 1 :], age[length - 1 :]
    open_end = row_index(length) - (length - 1) + age_last >= 0
    open_x[...] = to_lanes(jnp.where(open_end, jnp.exp(last - total), 0.0), spread[...])
    from_state[...] = open_x[...] * mm(activated(pre.at[:, :LANES]), grad_later[...])
    for at, width in column_blocks(inner):
        cols = slice(at, at + width)
        x_pre = pre[:, bc_width + at : bc_width + at + width].astype(F32)
        logistic = sigmoid(x_pre)
        values = x_pre * logistic
        fed = values * step_x[:, cols]
        fed_state[:, cols] = (fed * open_x[:, cols]).astype(BF16)
        arrived = from_state[:, cols]
        grad = grad_fed[:, cols] + arrived
        met_state[:, cols] = (values * arrived).astype(BF16)
        met_all[:, cols] = (values * grad).astype(BF16)
        grad_values = grad * step_x[:, cols] + skip[:, cols] * grad_mix[:, cols].astype(F32)
        slope[HALO:lead, bc_width + at : bc_width + at + width] = grad_values * (
            logistic * (1.0 + x_pre * (1.0 - logistic))
        )
    for at, extra in ((0, mm_nt(fed_state[...], grad_later[...])), (LANES, 0.0)):
        cols = slice(at, at + LANES)
        bc_pre = pre[:, cols].astype(F32)
        logistic = sigmoid(bc_pre)
        slope[HALO:lead, cols] = (grad_bc[:, cols] + extra) * (logistic * (1.0 + bc_pre * (1.0 - logistic)))
    state_sum, step_sum = mm(met_state[...], gather[...]) * step, mm(met_all[...], gather[...])
    kept = jnp.where(age_last > length - 1, jnp.exp(last), 0.0)
    met = jnp.sum(grad_later[...].astype(F32) * state_in[...].astype(F32), 0, keepdims=True)
    met = pick(jnp.broadcast_to(met, (8, inner)), gather[...], 3)[:1]
    end = met * kept + jnp.sum(state_sum, 0, keepdims=True)
    grad_a = pick_left(tri_up[...], grad_cum[...] - state_sum) + end
    head_sums[1] += folded(grad_a * rate * step)
    grad_step = (step_sum + grad_a * rate) * sigmoid(step_raw)
    head_sums[0] += folded(grad_step)
    grad_in[HALO:, bc_width : bc_width + LANES] = grad_step.astype(BF16)
    for at, width in column_blocks(channels):
        cols = slice(at, at + width)
        shifted = at if at < bc_width else at + LANES
        for top, rows in row_blocks(lead):
            here = slice(top, top + rows)
            own, fed_in = slope[here, cols], raw[here, shifted : shifted + width].astype(F32)
            total_in = taps[0:1, cols] * own
            conv_sums[0, :, cols] += folded(own * fed_in)
            conv_sums[4, :, cols] += folded(own)
            for lag in range(1, 4):
                later = keep[lag - 1, here, :width] * slope[top + lag : top + rows + lag, cols]
                conv_sums[lag, :, cols] += folded(later * fed_in)
                total_in = total_in + taps[lag : lag + 1, cols] * later
            grad_in[here, shifted : shifted + width] = total_in.astype(BF16)


def clear_margins(slope, keep, length):
    slope[:HALO] = jnp.zeros((HALO, slope.shape[1]), F32)
    slope[HALO + length :] = jnp.zeros((8, slope.shape[1]), F32)
    keep[...] = jnp.zeros_like(keep)


def features_back(grad_in, grad_gate, w_in, w_z, grad_normed, grad_halo, wide):
    wide[...] = mm_nt(grad_in[...], w_in[...])
    wide[HALO:] += mm_nt(grad_gate[...], w_z())
    grad_halo[...] = wide[:HALO].astype(BF16)
    grad_normed[...] = wide[HALO:].astype(BF16)


def gain_back(weights, gradients, sums):
    for top in range(0, weights.shape[0], 2 * LANES):
        rows = slice(top, top + 2 * LANES)
        total = 0.0
        for at, width in column_blocks(weights.shape[1]):
            cols = slice(at, at + width)
            total = total + weights[rows, cols].astype(F32) * gradients[rows, cols]
        sums[:, rows] += folded(total.T)


def backward_local(inner_all, mixer, gate, grad_gn, stats, pre, dt_raw, cum, age, age_row, state_in, normed, out_grad,
                   norm_gate, skip, heads, spread, gather,
                   grad_fed, grad_mix, grad_gate, grad_cum, grad_bc, grad_state, grad_wz, grad_wo, sums_out,
                   sums, sum_z, sum_o, seg, pair, grad_pair, carried, step_x, gated_low, from_state):
    @pl.when(is_first_step())
    def _():
        sum_z[...] = jnp.zeros_like(sum_z)
        sum_o[...] = jnp.zeros_like(sum_o)
        sums[...] = jnp.zeros_like(sums)

    gate_back(inner_all, mixer.at[0], gate.at[0], grad_gn.at[0], stats.at[0], pre.at[0], cum.at[0], age.at[0],
              state_in.at[0], normed.at[0], out_grad.at[0], norm_gate, spread, grad_mix.at[0],
              grad_gate.at[0], grad_bc.at[0, :, LANES:], grad_state.at[0], sums, sum_z, sum_o,
              carried, gated_low, from_state)
    within_back(mixer.at[0], pre.at[0], dt_raw.at[0], cum.at[0], age_row.at[0], grad_mix.at[0], skip, heads, spread,
                gather, grad_fed.at[0], grad_cum.at[0], grad_bc.at[0], sums, seg, pair, grad_pair, step_x, gated_low,
                from_state)

    @pl.when(is_last_step())
    def _():
        grad_wz[...] = sum_z[...].astype(BF16)
        grad_wo[...] = sum_o[...].astype(BF16)
        sums_out[...] = to_rows([sums[0], sums[1]])


def backward_finish(grad_later, state_in, pre, raw, dt_raw, cum, age, grad_fed, grad_mix, grad_cum, grad_bc, grad_gate,
                    normed, hid, halo, w_in, w_z, taps, skip, heads, spread, gather, tri_up,
                    grad_normed, grad_halo, grad_w, conv_out, head_out, norm_out,
                    conv_sums, head_sums, norm_sums, sum_w, step_x, open_x, from_state, fed_state, met_state, met_all,
                    slope, keep, grad_in, wide):
    @pl.when(is_first_step())
    def _():
        for sums in (sum_w, conv_sums, head_sums, norm_sums):
            sums[...] = jnp.zeros_like(sums)
        clear_margins(slope, keep, hid.shape[1])

    state_back(grad_later.at[0], state_in.at[0], pre.at[0], raw.at[0], dt_raw.at[0], cum.at[0], age.at[0],
               grad_fed.at[0], grad_mix.at[0], grad_cum.at[0], grad_bc.at[0], taps, skip, heads, spread, gather, tri_up,
               grad_in, conv_sums, head_sums, step_x, open_x, from_state, fed_state, met_state, met_all, slope,
               keep)
    features_back(grad_in, grad_gate.at[0], w_in, lambda: w_z[...], grad_normed.at[0], grad_halo.at[0], wide)
    for rows, kept in ((slice(0, HALO), halo.at[0]), (slice(HALO, None), hid.at[0])):
        hidden = kept[...].astype(F32)
        norm_sums[...] += folded(wide[rows] * hidden * normalised(hidden, 1.0)[1])
    sum_w[...] += mm_tn(normed[0], grad_in[...])

    @pl.when(is_last_step())
    def _():
        grad_w[...] = sum_w[...].astype(BF16)
        conv_out[...] = to_rows([conv_sums[k] for k in range(5)])
        head_out[...] = to_rows([head_sums[0], head_sums[1]])
        norm_out[...] = to_rows([norm_sums[...]])


def finish(inner_all, hid, out_grad, stats, norm_in, own_part, other_part, own_grad, other_grad, own_tail, other_tail,
           sums_zo, sums_w, conv_sums, norm_sums, head_sums, inner_sums, gather,
           out, in_grad, grad_wz, grad_wx, grad_wbc, grad_wdt, grad_wo, grad_conv_x, grad_conv_bc, grad_dt_bias,
           grad_a_log, grad_skip, grad_norm_gate, grad_norm_in, total):
    length = hid.shape[1]
    gain = norm_in[...].reshape(1, -1)
    for i in range(hid.shape[0]):

        def added(own, others, rows, i=i):
            found = own[i, rows].astype(F32)
            for k in range(others.shape[0]):
                found = found + others[k, i, rows].astype(F32)
            return found

        total[...] = added(own_grad, other_grad, slice(None))
        total[length - HALO :] += added(own_tail, other_tail, slice(None))
        scales = lax.rsqrt(stats[i].T[:, :1] / inner_all + EPSILON)
        for at in range(0, length, 64):
            rows = slice(at, at + 64)
            hidden = hid[i, rows].astype(F32)
            out[i, rows] = (hidden + scales[rows] * added(own_part, other_part, rows)).astype(BF16)
            scale = normalised(hidden, 1.0)[1]
            weighted = total[rows] * gain
            inner_mean = jnp.mean(weighted * hidden, -1, keepdims=True)
            in_grad[i, rows] = (
                out_grad[i, rows].astype(F32) + scale * weighted - hidden * (scale * scale * scale * inner_mean)
            ).astype(BF16)

    @pl.when(is_last_step())
    def _():
        inner, own_bc, head_count = grad_wz.shape[1], grad_wbc.shape[1], grad_wdt.shape[0]
        grad_wz[...] = sums_zo[:, :inner]
        grad_wo[...] = sums_zo[:, inner:]
        grad_wbc[...] = sums_w[:, :own_bc]
        grad_wdt[...] = sums_w[:, own_bc : own_bc + LANES].T[:head_count]
        grad_wx[...] = sums_w[:, own_bc + LANES :]
        grad_conv_bc[...] = conv_sums[:5, :own_bc]
        grad_conv_x[...] = conv_sums[:5, own_bc:]
        grad_dt_bias[...] = head_sums[0:1, :head_count]
        grad_a_log[...] = head_sums[1:2, :head_count]
        grad_norm_in[...] = norm_sums[0:1].reshape(-1)
        grad_norm_gate[...] = inner_sums[0:1].reshape(-1)
        grad_skip[...] = pick(inner_sums[...], gather[...], 3)[1:2, :head_count]


def by_piece(array):
    rest = array.shape[1:]
    return pl.BlockSpec((1,) + rest, lambda i: (i,) + (0,) * len(rest))


SPAN = 2


def by_span(array):
    rest = array.shape[1:]
    return pl.BlockSpec((SPAN,) + rest, lambda i: (i,) + (0,) * len(rest))


def by_span_second(array):
    rest = array.shape[2:]
    return pl.BlockSpec((array.shape[0], SPAN) + rest, lambda i: (0, i) + (0,) * len(rest))


def fixed(array):
    return pl.BlockSpec(array.shape, lambda i: (0,) * len(array.shape))


def call(kernel, pieces, inputs, outputs, scratch, name):
    return pl.pallas_call(
        kernel,
        grid=(pieces,),
        in_specs=[cut(array) for array, cut in inputs],
        out_specs=[cut(shape) for shape, cut in outputs],
        out_shape=[shape for shape, _ in outputs],
        scratch_shapes=[pltpu.VMEM(shape, kind) for shape, kind in scratch],
        compiler_params=pltpu.CompilerParams(vmem_limit_bytes=VMEM_BYTES),
        name=name,
    )(*[array for array, _ in inputs])


def shaped(kind, *dims):
    return jax.ShapeDtypeStruct(dims, kind)


MESH = pl.DeviceIdType.MESH
UP, DOWN, NEXT_X, NEXT_Y = range(4)


def coordinates():
    return lax.axis_index("shard"), lax.axis_index("context"), lax.axis_index("tensor")


def greet(partners):
    barrier = pltpu.get_barrier_semaphore()
    count = 0
    for there, device in partners:
        if there is True:
            pl.semaphore_signal(barrier, inc=1, device_id=device, device_id_type=MESH)
            count = count + 1
        else:
            pl.when(there)(
                functools.partial(pl.semaphore_signal, barrier, inc=1, device_id=device, device_id_type=MESH)
            )
            count = count + there.astype(jnp.int32)
    pl.semaphore_wait(barrier, count)


def neighbours(place):
    shard, context, _ = place
    count = lax.axis_size("context")
    return [
        (context + 1 < count, {"context": context + 1}),
        (context > 0, {"context": context - 1}),
        (True, {"shard": shard ^ 1}),
        (True, {"shard": shard ^ 2}),
    ]


def gather_step(step, start, arrived, stage, out, received):
    place = shard, context, _ = coordinates()
    count = lax.axis_size("context")
    up, down, next_x, next_y = neighbours(place)
    mine, beside_x, beside_y, across = [(shard ^ k) * count for k in (0, 1, 2, 3)]

    def pass_on(number, source, slot, to, there=True):
        if to[0] is not True:
            there = to[0] if there is True else there & to[0]
        start(number, source, out(slot), received.at[slot], to[1], there)

    def both_ways(distance):
        found = [(context - distance, context >= distance, up),
                 (context + distance, context + distance < count, down)]
        return [(jnp.clip(at, 0, count - 1), there, to) for at, there, to in found[: 2 if distance else 1]]

    if step == 0:
        for k, to in enumerate((up, down, next_x, next_y)):
            pass_on(k, stage, mine + context, to)
    elif step < count:
        for k, (at, there, to) in enumerate(both_ways(step)):
            slot = mine + at
            arrived(out(slot), received.at[slot], there)
            for m, target in enumerate((to, next_x, next_y)):
                pass_on(4 + (step - 1) * 6 + k * 3 + m, out(slot), slot, target, there)
    elif step < 2 * count:
        for k, (at, there, _) in enumerate(both_ways(step - count)):
            number = 4 + (count - 1) * 6 + (step - count) * 4 + k * 2
            slot_x, slot_y = beside_x + at, beside_y + at
            arrived(out(slot_x), received.at[slot_x], there)
            pass_on(number, out(slot_x), slot_x, next_y, there & (at < count // 2))
            arrived(out(slot_y), received.at[slot_y], there)
            pass_on(number + 1, out(slot_y), slot_y, next_x, there & (at >= count // 2))
    else:
        for at in range(count):
            arrived(out(across + at), received.at[across + at], True)


def gather_steps():
    return 2 * lax.axis_size("context") + 1


GATHER_COPIES = 40


class Numbered:
    def __init__(self, send):
        self.send = send

    def copy(self, number, source, target, received, device):
        return pltpu.make_async_remote_copy(
            src_ref=source, dst_ref=target, send_sem=self.send.at[number], recv_sem=received,
            device_id=device, device_id_type=MESH,
        )

    def when(self, there, action):
        if there is True:
            action()
        else:
            pl.when(there)(action)

    def start(self, number, source, target, received, device, there=True):
        self.when(there, self.copy(number, source, target, received, device).start)

    def sent(self, number, source, target, received, device, there=True):
        self.when(there, self.copy(number, source, target, received, device).wait_send)

    def arrived(self, target, received, there=True):
        other = {"tensor": 1 - lax.axis_index("tensor")}
        self.when(there, self.copy(0, target, target, received, other).wait_recv)

    def nothing(self, *_):
        pass


def scatter_scratch(rows, width):
    return [pltpu.VMEM((4, rows, width), BF16) for _ in range(4)] + [DMA((4, 4)), DMA((SCATTER_COPIES,))]


SCATTER_COPIES = 16


def scatter_steps():
    return 2 + lax.axis_size("context") // 2 + lax.axis_size("context")


def scatter_step(step, start, arrived, blocks, out, first, from_x, from_y, along, received, add=True):
    shard, context, _ = coordinates()
    count = lax.axis_size("context")
    half = count // 2
    _, _, next_x, next_y = neighbours(coordinates())
    mine, beside_x, beside_y, across = [(shard ^ k) * count for k in (0, 1, 2, 3)]
    if step == 0:
        for k in range(count):
            start(k, blocks.at[across + k], first.at[k], received.at[0, k], (next_y if k < half else next_x)[1], True)
        for k in (0, count - 1, *range(1, count - 1)):
            beside, target, row, to = (beside_y, from_y, 2, next_y) if k < half else (beside_x, from_x, 1, next_x)
            start(count + k, blocks.at[beside + k], target.at[k], received.at[row, k], to[1], True)
    elif step <= half:
        for k in (step - 1, count - step):
            beside, target, row, to = (beside_x, from_x, 1, next_x) if k < half else (beside_y, from_y, 2, next_y)
            arrived(first.at[k], received.at[0, k], True)
            if add:
                blocks[beside + k] = (blocks[beside + k].astype(F32) + first[k].astype(F32)).astype(BF16)
            start(2 * count + k, blocks.at[beside + k], target.at[k], received.at[row, k], to[1], True)
    elif step <= half + count:
        at = step - half - 1
        k = at // 2 if at % 2 == 0 else count - 1 - at // 2
        arrived(from_x.at[k], received.at[1, k], True)
        arrived(from_y.at[k], received.at[2, k], True)
        if add:
            found = blocks[mine + k].astype(F32) + from_x[k].astype(F32) + from_y[k].astype(F32)
            blocks[mine + k] = found.astype(BF16)

            @pl.when(context == k)
            def _():
                out[...] = found

        there = context != k
        start(3 * count + k, blocks.at[mine + k], along.at[context], received.at[3, context], {"context": k}, there)
    else:
        for k in range(count):

            @pl.when(context != k)
            def _(k=k):
                arrived(along.at[k], received.at[3, k], True)
                out[...] += along[k].astype(F32)


GATHER_TURNS = (0, 0, 1, 3, 2, 4, 6, 8, 10)
OUTER_TURNS = (24, 28, 29, 33, 33, 34, 34, 38)
OUTER_END = 39
SMALL_TURNS = (5, 6, 7)
UP_TURNS = ((4, 6, 8, 11, 14, 16, 18, 19), (7, 10, 12, 15, 17, 18, 20, 21))
DOWN_TURNS = ((20, 21, 22, 23, 24, 26, 28, 30), (22, 23, 24, 25, 27, 29, 31, 33))


def block(inner_all, out_grad, hid_all, doc_start, w_bc, w_dt_t, w_x, conv_bc, conv_x, norm_in_all, norm_gate_all,
          dt_bias, a_log, skip_d, w_z, w_out_t, spread, gather, tri, tri_up,
          stats_out, sums_zo, sums_w, conv_out, norm_out, head_out, inner_out, own_part, other_part, own_grad,
          other_grad, own_tail, other_tail,
          halo, ages, age_lanes, vectors, w_in, taps, heads, stage_w, dt_rows, out_grad_last,
          normed, pre, cum, gates, near, inputs, state_in, leaving, arrived, decay, both, grad_bc, grad_cum, sum_all,
          stage_in, stage, half_out, half_in, carried, step_x, low_a, low_b, low_c, slope, keep, wide, seg, pair,
          grad_pair, step_raw, tails, stats, stats_in, small, seen, conv_sums, head_sums, norm_sums,
          inner_sums,
          send_w, received_w, others_sent, others, send_in, received, states_up, states_down, send, got, grad_send, grad_got, stats_send, stats_got,
          part_send, part_got, stores, tail_send, tail_got, *buffers):
    outer, last_ones = buffers[:6], buffers[6:]
    shard, context, tensor = coordinates()
    phase, i = pl.program_id(0), pl.program_id(1)
    pieces = pl.num_programs(1)
    turn = phase * pieces + i
    count = lax.axis_size("context")
    length = hid_all.shape[1]
    model, inner = sum_all.shape[0], w_z.shape[1]
    in_width, channels = w_in.shape[1], taps.shape[1]
    lead = HALO + length
    bc_width = 2 * LANES
    own_bc = bc_width // 2
    rows = stage.shape[1]
    partner = {"tensor": 1 - tensor}
    below, above = context > 0, context < count - 1
    cols = pl.ds(pl.multiple_of(tensor * own_bc, LANES), own_bc)
    other_cols = pl.ds(pl.multiple_of((1 - tensor) * own_bc, LANES), own_bc)
    norm_in, norm_gate, skip = [vectors.at[k : k + 1] for k in range(3)]
    numbered, misc = Numbered(send_in), Numbered(send)
    act, features = wide.at[:length], wide.at[:, :model]

    def piece(array, k=i):
        return array.at[k]

    def link(number, source, target, device):
        return misc.copy(number, source, target, got.at[number], device)

    def half_link():
        return link(0, half_out, half_in, partner)

    def tail_link(k):
        return pltpu.make_async_remote_copy(
            src_ref=tails.at[k], dst_ref=own_tail.at[k], send_sem=tail_send.at[0, k], recv_sem=tail_got.at[0, k],
            device_id={"context": context - 1}, device_id_type=MESH,
        )

    def tail_partner_link(k):
        return to_partner(own_tail.at[k], other_tail.at[0, k], tail_send.at[1, k], tail_got.at[1, k])

    def tail_blanks(k):
        targets = (own_tail.at[k], other_tail.at[0, k])
        return [pltpu.make_async_copy(arrived.at[k, :HALO], target, tail_got.at[n, k]) for n, target in enumerate(targets)]

    def small_link(k):
        to = [partner, {"shard": shard ^ 1}, {"shard": shard ^ 2}, {"context": context ^ 1}, {"context": context ^ 2}]
        return link(3 + k, small.at[k], seen.at[k], to[k])

    def to_partner(source, target, sent, arrives):
        return pltpu.make_async_remote_copy(
            src_ref=source, dst_ref=target, send_sem=sent, recv_sem=arrives, device_id=partner, device_id_type=MESH
        )

    def stats_link(k):
        return to_partner(stats.at[k], stats_in.at[k], stats_send.at[k], stats_got.at[k])

    def part_link(k):
        return to_partner(low_c, other_part.at[0, k], part_send.at[k], part_got.at[k])

    def part_store(k):
        return pltpu.make_async_copy(low_c, own_part.at[k], stores.at[0, k])

    def grad_link(k):
        return to_partner(gates.at[k, :, :inner], other_grad.at[0, k], grad_send.at[k], grad_got.at[k])

    def grad_store(k):
        return pltpu.make_async_copy(gates.at[k, :, :inner], own_grad.at[k], stores.at[1, k])

    def passed(c, target, semaphores, by):
        return pltpu.make_async_remote_copy(
            src_ref=leaving.at[c], dst_ref=target.at[c], send_sem=semaphores.at[1, c], recv_sem=semaphores.at[0, c],
            device_id={"context": context + by}, device_id_type=MESH,
        )

    def up(c):
        return passed(c, state_in, states_up, 1)

    def down(c):
        return passed(c, arrived, states_down, -1)

    def pass_on(c, target, copy):
        copy.wait_recv()
        leaving[c] = (decay[c, :1] * target[c].astype(F32) + leaving[c].astype(F32)).astype(BF16)
        copy.start()

    def step_sizes(k):
        return mm(normed[k, HALO:], w_in[:, bc_width : bc_width + LANES])

    def age_of(k):
        return age_lanes.at[k]

    middle = below & above
    hops = count - 1 - context

    def fetch_features(k):
        return pltpu.make_async_copy(hid_all.at[k], gates.at[k, :, :model], stores.at[0, k])

    def w_in_block(slot):
        return w_in.at[pl.ds(pl.multiple_of(slot * rows, HALO), rows)]

    def both_block(slot):
        return both.at[slot]

    @pl.when(turn == 0)
    def _():
        for k in range(pieces_of(gates)):
            fetch_features(k).start()
        head_count = w_dt_t.shape[0]
        dt_rows[...] = jnp.zeros_like(dt_rows)
        for copy in range(3):
            dt_rows[copy * SLOTS : copy * SLOTS + head_count] = w_dt_t[...].astype(F32)
        stage_w[:, bc_width : bc_width + LANES] = dt_rows[...].T.astype(BF16)
        stage_w[:, bc_width + LANES :] = w_x[...]
        stage_w[:, cols] = w_bc[...]
        taps[...] = jnp.zeros_like(taps)
        taps[:5, cols] = conv_bc[...]
        taps[:5, bc_width:] = conv_x[...]
        greet([(True, partner), (True, {"shard": shard ^ 1}), (True, {"shard": shard ^ 2})]
              + [(True, {"context": context ^ k}) for k in range(1, count)])
        first_links = Numbered(others_sent)
        tail = pl.ds(length - HALO, HALO)
        first_copies = [(0, stage_w.at[:, cols], stage_w.at[:, cols], others.at[0], partner, True),
                        (1, taps.at[:, cols], taps.at[:, cols], others.at[1], partner, True),
                        (2, hid_all.at[:, tail], halo, others.at[2], {"context": context + 1}, above)]
        for copy in first_copies:
            first_links.start(*copy)
        first_links.arrived(stage_w.at[:, other_cols], others.at[0])
        half = in_width // 2 // LANES * LANES
        halves = []
        for k, cut in enumerate((slice(0, half), slice(half, in_width))):
            to = functools.partial(lambda slot, cut: w_in_block(slot).at[:, cut], cut=cut)
            halves.append((Numbered(send_w.at[k]), stage_w.at[:, cut], to, received_w.at[k]))
        for numbered_w, *refs in halves:
            gather_step(0, numbered_w.start, numbered_w.arrived, *refs)
        stage_in[:, :inner] = w_z[...]
        stage_in[:, inner:] = w_out_t[...]
        gather_step(0, numbered.start, numbered.arrived, stage_in, both_block, received)
        w_in_block(shard * count + context)[...] = stage_w[...]
        both[shard * count + context] = stage_in[...]
        lane = lax.broadcasted_iota(jnp.int32, (1, LANES), 1)
        slot = jnp.where(lane < 3 * SLOTS, lane % SLOTS, -1)
        lane_x = lax.broadcasted_iota(jnp.int32, (1, inner), 1)
        head_rows = [jnp.zeros((1, LANES), F32) for _ in range(8)]
        skips = jnp.zeros((1, inner), F32)
        for head in range(head_count):
            head_rows[0] = jnp.where(slot == head, dt_bias[head], head_rows[0])
            head_rows[1] = jnp.where(slot == head, a_log[head], head_rows[1])
            skips = jnp.where(lane_x // HEAD == head, skip_d[head], skips)
        heads[...] = jnp.concatenate(head_rows, 0)
        vectors[0:1] = norm_in_all[...].reshape(1, -1)
        vectors[1:2] = norm_gate_all[...].reshape(1, -1)
        vectors[2:3] = skips
        position = context * length + lax.broadcasted_iota(jnp.int32, (1, length), 1)
        for k in range(pieces_of(gates)):
            at = divmod(k, doc_start.shape[1])
            age = (position - doc_start[at[0], at[1] : at[1] + 1]).astype(F32)
            ages[k] = jnp.broadcast_to(age, (8, length))
        for k in range(pieces_of(gates)):
            fetch_features(k).wait()

        def one(k, carry):
            normalise(gates.at[k, :, :model], norm_in, normed.at[k, HALO:])
            return carry

        lax.fori_loop(0, pieces_of(gates), one, 0)
        for step in range(1, gather_steps()):
            for numbered_w, *refs in halves:
                gather_step(step, numbered_w.start, numbered_w.arrived, *refs)
        for step in range(gather_steps()):
            for numbered_w, *refs in halves:
                gather_step(step, numbered_w.sent, numbered_w.nothing, *refs)
        first_links.arrived(taps.at[:, other_cols], others.at[1])
        first_links.arrived(halo, others.at[2], below)
        for copy in first_copies:
            first_links.sent(*copy)

        @pl.when(jnp.logical_not(below))
        def _():
            halo[...] = jnp.zeros_like(halo)

        for sums in (sum_all, conv_sums, head_sums, norm_sums, inner_sums):
            sums[...] = jnp.zeros_like(sums)

    for c in range(len(UP_TURNS[0])):

        @pl.when((turn == jnp.where(context == 1, UP_TURNS[0][c], UP_TURNS[1][c])) & middle)
        def _(c=c):
            pass_on(c, state_in, up(c))

        @pl.when((turn == jnp.where(hops == 1, DOWN_TURNS[0][c], DOWN_TURNS[1][c])) & middle)
        def _(c=c):
            pass_on(c, arrived, down(c))

    @pl.when(phase == 0)
    def _():
        age_lanes[i] = jnp.broadcast_to(ages[i].T[:, :1], (length, LANES))
        age = age_of(i)
        normalise(halo.at[i], norm_in, normed.at[i, :HALO])
        project(age, w_in, taps, heads, spread, tri, normed.at[i], inputs.at[i],
                pre.at[i], step_raw, cum.at[i], leaving.at[i], decay.at[i], act, keep.at[:, :length], slope.at[:lead])

        @pl.when(jnp.logical_not(below))
        def _():
            state_in[i] = jnp.zeros(state_in.shape[1:], BF16)
            up(i).start()

    @pl.when(turn < 2 * pieces)
    def _():
        for step in range(1, gather_steps()):

            @pl.when(turn == GATHER_TURNS[step])
            def _(step=step):
                gather_step(step, numbered.start, numbered.arrived, stage_in, both_block, received)

        @pl.when(turn == 2 * pieces - 1)
        def _():
            for step in range(gather_steps()):
                gather_step(step, numbered.sent, numbered.nothing, stage_in, both_block, received)

    def w_z_all():
        return both[:, :, :inner].reshape(-1, inner)

    def w_out_all():
        return both[:, :, inner:].reshape(-1, inner)

    def gate_parts(k):
        return gates.at[k, :, :inner], gates.at[k, :, inner:]

    @pl.when(phase == 1)
    def _():
        mix_within(pre.at[i], step_sizes(i), cum.at[i], age_of(i), skip, heads, spread, near.at[i], seg, pair, step_x)

    @pl.when(phase == 2)
    def _():
        gate_products(normed.at[i], out_grad.at[0], w_z_all, w_out_all, *gate_parts(i))

        @pl.when(jnp.logical_not(above))
        def _():
            up(i).wait_recv()

        @pl.when(i >= 1)
        def _():
            part_link(i - 1).wait_send()
            part_store(i - 1).wait()

        mix_states(pre.at[i], cum.at[i], age_of(i), state_in.at[i], near.at[i], *gate_parts(i), w_out_all, norm_gate, spread,
                   near.at[i], low_c, stats.at[i], carried, low_a)
        stats_link(i).start()
        part_link(i).start()
        part_store(i).start()

        @pl.when(above)
        def _():
            up(i).wait_send()

    @pl.when((turn > 2 * pieces) & (turn <= 3 * pieces))
    def _():
        k = turn - 2 * pieces - 1
        stats_link(k).wait_recv()
        stats_out[k] = stats[k] + stats_in[k]
        gate, grad_gn = gate_parts(k)
        gate_back(inner_all, near.at[k], gate, grad_gn, stats_out.at[k], pre.at[k], cum.at[k], age_of(k), state_in.at[k],
                  normed.at[k], out_grad_last, norm_gate, spread, grad_gn, gate, grad_bc.at[k, :, LANES:],
                  leaving.at[k], inner_sums, sum_all.at[:, :inner], sum_all.at[:, inner:], carried, low_a, low_b)

        @pl.when(jnp.logical_not(above))
        def _():
            arrived[k] = jnp.zeros(arrived.shape[1:], BF16)
            down(k).start()

    @pl.when(phase == 2)
    def _():
        out_grad_last[...] = out_grad[0]

    @pl.when(turn == 3 * pieces)
    def _():
        part_link(pieces - 1).wait_send()
        part_store(pieces - 1).wait()
        gain_back(w_z_all(), sum_all.at[:, :inner], norm_sums)
        stage[...] = sum_all[...].reshape(stage.shape).astype(BF16)

    outer_links = Numbered(outer[5])

    @pl.when((turn >= OUTER_TURNS[0]) & (turn <= OUTER_END))
    def _():
        for step, when in enumerate(OUTER_TURNS):

            @pl.when(turn == when)
            def _(step=step):
                scatter_step(step, outer_links.start, outer_links.arrived, stage, sums_zo, *outer[:5])

        @pl.when(turn == OUTER_END)
        def _():
            for step in range(scatter_steps() - 1):
                scatter_step(step, outer_links.sent, outer_links.nothing, stage, sums_zo, *outer[:5], add=False)

    @pl.when(phase == 3)
    def _():
        within_back(near.at[i], pre.at[i], step_sizes(i), cum.at[i], ages.at[i], gates.at[i, :, inner:], skip, heads, spread, gather,
                    near.at[i], grad_cum.at[i], grad_bc.at[i], inner_sums, seg, pair, grad_pair, step_x, low_a,
                    low_b)

    @pl.when(phase == 4)
    def _():
        @pl.when(i == 0)
        def _():
            sum_all[...] = jnp.zeros_like(sum_all)
            clear_margins(slope, keep, length)

        @pl.when(jnp.logical_not(below))
        def _():
            down(i).wait_recv()

        state_back(arrived.at[i], state_in.at[i], pre.at[i], inputs.at[i], step_sizes(i), cum.at[i], age_of(i), near.at[i],
                   gates.at[i, :, inner:], grad_cum.at[i], grad_bc.at[i], taps, skip, heads, spread, gather, tri_up,
                   inputs.at[i], conv_sums, head_sums, step_x, carried, wide.at[:length, :inner], low_a, low_b, low_c,
                   slope, keep)
        sum_all[:, :in_width] += mm_tn(normed[i, HALO:], inputs[i, HALO:])

        @pl.when(below)
        def _():
            down(i).wait_send()

    last_stage = stage.at[:, :, : in_width - own_bc]
    last_links = Numbered(last_ones[5])

    def last_step(step):
        scatter_step(step, last_links.start, last_links.arrived, last_stage, sums_w, *last_ones[:5])

    @pl.when(turn == 5 * pieces - 1)
    def _():
        small[0] = to_rows([conv_sums[k] for k in range(5)])
        small[0, 5:6, model : model + LANES] = jnp.sum(head_sums[0], 0, keepdims=True)
        small[0, 5:6, model + LANES :] = jnp.sum(head_sums[1], 0, keepdims=True)
        small[0, 6:8, :inner] = to_rows([inner_sums[0], inner_sums[1]])[:2]
        small[0, 6:8, inner:] = jnp.zeros((2, channels - inner), F32)
        sum_all[:, :in_width] += mm_tn(
            normed[:, :HALO].reshape(-1, model), inputs[:, :HALO].reshape(-1, in_width)
        )
        half_out[...] = sum_all[:, other_cols].reshape(half_out.shape).astype(BF16)
        half_link().start()
        stage[:, :, own_bc : in_width - own_bc] = (
            sum_all[:, bc_width:in_width].reshape(16, rows, in_width - bc_width).astype(BF16)
        )
        gain_back(w_in, sum_all, norm_sums)
        small[0, 5:6, :model] = jnp.sum(norm_sums[...], 0, keepdims=True) / norm_in[...]
        small_link(0).start()

    def small_step(k):
        row = lax.broadcasted_iota(jnp.int32, small.shape[1:], 0)
        lane = lax.broadcasted_iota(jnp.int32, small.shape[1:], 1)
        shared = ((row < 5) & (lane < bc_width)) | ((row == 5) & (lane < model))
        small_link(k).wait_recv()
        small[k + 1] = small[k] + (jnp.where(shared, seen[k], 0.0) if k == 0 else seen[k])
        if k < 4:
            small_link(k + 1).start()

    for k, at in enumerate(SMALL_TURNS):
        pl.when(turn == 5 * pieces + at)(functools.partial(small_step, k))

    @pl.when(phase == 5)
    def _():
        features_back(inputs.at[i], gates.at[i, :, :inner], w_in, w_z_all, gates.at[i, :, :inner], tails.at[i], features)
        grad_link(i).start()
        grad_store(i).start()
        pl.when(below)(tail_link(i).start)

        @pl.when(jnp.logical_not(above))
        def _():
            for copy in tail_blanks(i):
                copy.start()

        @pl.when(above & (i >= 2))
        def _():
            tail_link(i - 2).wait_recv()
            tail_partner_link(i - 2).start()

        @pl.when(i == 0)
        def _():
            half_link().wait_recv()
            own_half = sum_all[:, cols].reshape(half_in.shape) + half_in[...].astype(F32)
            stage[:, :, :own_bc] = own_half.astype(BF16)
            last_step(0)

        @pl.when(i == 4)
        def _():
            last_step(1)

        @pl.when(i == 5)
        def _():
            last_step(2)

    @pl.when(turn == 6 * pieces - 1)
    def _():
        for k in (pieces_of(gates) - 2, pieces_of(gates) - 1):

            @pl.when(above)
            def _(k=k):
                tail_link(k).wait_recv()
                tail_partner_link(k).start()

        for step in range(3, scatter_steps()):
            last_step(step)
            if step in (5, 6):
                small_step(step - 2)
        total = small.at[5]
        conv_out[:, :own_bc] = total[:, cols]
        conv_out[:, own_bc:] = total[:, bc_width:]
        norm_out[...] = jnp.broadcast_to(total[5:6, :model], norm_out.shape)
        head_out[...] = jnp.zeros_like(head_out)
        head_out[0:1] = total[5:6, model : model + LANES]
        head_out[1:2] = total[5:6, model + LANES : model + 2 * LANES]
        inner_out[...] = jnp.zeros_like(inner_out)
        inner_out[0:2] = total[6:8, :inner]
        for k in range(pieces_of(gates)):

            @pl.when(above)
            def _(k=k):
                tail_partner_link(k).wait_recv()
                tail_partner_link(k).wait_send()

            @pl.when(jnp.logical_not(above))
            def _(k=k):
                for copy in tail_blanks(k):
                    copy.wait()

            pl.when(below)(tail_link(k).wait_send)
            grad_link(k).wait_recv()
            grad_link(k).wait_send()
            grad_store(k).wait()
            part_link(k).wait_recv()
            stats_link(k).wait_send()
        half_link().wait_send()
        for k in range(5):
            small_link(k).wait_send()
        for step in range(scatter_steps() - 1):
            scatter_step(step, last_links.sent, last_links.nothing, last_stage, sums_w, *last_ones[:5], add=False)


def pieces_of(array):
    return array.shape[0]


ANY = pl.BlockSpec(memory_space=pl.ANY)
IN_VMEM = pl.BlockSpec(memory_space=pltpu.VMEM)
DMA = pltpu.SemaphoreType.DMA


def gather_rows(rows):
    return lax.all_gather(rows, ("shard", "context"), axis=0, tiled=True)


def scatter_rows(rows):
    return lax.psum_scatter(rows.astype(F32), ("shard", "context"), scatter_dimension=0, tiled=True)


def passed_along(value, by):
    length = lax.axis_size("context")
    return lax.ppermute(value, "context", [(i, i + by) for i in range(length) if 0 <= i + by < length])


def chain(local, decay, by):
    arrived = jnp.zeros_like(local)
    for _ in range(lax.axis_size("context") - 1):
        leaving = decay[:, :1] * arrived.astype(F32) + local.astype(F32)
        arrived = passed_along(leaving.astype(BF16), by)
    return arrived


def exchange(value):
    everything = lax.all_gather(value, "tensor")
    return everything[0], everything[1:]


def part_of(width, at):
    return lambda array: pl.BlockSpec((array.shape[0], width), lambda i: (0, at))


class AnyMesh:
    def prepare(self, hid, doc_start, norm_in, norm_gate, dt_bias, a_log, skip_d, w_bc, w_dt, w_x, conv_bc, conv_x):
        pieces, length, _ = hid.shape
        head_count = w_dt.shape[1]

        def head_row(row):
            return jnp.pad(jnp.tile(jnp.pad(row, (0, SLOTS - head_count)), 3), (0, LANES - 3 * SLOTS))

        heads = jnp.stack([head_row(dt_bias), head_row(a_log)] + [jnp.zeros((LANES,), F32)] * 6)
        vectors = (norm_in[None], norm_gate[None], jnp.repeat(skip_d, HEAD)[None])
        position = lax.axis_index("context") * length + jnp.arange(length, dtype=jnp.int32)
        ages = (position - doc_start.reshape(pieces, length)).astype(F32)
        age = jnp.broadcast_to(ages[:, :, None], (pieces, length, LANES))
        age_row = jnp.broadcast_to(ages[:, None, :], (pieces, 8, length))
        conv_bc_all = lax.all_gather(conv_bc, "tensor", axis=1, tiled=True)
        taps = jnp.pad(jnp.concatenate([conv_bc_all, conv_x], 1), ((0, 3), (0, 0)))
        w_bc_all = lax.all_gather(w_bc, "tensor", axis=1, tiled=True)
        w_dt_wide = jnp.pad(jnp.tile(jnp.pad(w_dt, ((0, 0), (0, SLOTS - w_dt.shape[1]))), (1, 3)), ((0, 0), (0, LANES - 3 * SLOTS)))
        w_in = gather_rows(jnp.concatenate([w_bc_all, w_dt_wide, w_x], 1))
        return w_in, passed_along(hid[:, length - HALO :], 1), taps, heads, vectors, (age, age_row)

    def forward(self, hid, seed, prepared, w_z, w_out, spread, tri):
        w_in, halo, taps, heads, (norm_in, norm_gate, skip), (age, _) = prepared
        pieces, length, model = hid.shape
        inner, channels = w_z.shape[1], taps.shape[1]
        token = functools.partial(shaped, F32, pieces, length)
        token_low = functools.partial(shaped, BF16, pieces, length)
        normed, raw, pre, dt_raw, cum, local, decay = call(
            forward_local, pieces,
            [(hid, by_piece), (halo, by_piece), (age, by_piece), (norm_in, fixed), (w_in, fixed), (taps, fixed),
             (heads, fixed), (spread, fixed), (tri, fixed)],
            [(shaped(BF16, pieces, HALO + length, model), by_piece),
             (shaped(BF16, pieces, HALO + length, w_in.shape[1]), by_piece), (token_low(channels), by_piece),
             (token(LANES), by_piece), (token(LANES), by_piece), (shaped(BF16, pieces, LANES, inner), by_piece),
             (shaped(F32, pieces, 8, inner), by_piece)],
            [((length, channels), F32), ((3, length, LANES), F32), ((HALO + length, channels), F32)], "forward_local",
        )
        state_in = chain(local, decay, 1)
        w_z_all, w_out_t = gather_rows(w_z), gather_rows(w_out.T)
        square = ((length, length), F32)
        token_wide = ((length, inner), F32)
        mixer, gate, grad_gn, part, stats = call(
            forward_mix, pieces,
            [(pre, by_piece), (dt_raw, by_piece), (cum, by_piece), (age, by_piece), (state_in, by_piece),
             (normed, by_piece), (seed, by_piece), (w_z_all, fixed), (w_out_t, fixed), (norm_gate, fixed),
             (skip, fixed), (heads, fixed), (spread, fixed)],
            [(token(inner), by_piece), (token_low(inner), by_piece), (token_low(inner), by_piece),
             (token_low(model), by_piece), (shaped(F32, pieces, 8, length), by_piece)],
            [token_wide, square, square, token_wide, token_wide, ((length, inner), BF16)], "forward_mix",
        )
        return normed, raw, pre, dt_raw, cum, decay, state_in, mixer, gate, grad_gn, part, stats, (w_z_all, fixed)

    def backward(self, inner_all, hid, seed, prepared, saved, own_bc, spread, gather, tri_up):
        w_in, halo, taps, heads, (norm_in, norm_gate, skip), (age, age_row) = prepared
        normed, raw, pre, dt_raw, cum, decay, state_in, mixer, gate, grad_gn, part, stats, w_z_all = saved
        pieces, length, model = hid.shape
        inner, channels, in_width, lead = mixer.shape[2], taps.shape[1], w_in.shape[1], HALO + length
        token = functools.partial(shaped, F32, pieces, length)
        token_low = functools.partial(shaped, BF16, pieces, length)
        square, token_wide, token_narrow = ((length, length), F32), ((length, inner), F32), ((length, inner), BF16)
        stats = lax.psum(stats, "tensor")
        grad_fed, grad_mix, grad_gate, grad_cum, grad_bc, grad_state, grad_wz, grad_wo, sums = call(
            functools.partial(backward_local, inner_all), pieces,
            [(mixer, by_piece), (gate, by_piece), (grad_gn, by_piece), (stats, by_piece), (pre, by_piece),
             (dt_raw, by_piece), (cum, by_piece), (age, by_piece), (age_row, by_piece), (state_in, by_piece),
             (normed, by_piece), (seed, by_piece), (norm_gate, fixed), (skip, fixed), (heads, fixed), (spread, fixed),
             (gather, fixed)],
            [(token(inner), by_piece), (token_low(inner), by_piece), (token_low(inner), by_piece),
             (token(LANES), by_piece), (token(2 * LANES), by_piece), (shaped(BF16, pieces, LANES, inner), by_piece),
             (shaped(BF16, model, inner), fixed), (shaped(BF16, model, inner), fixed), (shaped(F32, 8, inner), fixed)],
            [((2, 8, inner), F32), ((model, inner), F32), ((model, inner), F32), square, square, square, token_wide, token_wide, token_narrow,
             token_narrow], "backward_local",
        )
        grad_later = chain(grad_state, decay, -1)
        grad_normed, grad_halo, grad_w, conv_sums, head_sums, norm_sums = call(
            backward_finish, pieces,
            [(grad_later, by_piece), (state_in, by_piece), (pre, by_piece), (raw, by_piece), (dt_raw, by_piece),
             (cum, by_piece), (age, by_piece), (grad_fed, by_piece), (grad_mix, by_piece), (grad_cum, by_piece),
             (grad_bc, by_piece), (grad_gate, by_piece), (normed, by_piece), (hid, by_piece), (halo, by_piece),
             (w_in, fixed), w_z_all, (taps, fixed), (skip, fixed), (heads, fixed), (spread, fixed), (gather, fixed),
             (tri_up, fixed)],
            [(token_low(model), by_piece), (shaped(BF16, pieces, HALO, model), by_piece),
             (shaped(BF16, model, in_width), fixed), (shaped(F32, 8, channels), fixed), (shaped(F32, 8, LANES), fixed),
             (shaped(F32, 8, model), fixed)],
            [((5, 8, channels), F32), ((2, 8, LANES), F32), ((8, model), F32), ((model, in_width), F32), token_wide,
             token_wide, token_wide, token_narrow, token_narrow, token_narrow, ((lead + 8, channels), F32), ((3, lead + 8, LANES), F32),
             ((lead, in_width), BF16), ((lead, model), F32)],
            "backward_finish",
        )
        sums_zo = jnp.concatenate([scatter_rows(grad_wz), scatter_rows(grad_wo)], 1)
        mine, bc_width = lax.axis_index("tensor"), 2 * LANES
        grad_w = scatter_rows(grad_w)
        grad_w_bc = lax.psum_scatter(grad_w[:, :bc_width], "tensor", scatter_dimension=1, tiled=True)
        norm_sums, conv_bc = lax.psum((norm_sums, conv_sums[:, :bc_width]), ("shard", "context", "tensor"))
        conv_x, head_sums, sums = lax.psum((conv_sums[:, bc_width:], head_sums, sums), ("shard", "context"))
        conv_bc = lax.dynamic_slice_in_dim(conv_bc, mine * own_bc, own_bc, 1)
        sums_w = jnp.concatenate([grad_w_bc, grad_w[:, bc_width:]], 1)
        small = (jnp.concatenate([conv_bc, conv_x], 1), norm_sums, head_sums, sums)
        return stats, sums_zo, sums_w, small, exchange(part), exchange(grad_normed), exchange(passed_along(grad_halo, -1))

    def run(self, inner_all, hid, seed, prepared, w_z, w_out, own_bc, spread, gather, tri, tri_up):
        saved = self.forward(hid, seed, prepared, w_z, w_out, spread, tri)
        return self.backward(inner_all, hid, seed, prepared, saved, own_bc, spread, gather, tri_up)


class FourByFourByTwo:
    def prepare(self, hid, *parameters):
        return parameters

    def run(self, inner_all, hid, seed, prepared, w_z, w_out, own_bc, spread, gather, tri, tri_up):
        doc_start, norm_in, norm_gate, dt_bias, a_log, skip_d, w_bc, w_dt, w_x, conv_bc, conv_x = prepared
        pieces, length, model = hid.shape
        rows, inner = w_z.shape
        channels, in_width, lead = 2 * LANES + inner, 3 * LANES + inner, HALO + length
        width = in_width - own_bc

        def gradients(p, i):
            return (jnp.where(p == 2, i, jnp.where(p < 2, 0, pieces - 1)), 0, 0)

        def block_of(where):
            return lambda array: pl.BlockSpec((1,) + array.shape[1:], where)

        def once(array):
            return pl.BlockSpec(array.shape, lambda p, i: (0,) * array.ndim, pipeline_mode=pl.Buffered(1))

        kept = once

        def anywhere(array):
            return ANY

        def vmem(kind, *dims):
            return pltpu.VMEM(dims, kind)

        token_low, tail = shaped(BF16, pieces, length, model), shaped(BF16, pieces, HALO, model)
        stats = shaped(F32, pieces, 8, length)
        def in_smem(array):
            return pl.BlockSpec(memory_space=pltpu.SMEM)

        inputs = [(seed, block_of(gradients)), (hid, anywhere), (doc_start, once), (w_bc, once),
                  (w_dt.T, once), (w_x, once), (conv_bc, once), (conv_x, once), (norm_in, once), (norm_gate, once),
                  (dt_bias, in_smem), (a_log, in_smem), (skip_d, in_smem), (w_z, once), (w_out.T, once), (spread, once),
                  (gather, once), (tri, once), (tri_up, once)]
        outputs = [(stats, kept), (shaped(F32, rows, 2 * inner), kept), (shaped(F32, rows, width), kept),
                   (shaped(F32, 8, channels - own_bc), kept), (shaped(F32, 8, model), kept), (shaped(F32, 8, LANES), kept),
                   (shaped(F32, 8, inner), kept), (token_low, anywhere), (shaped(BF16, 1, *token_low.shape), anywhere),
                   (token_low, anywhere), (shaped(BF16, 1, *token_low.shape), anywhere), (tail, anywhere),
                   (shaped(BF16, 1, *tail.shape), anywhere)]
        state, square, low = vmem(BF16, pieces, LANES, inner), vmem(F32, length, length), vmem(BF16, length, inner)
        per_piece = DMA((pieces,))
        scratch = [
            vmem(BF16, *tail.shape), vmem(F32, *stats.shape), vmem(F32, pieces, length, LANES), vmem(F32, 8, inner),
            vmem(BF16, model, in_width),
            vmem(F32, 8, channels), vmem(F32, 8, LANES), vmem(BF16, rows, in_width), vmem(F32, LANES, rows),
            vmem(BF16, length, model),
            vmem(BF16, pieces, lead, model), vmem(BF16, pieces, length, channels), vmem(F32, pieces, length, LANES),
            vmem(BF16, pieces, length, 2 * inner), vmem(F32, pieces, length, inner), vmem(BF16, pieces, lead, in_width),
            state, state, state, vmem(F32, pieces, 8, inner), vmem(BF16, 16, rows, 2 * inner),
            vmem(F32, pieces, length, 2 * LANES), vmem(F32, pieces, length, LANES), vmem(F32, model, 2 * inner),
            vmem(BF16, rows, 2 * inner), vmem(BF16, 16, rows, 2 * inner), vmem(BF16, 16, rows, own_bc),
            vmem(BF16, 16, rows, own_bc), vmem(F32, length, inner), vmem(F32, length, inner), low, low, low,
            vmem(F32, lead + 8, channels), vmem(F32, 3, lead + 8, LANES), vmem(F32, lead, channels), square, square,
            square, vmem(F32, length, LANES), vmem(BF16, *tail.shape),
            vmem(F32, *stats.shape), vmem(F32, *stats.shape), vmem(F32, 6, 8, channels),
            vmem(F32, 5, 8, channels), vmem(F32, 5, 8, channels), vmem(F32, 2, 8, LANES), vmem(F32, 8, model),
            vmem(F32, 2, 8, inner), DMA((2, GATHER_COPIES)), DMA((2, 16)), DMA((3,)), DMA((3,)), DMA((GATHER_COPIES,)),
            DMA((16,)), DMA((2, pieces)), DMA((2, pieces)), DMA((8,)),
            DMA((8,)), per_piece, per_piece, per_piece, per_piece, per_piece, per_piece, DMA((2, pieces)),
            DMA((2, pieces)), DMA((2, pieces)),
        ]
        (stats, sums_zo, sums_w, conv_sums, norm_sums, head_sums, sums, own_part, other_part, own_grad, other_grad,
         own_tail, other_tail) = pl.pallas_call(
            functools.partial(block, inner_all),
            grid=(6, pieces),
            in_specs=[cut(array) for array, cut in inputs],
            out_specs=[cut(shape) for shape, cut in outputs],
            out_shape=[shape for shape, _ in outputs],
            scratch_shapes=scratch + scatter_scratch(rows, 2 * inner) + scatter_scratch(rows, width),
            compiler_params=pltpu.CompilerParams(
                collective_id=1, has_side_effects=True, vmem_limit_bytes=BLOCK_VMEM_BYTES
            ),
            name="block",
        )(*[array for array, _ in inputs])
        small = (conv_sums, norm_sums, head_sums, sums)
        return stats, sums_zo, sums_w, small, (own_part, other_part), (own_grad, other_grad), (own_tail, other_tail)


def links():
    sizes = tuple(lax.axis_size(axis) for axis in ("shard", "context", "tensor"))
    return FourByFourByTwo() if sizes == (4, 4, 2) else AnyMesh()


def shards(inner_all, hidden_in, out_grad, doc_start, norm_in, w_z, w_x, w_bc, w_dt, conv_x, conv_bc, dt_bias, a_log,
           skip_d, norm_gate, w_out):
    micro, per_device, length, model = hidden_in.shape
    pieces = micro * per_device
    inner = w_z.shape[1]
    head_count, own_bc = w_dt.shape[1], w_bc.shape[1]

    head_of = np.arange(inner) // HEAD
    slot = np.where(np.arange(LANES) < 3 * SLOTS, np.arange(LANES) % SLOTS, -1)
    gather = jnp.asarray(head_of[:, None] == np.arange(LANES)[None], BF16)
    spread = jnp.asarray(head_of[None] == slot[:, None], BF16)
    tri = jnp.asarray(np.tril(np.ones((length, length))), BF16)
    tri_up = jnp.asarray(np.triu(np.ones((length, length))), BF16)

    hid = hidden_in.reshape(pieces, length, model)
    seed = out_grad.reshape(pieces, length, model)
    between = links()
    prepared = between.prepare(
        hid, doc_start, norm_in, norm_gate, dt_bias, a_log, skip_d, w_bc, w_dt, w_x, conv_bc, conv_x
    )
    stats, sums_zo, sums_w, small, (own_part, other_part), (own_grad, other_grad), (own_tail, other_tail) = (
        between.run(inner_all, hid, seed, prepared, w_z, w_out, own_bc, spread, gather, tri, tri_up)
    )
    token_low = functools.partial(shaped, BF16, pieces, length)
    rows = w_z.shape[0]
    outputs = [shaped(F32, rows, inner), shaped(F32, rows, inner), shaped(F32, rows, own_bc),
               shaped(F32, head_count, rows), shaped(F32, rows, inner), shaped(F32, 5, inner), shaped(F32, 5, own_bc),
               shaped(F32, 1, head_count), shaped(F32, 1, head_count), shaped(F32, 1, head_count),
               shaped(F32, inner), shaped(F32, model)]
    (out, in_grad, grad_wz, grad_wx, grad_wbc, grad_wdt, grad_wo, grad_conv_x, grad_conv_bc, grad_dt_bias, grad_a_log,
     grad_skip, grad_norm_gate, grad_norm_in) = call(
        functools.partial(finish, inner_all), pieces // SPAN,
        [(hid, by_span), (seed, by_span), (stats, by_span), (norm_in, fixed), (own_part, by_span),
         (other_part, by_span_second), (own_grad, by_span), (other_grad, by_span_second), (own_tail, by_span),
         (other_tail, by_span_second), (sums_zo, fixed), (sums_w, fixed)] + [(array, fixed) for array in small]
        + [(gather, fixed)],
        [(token_low(model), by_span), (token_low(model), by_span)] + [(shape, fixed) for shape in outputs],
        [((length, model), F32)], "finish",
    )
    return (
        out.reshape(hidden_in.shape),
        in_grad.reshape(hidden_in.shape),
        grad_norm_in,
        grad_wz,
        grad_wx,
        grad_wbc,
        grad_wdt.T,
        grad_conv_x,
        grad_conv_bc,
        grad_dt_bias[0],
        grad_a_log[0],
        grad_skip[0],
        grad_norm_gate,
        grad_wo.T,
    )


def solution(mesh):
    whole = P(None, "shard", "context", None)
    rows = P(("shard", "context"), "tensor")
    lanes = P(None, "tensor")
    heads = P("tensor")
    w_out = P("tensor", ("shard", "context"))
    inputs = (whole, whole, P(None, "shard", "context"), P(), rows, rows, rows, rows, lanes, lanes, heads, heads, heads, heads, w_out)
    outputs = (whole, whole, P(), rows, rows, rows, rows, lanes, lanes, heads, heads, heads, heads, w_out)

    def placed(*arrays):
        inner_all = arrays[4].shape[1]
        return jax.shard_map(
            functools.partial(shards, inner_all), mesh=mesh, in_specs=inputs, out_specs=outputs, check_vma=False
        )(*arrays)

    return placed
```

time: 271 us -> 208 us (0.77)
  Pallas kernels: 252 us -> 207 us
  local copies, waits for them, and re-layouts: 13.7 us -> 0 us
  other arithmetic: 3.25 us -> 0 us
    pallas_call x3 -> x1, Pallas kernels: 239 us -> 195 us  [run(): pl.pallas_call(functools.partial(block, inner_all), grid=(6, pieces), in_...]
    unnamed x4 -> x0, local copies, waits for them, and re-layouts: 6.29 us -> none
    broadcast_in_dim x5 -> x0, local copies, waits for them, and re-layouts: 5.19 us -> none  [the longest x2 2.53 us: shards(): norm_in, norm_gate = (norm_in[None], norm_gate[None])]
where the time goes in v5:
time: 208 us
  Pallas kernels  207 us (100%)
    pallas_call x1, Pallas kernels, run(): pl.pallas_call(functools.partial(block, inner_all), grid=(6, pieces), in_...  195 us
    pallas_call x1, Pallas kernels, call(): pl.pallas_call(kernel, grid=(pieces,), in_specs=[cut(array) for array, cu...  12.3 us

profile of v5, /device:TPU:0, one launch (start us, length us, event | category | flops | bytes accessed | tf_op | source)
XLA Modules:
  0.0 208.1 jit_solution(12419036494291437932)
XLA Ops:
  0.6 195.1 %block.1 = (f32[8,8,256]{2,1,0:T(8,128)}, f32[48,1536]{1,0:T(8,128)}, f32[48,1024]{1,0:T(8,128)}, f32[8,896]{1,0:T(8,128)}, f32[8,768]{1,0:T(8,128)}, /*index=5*...) custom-call(bf16[8,256,768]{2,1,0:T(8,128)(2,1)} %bitcast.13, ...), custom_call_target="tpu_custom_call" | custom-call | tf_op jit(solution)/shard_map/block/pallas_call | solution.py:1375
  195.8 12.3 %finish.1 = (bf16[8,256,768]{2,1,0:T(8,128)(2,1)}, bf16[8,256,768]{2,1,0:T(8,128)(2,1)}, f32[48,768]{1,0:T(8,128)}, f32[48,768]{1,0:T(8,128)}, f32[48,128]{1,0:T...) custom-call(bf16[8,256,768]{2,1,0:T(8,128)(2,1)} %bitcast.12, ...), custom_call_target="tpu_custom_call" | custom-call | tf_op jit(solution)/shard_map/finish/pallas_call | solution.py:530

commit v6 on v5

--- a/solution.py
+++ b/solution.py
@@ -810,7 +810,7 @@
         copy.start()
 
     def step_sizes(k):
-        return mm(normed[k, HALO:], w_in[:, bc_width : bc_width + LANES])
+        return step_raw.at[k]
 
     def age_of(k):
         return age_lanes.at[k]
@@ -923,7 +923,7 @@
         age = age_of(i)
         normalise(halo.at[i], norm_in, normed.at[i, :HALO])
         project(age, w_in, taps, heads, spread, tri, normed.at[i], inputs.at[i],
-                pre.at[i], step_raw, cum.at[i], leaving.at[i], decay.at[i], act, keep.at[:, :length], slope.at[:lead])
+                pre.at[i], step_raw.at[i], cum.at[i], leaving.at[i], decay.at[i], act, keep.at[:, :length], slope.at[:lead])
 
         @pl.when(jnp.logical_not(below))
         def _():
@@ -1363,7 +1363,7 @@
             vmem(BF16, rows, 2 * inner), vmem(BF16, 16, rows, 2 * inner), vmem(BF16, 16, rows, own_bc),
             vmem(BF16, 16, rows, own_bc), vmem(F32, length, inner), vmem(F32, length, inner), low, low, low,
             vmem(F32, lead + 8, channels), vmem(F32, 3, lead + 8, LANES), vmem(F32, lead, channels), square, square,
-            square, vmem(F32, length, LANES), vmem(BF16, *tail.shape),
+            square, vmem(F32, pieces, length, LANES), vmem(BF16, *tail.shape),
             vmem(F32, *stats.shape), vmem(F32, *stats.shape), vmem(F32, 6, 8, channels),
             vmem(F32, 5, 8, channels), vmem(F32, 5, 8, channels), vmem(F32, 2, 8, LANES), vmem(F32, 8, model),
             vmem(F32, 2, 8, inner), DMA((2, GATHER_COPIES)), DMA((2, 16)), DMA((3,)), DMA((3,)), DMA((GATHER_COPIES,)),

time: 208 us -> 204 us (0.981)
  Pallas kernels: 207 us -> 203 us
    pallas_call x1, Pallas kernels: 195 us -> 191 us  [run(): pl.pallas_call(functools.partial(block, inner_all), grid=(6, pieces), in_...]
where the time goes in v6:
time: 204 us
  Pallas kernels  203 us (100%)
    pallas_call x1, Pallas kernels, run(): pl.pallas_call(functools.partial(block, inner_all), grid=(6, pieces), in_...  191 us
    pallas_call x1, Pallas kernels, call(): pl.pallas_call(kernel, grid=(pieces,), in_specs=[cut(array) for array, cu...  12.3 us

profile of v6, /device:TPU:0, one launch (start us, length us, event | category | flops | bytes accessed | tf_op | source)
XLA Modules:
  0.0 203.9 jit_solution(8767265063073061886)
XLA Ops:
  0.6 191.0 %block.1 = (f32[8,8,256]{2,1,0:T(8,128)}, f32[48,1536]{1,0:T(8,128)}, f32[48,1024]{1,0:T(8,128)}, f32[8,896]{1,0:T(8,128)}, f32[8,768]{1,0:T(8,128)}, /*index=5*...) custom-call(bf16[8,256,768]{2,1,0:T(8,128)(2,1)} %bitcast.13, ...), custom_call_target="tpu_custom_call" | custom-call | tf_op jit(solution)/shard_map/block/pallas_call | solution.py:1375
  191.6 12.3 %finish.1 = (bf16[8,256,768]{2,1,0:T(8,128)(2,1)}, bf16[8,256,768]{2,1,0:T(8,128)(2,1)}, f32[48,768]{1,0:T(8,128)}, f32[48,768]{1,0:T(8,128)}, f32[48,128]{1,0:T...) custom-call(bf16[8,256,768]{2,1,0:T(8,128)(2,1)} %bitcast.12, ...), custom_call_target="tpu_custom_call" | custom-call | tf_op jit(solution)/shard_map/finish/pallas_call | solution.py:530
